TPU v7x, 128 devices: a whole 4x4x4 slice. The times are simulated.
128 devices in a mesh: section: 4 (over x), dp: 32 (over y, z, core).
Axes of the slice: x: 4, y: 4, z: 4, core: 2. Of those that a mesh axis runs over, the one named last changes fastest.
Arguments:
- hidden_acts: bfloat16 [4, 4096, 28672], P('section', 'dp'), may hold values from -6 to 6
- layer_inputs: bfloat16 [4, 4096, 8192], P('section', 'dp'), may hold values from -20 to 20
- norm_gains: bfloat16 [4, 8192], P('section'), may hold values from 0.099609375 to 0.59765625
- top_cotangent: bfloat16 [4096, 8192], P('dp'), may hold values from -6 to 6
- up_factors: bfloat16 [32, 4, 32, 28672], P('dp', 'section'), may hold values from -0.005859375 to 0.005859375
- down_factors: bfloat16 [32, 4, 32, 8192], P('dp', 'section'), may hold values from -0.0625 to 0.0625
- candidates: int32 [32, 8], replicated, may hold values from 0 to 31, all different within a row; in each aligned block of 32 rows (0 to 31, 32 to 63, ...) at most 10 rows name the same one
- counts: int32 [32], P('dp'), may hold values from 1 to 128, 3072 in all
Outputs:
- scores: float32 [4, 4096, 32], P('section', 'dp')
Inputs may be any that keep to these rules, and one draw needn't show every extreme that they name: `candidates`: each row lists 8 different shards; every shard is listed by at most 10 queries, a bound that some block reaches.
All inputs are finite; a program needn't handle non-finite values. No bound on the sum of `counts` on one device may be relied on, other than what follows from the above.
Results may differ from a plain program's by a relative error of at most 0.0029.
Values may be sent and summed in bfloat16 or wider, within the bound.
No kernel may reach another device: no remote copies, remote signals or barrier semaphores. Data moves between devices by JAX's collectives and lax.ppermute only.
A program may use at most 192 MiB of HBM per device.

v0:
```python
import jax
import jax.numpy as jnp
from jax import lax
from jax.sharding import PartitionSpec as P

EPSILON = 1e-05


def passed_along(block, axis, distance):
    devices = range(lax.axis_size(axis))
    route = [(i - distance, i) for i in devices if i - distance in devices]
    return lax.ppermute(block, axis, route)


def norm_terms(inputs):
    values = inputs.astype(jnp.float32)
    inverse = lax.rsqrt(jnp.mean(values * values, axis=-1, keepdims=True) + EPSILON)
    return (values * inverse, inverse)


def transition(cotangent, normed, inverse, gain_row):
    scaled = gain_row * cotangent
    return (
        cotangent
        + scaled * inverse
        - normed * inverse * jnp.mean(normed * scaled, axis=-1, keepdims=True)
    )


def body(
    hidden_acts,
    layer_inputs,
    norm_gains,
    top_cotangent,
    up_factors,
    down_factors,
    candidates,
    counts,
):
    sections = lax.axis_size("section")
    section_id = lax.axis_index("section")
    top_rows = top_cotangent.astype(jnp.float32)
    is_last = section_id == sections - 1
    normed, inverse = norm_terms(layer_inputs[0])
    gain_row = norm_gains[0].astype(jnp.float32)[None, :]
    cotangent = top_rows
    for round_index in range(sections - 1):
        arrived = passed_along(transition(cotangent, normed, inverse, gain_row), "section", -1)
        cotangent = jnp.where(is_last, top_rows, arrived)
    shards = lax.axis_size("dp")
    own_shard = lax.axis_index("dp")
    spread_up, spread_down = (
        lax.all_to_all(up_factors[:, 0], "dp", split_axis=1, concat_axis=0, tiled=True),
        lax.all_to_all(down_factors[:, 0], "dp", split_axis=1, concat_axis=0, tiled=True),
    )
    listed = candidates.shape[1]
    capacity = listed + listed // 4
    member = jnp.any(
        candidates[:, :, None] == jnp.arange(shards, dtype=jnp.int32)[None, None, :], axis=1
    ).astype(jnp.int32)
    position = jnp.cumsum(member, axis=0) - member
    slot_hits = (
        (member.T[:, None, :] == 1)
        & (position.T[:, None, :] == jnp.arange(capacity, dtype=jnp.int32)[None, :, None])
    ).astype(jnp.bfloat16)
    outgoing_up = jnp.einsum(
        "dsq,qrf->dsrf", slot_hits, spread_up, preferred_element_type=jnp.float32
    ).astype(jnp.bfloat16)
    outgoing_down = jnp.einsum(
        "dsq,qrf->dsrf", slot_hits, spread_down, preferred_element_type=jnp.float32
    ).astype(jnp.bfloat16)
    arrived_up, arrived_down = (
        lax.all_to_all(outgoing_up, "dp", split_axis=0, concat_axis=2, tiled=True),
        lax.all_to_all(outgoing_down, "dp", split_axis=0, concat_axis=2, tiled=True),
    )
    own_hits = lax.dynamic_index_in_dim(slot_hits, own_shard, 0, keepdims=False).astype(jnp.float32)
    proj_up = jnp.einsum(
        "tf,srf->tsr", hidden_acts[0], arrived_up[0], preferred_element_type=jnp.float32
    )
    proj_down = jnp.einsum(
        "td,srd->tsr",
        cotangent.astype(jnp.bfloat16),
        arrived_down[0],
        preferred_element_type=jnp.float32,
    )
    slot_scores = jnp.sum(proj_up * proj_down, axis=-1)
    dense = jnp.dot(
        slot_scores, own_hits, precision=lax.Precision.HIGHEST, preferred_element_type=jnp.float32
    )
    live_rows = (jnp.arange(dense.shape[0], dtype=jnp.int32) < counts[0]).astype(jnp.float32)[
        :, None
    ]
    return (dense * live_rows)[None]


def solution(mesh):
    return jax.shard_map(
        body,
        mesh=mesh,
        in_specs=(
            P("section", "dp", None),
            P("section", "dp", None),
            P("section", None),
            P("dp", None),
            P("dp", "section", None, None),
            P("dp", "section", None, None),
            P(),
            P("dp"),
        ),
        out_specs=P("section", "dp", None),
        check_vma=False,
    )
```

profile of v0, /device:TPU:32, one launch (start us, length us, event | category | flops | bytes accessed | tf_op | source)
XLA Modules:
  0.0 726.7 jit_solution(2366373318101315571)
XLA Ops:
  0.0 7.2 copy.89
  7.2 0.5 broadcast.47
  7.7 12.4 %reduce = bf16[32,28672]{1,0:T(8,128)(2,1)S(1)} reduce(bf16[32,1,28672]{2,1,0:T(2,128)(2,1)} %bitcast.77, bf16[]{:T(256)} %broadcast.47), dimensions={1}, to_apply=%bitcast.74.reduce_sub_computation | reduce | bytes 3670018
  20.1 0.0 copy-start.8
  20.1 0.0 copy-start.6
  20.1 2.3 reshape.61
  22.4 8.2 %all-to-all-start = ((bf16[32,2,14336]{2,1,0:T(2,128)(2,1)}), bf16[32,2,14336]{2,1,0:T(2,128)(2,1)S(1)}, u32[]{:S(2)}, u32[]{:S(2)}) async-start(bf16[32,2,14336]{2,1,0:T(2,128)(2,1)} %reshape.61), calls=%async_computation | async-start | bytes 3670016 | tf_op jit(solution)/shard_map/all_to_all | solution.py:53
  30.6 0.1 copy.48
  30.7 0.1 fusion.49
  30.9 0.1 reduce_window_sum.11
  30.9 0.1 copy.50
  31.0 0.1 copy.49
  31.1 1.1 copy.90
  32.2 3.8 reduce.1
  36.0 1.2 reshape.63
  37.2 0.1 fusion.48
  37.3 17.2 %all-to-all-done = bf16[32,2,14336]{2,1,0:T(2,128)(2,1)S(1)} async-done(((bf16[32,2,14336]{2,1,0:T(2,128)(2,1)}), bf16[32,2,14336]{2,1,0:T(2,128)(2,1)S(1)}, u32[]{:S(2)}, u32[]{:S(2)}) %all-to-all-start) | async-done | bytes 1835040 | tf_op jit(solution)/shard_map/all_to_all | solution.py:53
  54.5 6.5 all-to-all-start.2
  61.0 6.5 reshape.62
  67.6 11.1 %fusion = bf16[32,10,1,28672]{3,0,1,2:T(8,128)(2,1)} fusion(bf16[1,32,28672]{2,0,1:T(2,128)(2,1)} %bitcast.78, pred[32,10,32]{2,1,0:T(8,128)(4,1)S(1)} %fusion.48), kind=kOutput, calls=%fused_computation.1 | convolution fusion | flops 596377600 | bytes 20195328 | tf_op jit(solution)/shard_map/dsq,qrf->dsrf/dot_general | solution.py:66
  78.6 20.2 %copy.53 = bf16[32,10,1,28672]{3,1,2,0:T(8,128)(2,1)} copy(bf16[32,10,1,28672]{3,0,1,2:T(8,128)(2,1)} %fusion) | data formatting | bytes 36700160 | tf_op jit(solution)/shard_map/convert_element_type | solution.py:68
  98.9 0.0 all-to-all-done.2
  98.9 0.8 copy-done.5
  99.7 7.7 %all-to-all-start.1 = ((bf16[32,10,1,28672]{3,1,2,0:T(8,128)(2,1)}), bf16[32,10,1,28672]{3,1,2,0:T(8,128)(2,1)}, u32[]{:S(2)}, u32[]{:S(2)}) async-start(bf16[32,10,1,28672]{3,1,2,0:T(8,128)(2,1)} %copy.53), calls=%async_computation.1 | async-start | bytes 58720256 | tf_op jit(solution)/shard_map/all_to_all | solution.py:73
  107.4 0.0 copy-start.1
  107.4 0.5 fusion.23
  107.9 2.6 fusion.20
  110.6 3.2 fusion.17
  113.8 1.3 collective-permute-start
  115.1 0.0 copy-start.2
  115.1 93.5 %collective-permute-done = f32[128,8192]{1,0:T(8,128)} collective-permute-done((f32[128,8192]{1,0:T(8,128)}, f32[128,8192]{1,0:T(8,128)}, u32[]{:S(2)}, u32[]{:S(2)}) %collective-permute-start) | collective-permute-done | bytes 4194336 | tf_op jit(solution)/shard_map/ppermute | solution.py:12
  208.6 4.0 fusion.21
  212.6 5.6 fusion.18
  218.2 1.5 collective-permute-start.1
  220.3 3.6 reshape.64
  223.9 1.6 fusion.4
  225.5 0.0 copy-start.3
  225.5 6.4 copy.57
  231.9 80.3 %collective-permute-done.1 = f32[128,8192]{1,0:T(8,128)} collective-permute-done((f32[128,8192]{1,0:T(8,128)}, f32[128,8192]{1,0:T(8,128)}, u32[]{:S(2)}, u32[]{:S(2)}) %collective-permute-start.1) | collective-permute-done | bytes 4194336 | tf_op jit(solution)/shard_map/ppermute | solution.py:12
  312.2 3.3 fusion.22
  315.5 271.1 %all-to-all-done.1 = bf16[32,10,1,28672]{3,1,2,0:T(8,128)(2,1)} async-done(((bf16[32,10,1,28672]{3,1,2,0:T(8,128)(2,1)}), bf16[32,10,1,28672]{3,1,2,0:T(8,128)(2,1)}, u32[]{:S(2)}, u32[]{:S(2)}) %all-to-all-start.1) | async-done | bytes 18350112 | tf_op jit(solution)/shard_map/all_to_all | solution.py:73
  586.6 6.9 all-to-all-start.3
  593.5 5.7 fusion.19
  599.3 1.6 collective-permute-start.2
  600.9 21.7 %fusion.30 = f32[128,10,32]{0,2,1:T(8,128)S(1)} fusion(bf16[1,128,28672]{2,1,0:T(8,128)(2,1)} %param.8, bf16[32,10,1,28672]{3,1,2,0:T(8,128)(2,1)} %all-to-all-done.1), kind=kOutput, calls=%fused_computation.38 | convolution fusion | flops 2348810240 | bytes 25853952 | tf_op jit(solution)/shard_map/tf,srf->tsr/dot_general | solution.py:77
  622.7 95.1 %all-to-all-done.3 = bf16[32,10,1,8192]{3,1,2,0:T(8,128)(2,1)} async-done(((bf16[32,10,1,8192]{3,1,2,0:T(8,128)(2,1)}), bf16[32,10,1,8192]{3,1,2,0:T(8,128)(2,1)}, u32[]{:S(2)}, u32[]{:S(2)}) %all-to-all-start.3) | async-done | bytes 5242912 | tf_op jit(solution)/shard_map/all_to_all | solution.py:74
  717.8 7.9 %fusion.40 = f32[128,10]{0,1:T(8,128)S(1)} fusion(f32[128,10,32]{0,2,1:T(8,128)S(1)} %fusion.30, bf16[32,10,1,8192]{3,1,2,0:T(8,128)(2,1)} %all-to-all-done.3, bf16[128,8192]{1,0:T(8,128)(2,1)} %collective-permute-done.2, bf16[128,8192]{1,0:T(8,128)(2,1)S(1)} %copy-done.4, pred[]{:T(512)S(6)} %eq.48), kind=kOutput, calls=%fused_computation.40 | convolution fusion | flops 673266432 | bytes 9606145 | tf_op jit(solution)/shard_map/td,srd->tsr/dot_general | solution.py:80
  725.6 0.8 fusion.45
  (21 shorter events, 0.1 us)
Async XLA Ops:
  20.1 10.5 %copy-start.8 = (s32[32,8]{0,1:T(8,128)S(1)}, s32[32,8]{0,1:T(8,128)}, u32[]{:S(2)}) copy-start(s32[32,8]{0,1:T(8,128)} %param.14) | copy-start | bytes 3076
  20.1 11.0 %copy-start.6 = (bf16[1,1,32,8192]{3,2,1,0:T(8,128)(2,1)S(1)}, bf16[1,1,32,8192]{3,2,1,0:T(8,128)(2,1)}, u32[]{:S(2)}) copy-start(bf16[1,1,32,8192]{3,2,1,0:T(8,128)(2,1)} %param.13) | copy-start | bytes 1572868
  22.4 32.1 %all-to-all-start = ((bf16[32,2,14336]{2,1,0:T(2,128)(2,1)}), bf16[32,2,14336]{2,1,0:T(2,128)(2,1)S(1)}, u32[]{:S(2)}, u32[]{:S(2)}) async-start(bf16[32,2,14336]{2,1,0:T(2,128)(2,1)} %reshape.61), calls=%async_computation | async-start | bytes 3670016 | tf_op jit(solution)/shard_map/all_to_all | solution.py:53
  54.5 44.4 %all-to-all-start.2 = ((bf16[32,2,4096]{2,1,0:T(2,128)(2,1)}), bf16[32,2,4096]{2,1,0:T(2,128)(2,1)S(1)}, u32[]{:S(2)}, u32[]{:S(2)}) async-start(bf16[32,2,4096]{2,1,0:T(2,128)(2,1)} %reshape.63), calls=%async_computation.2 | async-start | bytes 1048576 | tf_op jit(solution)/shard_map/all_to_all | solution.py:54
  98.9 8.5 %copy-start.7 = (bf16[1,8192]{1,0:T(2,128)(2,1)S(1)}, bf16[1,8192]{1,0:T(2,128)(2,1)}, u32[]{:S(2)}) copy-start(bf16[1,8192]{1,0:T(2,128)(2,1)} %param.10) | copy-start | bytes 49156
  98.9 8.6 %copy-start = (bf16[1,128,8192]{2,1,0:T(8,128)(2,1)S(1)}, bf16[1,128,8192]{2,1,0:T(8,128)(2,1)}, u32[]{:S(2)}) copy-start(bf16[1,128,8192]{2,1,0:T(8,128)(2,1)} %param.9) | copy-start | bytes 6291460
  98.9 0.8 copy-start.5
  99.7 486.9 %all-to-all-start.1 = ((bf16[32,10,1,28672]{3,1,2,0:T(8,128)(2,1)}), bf16[32,10,1,28672]{3,1,2,0:T(8,128)(2,1)}, u32[]{:S(2)}, u32[]{:S(2)}) async-start(bf16[32,10,1,28672]{3,1,2,0:T(8,128)(2,1)} %copy.53), calls=%async_computation.1 | async-start | bytes 58720256 | tf_op jit(solution)/shard_map/all_to_all | solution.py:73
  107.4 3.2 copy-start.1
  113.8 94.8 %collective-permute-start = (f32[128,8192]{1,0:T(8,128)}, f32[128,8192]{1,0:T(8,128)}, u32[]{:S(2)}, u32[]{:S(2)}) collective-permute-start(f32[128,8192]{1,0:T(8,128)} %fusion.17), channel_id=1, source_target_pairs={{32,0},{64,32},{96,64},{33,1},{65,33},{97,65},{34,2},{66,34},{98,6... | collective-permute-start | bytes 12582920 | tf_op jit(solution)/shard_map/ppermute | solution.py:12
  115.1 97.5 %copy-start.2 = (bf16[128,8192]{1,0:T(8,128)(2,1)S(1)}, bf16[128,8192]{1,0:T(8,128)(2,1)}, u32[]{:S(2)}) copy-start(bf16[128,8192]{1,0:T(8,128)(2,1)} %param.11) | copy-start | bytes 6291460
  218.2 94.0 %collective-permute-start.1 = (f32[128,8192]{1,0:T(8,128)}, f32[128,8192]{1,0:T(8,128)}, u32[]{:S(2)}, u32[]{:S(2)}) collective-permute-start(f32[128,8192]{1,0:T(8,128)} %fusion.18), channel_id=1, source_target_pairs={{32,0},{64,32},{96,64},{33,1},{65,33},{97,65},{34,2},{66,34},{98,6... | collective-permute-start | bytes 12582920 | tf_op jit(solution)/shard_map/ppermute | solution.py:12
  225.5 86.7 %copy-start.3 = (bf16[128,8192]{1,0:T(8,128)(2,1)S(1)}, bf16[128,8192]{1,0:T(8,128)(2,1)}, u32[]{:S(2)}) copy-start(bf16[128,8192]{1,0:T(8,128)(2,1)} %param.11) | copy-start | bytes 6291460
  586.6 131.2 %all-to-all-start.3 = ((bf16[32,10,1,8192]{3,1,2,0:T(8,128)(2,1)}), bf16[32,10,1,8192]{3,1,2,0:T(8,128)(2,1)}, u32[]{:S(2)}, u32[]{:S(2)}) async-start(bf16[32,10,1,8192]{3,1,2,0:T(8,128)(2,1)} %copy.57), calls=%async_computation.3 | async-start | bytes 16777216 | tf_op jit(solution)/shard_map/all_to_all | solution.py:74
  599.3 118.5 %copy-start.4 = (bf16[128,8192]{1,0:T(8,128)(2,1)S(1)}, bf16[128,8192]{1,0:T(8,128)(2,1)}, u32[]{:S(2)}) copy-start(bf16[128,8192]{1,0:T(8,128)(2,1)} %param.11) | copy-start | bytes 6291460
  599.3 118.5 %collective-permute-start.2 = (bf16[128,8192]{1,0:T(8,128)(2,1)}, bf16[128,8192]{1,0:T(8,128)(2,1)}, u32[]{:S(2)}, u32[]{:S(2)}) collective-permute-start(bf16[128,8192]{1,0:T(8,128)(2,1)} %fusion.19), channel_id=1, source_target_pairs={{32,0},{64,32},{96,64},{33,1},{65,33},{97,65},{34,2},{66,34},{98,6... | collective-permute-start | bytes 6291464 | tf_op jit(solution)/shard_map/ppermute | solution.py:12
where the time goes:
time: 736 us; the launch traced here: 727 us
  waiting for transfers between devices  557 us (76%)
  local copies, waits for them, and re-layouts  50.1 us (7%)
  matrix products  43 us (6%)
  other arithmetic  41.4 us (6%)
  starting transfers between devices  33.7 us (5%)
    all_to_all x1, waiting for transfers between devices, body(): lax.all_to_all(outgoing_up, 'dp', split_axis=0, concat_axis=2, tiled=True)  271 us
    ppermute x3, waiting for transfers between devices, passed_along(): return lax.ppermute(block, axis, route)  174 us
    all_to_all x1, waiting for transfers between devices, body(): lax.all_to_all(outgoing_down, 'dp', split_axis=0, concat_axis=2, tiled=True)  95.1 us
    dot_general x1, matrix products, body(): jnp.einsum('tf,srf->tsr', hidden_acts[0], arrived_up[0], preferred_elemen...  21.7 us
    convert_element_type x1, local copies, waits for them, and re-layouts, body(): outgoing_up = jnp.einsum('dsq,qrf->dsrf', slot_hits, spread_up, preferred...  20.2 us
    all_to_all x1, waiting for transfers between devices, body(): lax.all_to_all(up_factors[:, 0], 'dp', split_axis=1, concat_axis=0, tiled...  17.2 us
    unnamed x2, other arithmetic  16.2 us
    unnamed x24, local copies, waits for them, and re-layouts  15.1 us
  transfers between devices with their start and end apart: 7, of which 5 were waited for; matrix products, arithmetic and copies ran while one was open for 14% of the time, Pallas kernels for 0%

commit v1 on v0

v1 whole, which is shorter than its diff:
```python
import functools

import jax
import jax.numpy as jnp
from jax import lax
from jax.experimental import pallas as pl
from jax.experimental.pallas import tpu as pltpu
from jax.sharding import PartitionSpec as P

EPSILON = 1e-05
SIDE = 4
CORES = 2
RELATIVE = (0, 3, 1, 2)


def device_id(y, z, c):
    return ((y % SIDE) * SIDE + z % SIDE) * CORES + c % CORES


def shifted(block, dy=0, dz=0, dc=0):
    route = [
        (device_id(y, z, c), device_id(y + dy, z + dz, c + dc))
        for y in range(SIDE)
        for z in range(SIDE)
        for c in range(CORES)
    ]
    return lax.ppermute(block, "dp", route)


def chain_kernel(inputs_ref, gains_ref, top_ref, out_ref):
    sections = inputs_ref.shape[0]
    out_ref[sections - 1] = top_ref[...]
    cotangent = top_ref[...].astype(jnp.float32)
    for layer in range(sections - 1, 0, -1):
        values = inputs_ref[layer].astype(jnp.float32)
        inverse = lax.rsqrt(jnp.mean(values * values, axis=-1, keepdims=True) + EPSILON)
        normed = values * inverse
        scaled = gains_ref[layer : layer + 1, :].astype(jnp.float32) * cotangent
        pulled = jnp.mean(normed * scaled, axis=-1, keepdims=True)
        cotangent = cotangent + scaled * inverse - normed * inverse * pulled
        out_ref[layer - 1] = cotangent.astype(out_ref.dtype)


def chain(inputs, gains, top):
    sections, rows, width = inputs.shape
    step = 16
    return pl.pallas_call(
        chain_kernel,
        grid=(rows // step,),
        in_specs=[
            pl.BlockSpec((sections, step, width), lambda i: (0, i, 0)),
            pl.BlockSpec((sections, width), lambda i: (0, 0)),
            pl.BlockSpec((step, width), lambda i: (i, 0)),
        ],
        out_specs=pl.BlockSpec((sections, step, width), lambda i: (0, i, 0)),
        out_shape=jax.ShapeDtypeStruct(inputs.shape, jnp.bfloat16),
        compiler_params=pltpu.CompilerParams(vmem_limit_bytes=48 << 20),
        cost_estimate=pl.CostEstimate(
            flops=40 * rows * width, bytes_accessed=18 * rows * width, transcendentals=0
        ),
        name="cotangent_chain",
    )(inputs, gains, top)


def proj_kernel(capacity, where_ref, tokens_ref, *refs):
    del where_ref
    factor_refs, out_ref, total_ref = refs[:capacity], refs[capacity], refs[capacity + 1]
    step = pl.program_id(0)
    factors = jnp.concatenate([ref[0] for ref in factor_refs], axis=0)
    part = lax.dot_general(
        factors, tokens_ref[...], (((1,), (1,)), ((), ())), preferred_element_type=jnp.float32
    )

    @pl.when(step == 0)
    def _():
        total_ref[...] = part

    @pl.when(step > 0)
    def _():
        total_ref[...] += part

    @pl.when(step == pl.num_programs(0) - 1)
    def _():
        out_ref[...] = total_ref[...].astype(out_ref.dtype)


def project(tokens, factors, where, first, block, dtype):
    rows, width = tokens.shape
    rank = factors.shape[1]
    capacity = where.shape[0]
    offset = first // block

    def pick(slot):
        return pl.BlockSpec((1, rank, block), lambda k, where_ref: (where_ref[slot], 0, k + offset))

    return pl.pallas_call(
        functools.partial(proj_kernel, capacity),
        grid_spec=pltpu.PrefetchScalarGridSpec(
            num_scalar_prefetch=1,
            grid=(width // block,),
            in_specs=[pl.BlockSpec((rows, block), lambda k, where_ref: (0, k))]
            + [pick(slot) for slot in range(capacity)],
            out_specs=pl.BlockSpec((capacity * rank, rows), lambda k, where_ref: (0, 0)),
            scratch_shapes=[pltpu.VMEM((capacity * rank, rows), jnp.float32)],
        ),
        out_shape=jax.ShapeDtypeStruct((capacity * rank, rows), dtype),
        compiler_params=pltpu.CompilerParams(vmem_limit_bytes=32 << 20),
        cost_estimate=pl.CostEstimate(
            flops=2 * capacity * rank * rows * width,
            bytes_accessed=2 * width * (rows + capacity * rank),
            transcendentals=0,
        ),
        name="project",
    )(where, tokens, *([factors] * capacity))


def score_kernel(parts, hits_ref, live_ref, *refs):
    up_refs, down_refs, out_ref = refs[:parts], refs[parts : 2 * parts], refs[2 * parts]
    capacity = hits_ref.shape[1]
    rank = up_refs[0].shape[0] // capacity
    up = sum(ref[...].astype(jnp.float32) for ref in up_refs)
    down = sum(ref[...].astype(jnp.float32) for ref in down_refs)
    products = up * down
    dense = jnp.zeros((hits_ref.shape[0], products.shape[1]), jnp.float32)
    for slot in range(capacity):
        row = jnp.sum(products[slot * rank : (slot + 1) * rank], axis=0, keepdims=True)
        dense = dense + hits_ref[:, slot : slot + 1] * row
    out_ref[...] = (dense * live_ref[...]).T


def scores_of(hits, live, up_parts, down_parts):
    return pl.pallas_call(
        functools.partial(score_kernel, len(up_parts)),
        out_shape=jax.ShapeDtypeStruct((live.shape[1], hits.shape[0]), jnp.float32),
        name="scores",
    )(hits, live, *up_parts, *down_parts)


def spread(pieces_of, axis):
    return [
        pieces_of(0),
        shifted(pieces_of(1), **{axis: 1}),
        shifted(pieces_of(-1), **{axis: -1}),
        shifted(pieces_of(2), **{axis: 2}),
    ]


def gathered(block, axis):
    half = block.shape[0] // 2
    before = shifted(block, **{axis: 1})
    after = shifted(block, **{axis: -1})
    far_first = shifted(before[:half], **{axis: 1})
    far_second = shifted(after[half:], **{axis: -1})
    return jnp.concatenate([block, before, after, far_first, far_second], axis=0)


def body(
    hidden_acts,
    layer_inputs,
    norm_gains,
    top_cotangent,
    up_factors,
    down_factors,
    candidates,
    counts,
):
    sections = lax.axis_size("section")
    section = lax.axis_index("section")
    me = lax.axis_index("dp")
    shards = lax.axis_size("dp")
    c = me % CORES
    z = (me // CORES) % SIDE
    y = me // (CORES * SIDE)
    rows, width = layer_inputs.shape[1:]
    hidden = hidden_acts[0]
    up, down = up_factors[0, 0], down_factors[0, 0]
    ff = hidden.shape[1]
    rank = up.shape[0]
    up_wide, down_wide = ff // (2 * SIDE), width // (2 * SIDE)

    def columns(array, half, place, wide):
        start = half * SIDE * wide + (place % SIDE) * wide
        return lax.dynamic_slice_in_dim(array, start, wide, axis=1)

    queries, listed = candidates.shape
    capacity = listed + listed // 4
    member = jnp.any(
        candidates[:, :, None] == jnp.arange(shards, dtype=jnp.int32)[None, None, :], axis=1
    ).astype(jnp.int32)
    position = jnp.cumsum(member, axis=0) - member
    hits = (
        (member.T[:, None, :] == 1)
        & (position.T[:, None, :] == jnp.arange(capacity, dtype=jnp.int32)[None, :, None])
    )
    query = jnp.arange(queries, dtype=jnp.int32)
    order = jnp.array([0, 2, 3, 1], jnp.int32)
    far_y = order[(query // (CORES * SIDE) - y) % SIDE]
    far_z = order[(query // CORES % SIDE - z) % SIDE]
    other = (query % CORES != c).astype(jnp.int32) * SIDE * SIDE
    kept = (other + far_y * SIDE + far_z, other + far_z * SIDE + far_y)
    where = [jnp.sum(jnp.where(hits, place[None, None, :], 0), axis=2) for place in kept]
    own_hits = lax.dynamic_index_in_dim(hits, me, 0, keepdims=False).astype(jnp.float32).T
    live = (jnp.arange(rows, dtype=jnp.int32) < counts[0]).astype(jnp.float32)[None, :]

    places, axes, gather_axes = (z, y), ("dz", "dy"), ("dy", "dz")

    block = rows // sections
    inputs = lax.all_to_all(
        layer_inputs[0].reshape(sections, block, width), "section", 0, 0, tiled=True
    )
    gains = lax.all_gather(norm_gains, "section", axis=0, tiled=True)
    top = lax.dynamic_slice_in_dim(top_cotangent, section * block, block, axis=0)
    cotangents = chain(inputs, gains, top)
    cotangent = lax.all_to_all(cotangents, "section", 0, 0, tiled=True).reshape(rows, width)

    factors = []
    for half in range(2):
        pieces = spread(
            lambda d, half=half: jnp.concatenate(
                [
                    columns(up, half, places[half] + d, up_wide),
                    columns(down, half, places[half] + d, down_wide),
                ],
                axis=1,
            ),
            axes[half],
        )
        mine = gathered(jnp.concatenate(pieces, axis=0), gather_axes[half])
        whole = jnp.concatenate([mine, shifted(mine, dc=1)], axis=0)
        factors.append(whole.reshape(queries, rank, up_wide + down_wide))

    def shard_at(half, distance):
        if half == 0:
            return (y * SIDE + (z + distance) % SIDE) * CORES + c
        return (((y + distance) % SIDE) * SIDE + z) * CORES + c

    def partials(array, wide, first, block):
        parts = []
        for half in range(2):
            arrived = spread(
                lambda d, half=half: columns(array, half, places[half] + d, wide), axes[half]
            )
            for tokens, distance in zip(arrived, RELATIVE):
                listed_here = lax.dynamic_index_in_dim(
                    where[half], shard_at(half, distance), 0, keepdims=False
                )
                dtype = jnp.float32 if distance == 0 else jnp.bfloat16
                part = project(tokens, factors[half], listed_here, first, block, dtype)
                if distance:
                    part = shifted(part, **{axes[half]: distance})
                parts.append(part)
        return parts

    up_parts = partials(hidden, up_wide, 0, up_wide // 2)
    down_parts = partials(cotangent, down_wide, up_wide, down_wide // 2)
    return scores_of(own_hits, live, up_parts, down_parts)[None]


def solution(mesh):
    return jax.shard_map(
        body,
        mesh=mesh,
        in_specs=(
            P("section", "dp", None),
            P("section", "dp", None),
            P("section", None),
            P("dp", None),
            P("dp", "section", None, None),
            P("dp", "section", None, None),
            P(),
            P("dp"),
        ),
        out_specs=P("section", "dp", None),
        check_vma=False,
    )
```

time: 736 us -> 259 us (0.35)
  waiting for transfers between devices: 557 us -> 61.2 us
  Pallas kernels: 0 us -> 51.8 us
  matrix products: 43 us -> 0 us
  other arithmetic: 41.4 us -> 4.78 us
  blocking collectives: 0 us -> 32.5 us
  starting transfers between devices: 33.7 us -> 61 us
  local copies, waits for them, and re-layouts: 50.1 us -> 41.9 us
    all_to_all x4 -> x2, waiting for transfers between devices: 383 us -> 18.4 us  [the longest x1 18.4 us: body(): lax.all_to_all(cotangents, 'section', 0, 0, tiled=True).reshape(rows, width)]
    ppermute x3 -> x40, waiting for transfers between devices: 174 us -> 42.8 us  [shifted(): return lax.ppermute(block, 'dp', route)]
    pallas_call x0 -> x18, Pallas kernels: none -> 51.8 us  [the longest x16 44.8 us: project(): pl.pallas_call(functools.partial(proj_kernel, capacity), grid_spec=pltpu....]
    ppermute x3 -> x40, starting transfers between devices: 4.36 us -> 52.1 us  [shifted(): return lax.ppermute(block, 'dp', route)]
    dot_general x5 -> x0, matrix products: 43 us -> none  [the longest x1 21.7 us: body(): jnp.einsum('tf,srf->tsr', hidden_acts[0], arrived_up[0], preferred_elemen...]
    all_gather x0 -> x1, blocking collectives: none -> 32.5 us  [body(): gains = lax.all_gather(norm_gains, 'section', axis=0, tiled=True)]
    convert_element_type x2 -> x0, local copies, waits for them, and re-layouts: 26.6 us -> none  [the longest x1 20.2 us: body(): outgoing_up = jnp.einsum('dsq,qrf->dsrf', slot_hits, spread_up, preferred...]
    all_to_all x4 -> x2, starting transfers between devices: 29.3 us -> 8.88 us  [the longest x1 4.44 us: body(): lax.all_to_all(layer_inputs[0].reshape(sections, block, width), 'section'...]
  transfers between devices with their start and end apart: 7 -> 42, of which waited for: 5 -> 14; matrix products, arithmetic and copies ran while one was open for 14% -> 15% of each run, Pallas kernels for 0% -> 19%
where the time goes in v1:
time: 259 us; the launch traced here: 254 us
  waiting for transfers between devices  61.2 us (24%)
  starting transfers between devices  61 us (24%)
  Pallas kernels  51.8 us (20%)
  local copies, waits for them, and re-layouts  41.9 us (16%)
  blocking collectives  32.5 us (13%)
  other arithmetic  4.78 us (2%)
    ppermute x40, starting transfers between devices, shifted(): return lax.ppermute(block, 'dp', route)  52.1 us
    pallas_call x16, Pallas kernels, project(): pl.pallas_call(functools.partial(proj_kernel, capacity), grid_spec=pltpu....  44.8 us
    ppermute x40, waiting for transfers between devices, shifted(): return lax.ppermute(block, 'dp', route)  42.8 us
    all_gather x1, blocking collectives, body(): gains = lax.all_gather(norm_gains, 'section', axis=0, tiled=True)  32.5 us
    all_to_all x1, waiting for transfers between devices, body(): lax.all_to_all(cotangents, 'section', 0, 0, tiled=True).reshape(rows, width)  18.4 us
    unnamed x52, local copies, waits for them, and re-layouts  17.1 us
    dynamic_slice x4, local copies, waits for them, and re-layouts, columns(): return lax.dynamic_slice_in_dim(array, start, wide, axis=1)  11.1 us
    concatenate x2, local copies, waits for them, and re-layouts, body(): whole = jnp.concatenate([mine, shifted(mine, dc=1)], axis=0)  9.56 us
  transfers between devices with their start and end apart: 42, of which 14 were waited for; matrix products, arithmetic and copies ran while one was open for 15% of the time, Pallas kernels for 19%

profile of v1, /device:TPU:32, one launch (start us, length us, event | category | flops | bytes accessed | tf_op | source)
XLA Modules:
  0.0 254.4 jit_solution(18332764785953322801)
XLA Ops:
  6.4 2.1 collective-permute-start.16
  8.5 2.0 collective-permute-start
  13.1 3.0 %collective-permute-start.2 = (bf16[32,4608]{1,0:T(8,128)(2,1)S(1)}, bf16[32,4608]{1,0:T(8,128)(2,1)S(1)}, u32[]{:S(2)}, u32[]{:S(2)}) collective-permute-start(bf16[32,4608]{1,0:T(8,128)(2,1)S(1)} %pad_maximum_fusion.4), channel_id=1, source_target_pairs={{0,4},{1,5},{2,6},{3,7},{4,0},{5,1},{6,2},{7,3},{8,12},{9,13},{10,... | collective-permute-start | bytes 884744 | tf_op jit(solution)/shard_map/ppermute | solution.py:27
  16.1 4.5 %collective-permute-done.16 = bf16[32,4608]{1,0:T(8,128)(2,1)S(1)} collective-permute-done((bf16[32,4608]{1,0:T(8,128)(2,1)S(1)}, bf16[32,4608]{1,0:T(8,128)(2,1)S(1)}, u32[]{:S(2)}, u32[]{:S(2)}) %collective-permute-start.16) | collective-permute-done | bytes 294944 | tf_op jit(solution)/shard_map/ppermute | solution.py:27
  20.7 2.0 collective-permute-start.17
  22.8 3.4 %collective-permute-done.2 = bf16[32,4608]{1,0:T(8,128)(2,1)S(1)} collective-permute-done((bf16[32,4608]{1,0:T(8,128)(2,1)S(1)}, bf16[32,4608]{1,0:T(8,128)(2,1)S(1)}, u32[]{:S(2)}, u32[]{:S(2)}) %collective-permute-start.2) | collective-permute-done | bytes 294944 | tf_op jit(solution)/shard_map/ppermute | solution.py:27
  26.7 2.8 %collective-permute-start.4 = (bf16[128,4608]{1,0:T(8,128)(2,1)S(1)}, bf16[128,4608]{1,0:T(8,128)(2,1)S(1)}, u32[]{:S(2)}, u32[]{:S(2)}) collective-permute-start(bf16[128,4608]{1,0:T(8,128)(2,1)S(1)} %pad_maximum_fusion), channel_id=1, source_target_pairs={{0,24},{1,25},{2,26},{3,27},{4,28},{5,29},{6,30},{7,31},{8,0},{9,1... | collective-permute-start | bytes 3538952 | tf_op jit(solution)/shard_map/ppermute | solution.py:27
  34.6 13.7 %collective-permute-done.17 = bf16[128,4608]{1,0:T(8,128)(2,1)S(1)} collective-permute-done((bf16[128,4608]{1,0:T(8,128)(2,1)S(1)}, bf16[128,4608]{1,0:T(8,128)(2,1)S(1)}, u32[]{:S(2)}, u32[]{:S(2)}) %collective-permute-start.17) | collective-permute-done | bytes 1179680 | tf_op jit(solution)/shard_map/ppermute | solution.py:27
  48.4 1.7 collective-permute-start.19
  52.8 3.3 %collective-permute-start.6 = (bf16[64,4608]{1,0:T(8,128)(2,1)S(1)}, bf16[64,4608]{1,0:T(8,128)(2,1)S(1)}, u32[]{:S(2)}, u32[]{:S(2)}) collective-permute-start(bf16[64,4608]{1,0:T(8,128)(2,1)S(1)} %slice.27), channel_id=1, source_target_pairs={{0,24},{1,25},{2,26},{3,27},{4,28},{5,29},{6,30},{7,31},{8,0},{9,1... | collective-permute-start | bytes 1769480 | tf_op jit(solution)/shard_map/ppermute | solution.py:27
  62.4 2.7 %collective-permute-done.19 = bf16[64,4608]{1,0:T(8,128)(2,1)S(1)} collective-permute-done((bf16[64,4608]{1,0:T(8,128)(2,1)S(1)}, bf16[64,4608]{1,0:T(8,128)(2,1)S(1)}, u32[]{:S(2)}, u32[]{:S(2)}) %collective-permute-start.19) | collective-permute-done | bytes 589856 | tf_op jit(solution)/shard_map/ppermute | solution.py:27
  70.3 4.4 %all-to-all-start = ((bf16[4,32,8192]{2,1,0:T(8,128)(2,1)}), bf16[4,32,8192]{2,1,0:T(8,128)(2,1)}, u32[]{:S(2)}, u32[]{:S(2)}) async-start(bf16[4,32,8192]{2,1,0:T(8,128)(2,1)} %bitcast.96), calls=%async_computation | async-start | bytes 4194304 | tf_op jit(solution)/shard_map/all_to_all | solution.py:208
  74.8 32.5 %all-gather = bf16[4,1,8192]{2,1,0:T(2,128)(2,1)S(1)} all-gather(bf16[1,1,8192]{2,1,0:T(2,128)(2,1)S(1)} %bitcast.98), channel_id=1, replica_groups=mesh['section'=4,'dp'=32] {'section'}, dimensions={0}, use_global_device_ids=true | all-gather | bytes 81920 | tf_op jit(solution)/shard_map/all_gather | solution.py:211
  107.4 4.6 %cotangent_chain.1 = bf16[4,32,8192]{2,1,0:T(8,128)(2,1)} custom-call(bf16[4,32,8192]{2,1,0:T(8,128)(2,1)} %all-to-all-done.inputs_ref, bf16[4,8192]{1,0:T(4,128)(2,1)S(1)} %bitcast.95, bf16[32,8192]{1,0:T(8,128)(2,1)S(1)} %constant_dynamic-slice_fusion.7.top_ref), custom_call_target="tpu_custom_call" | custom-call | flops 10485760 | bytes 4718592 | tf_op jit(solution)/shard_map/cotangent_chain/pallas_call | solution.py:47
  112.0 4.4 %all-to-all-start.1 = ((bf16[4,32,8192]{2,1,0:T(8,128)(2,1)}), bf16[4,32,8192]{2,1,0:T(8,128)(2,1)}, u32[]{:S(2)}, u32[]{:S(2)}) async-start(bf16[4,32,8192]{2,1,0:T(8,128)(2,1)} %cotangent_chain.1), calls=%async_computation.1 | async-start | bytes 4194304 | tf_op jit(solution)/shard_map/all_to_all | solution.py:214
  116.5 5.6 %dynamic-slice_bitcast_fusion = (bf16[128,3584]{1,0:T(8,128)(2,1)}, bf16[128,3584]{1,0:T(8,128)(2,1)}, bf16[128,3584]{1,0:T(8,128)(2,1)S(1)}, bf16[128,3584]{1,0...) fusion(bf16[1,128,28672]{2,1,0:T(8,128)(2,1)} %param.9, ...), kind=kLoop, calls=%fused_computation.2 | loop fusion | bytes 14680096 | tf_op jit(solution)/shard_map/dynamic_slice | solution.py:183
  123.0 18.4 %all-to-all-done.1 = bf16[4,32,8192]{2,1,0:T(8,128)(2,1)} async-done(((bf16[4,32,8192]{2,1,0:T(8,128)(2,1)}), bf16[4,32,8192]{2,1,0:T(8,128)(2,1)}, u32[]{:S(2)}, u32[]{:S(2)}) %all-to-all-start.1) | async-done | bytes 2097184 | tf_op jit(solution)/shard_map/all_to_all | solution.py:214
  141.4 2.6 %constant_dynamic-slice_fusion.16 = (bf16[128,1024]{1,0:T(8,128)(2,1)S(1)}, bf16[128,1024]{1,0:T(8,128)(2,1)}, bf16[128,1024]{1,0:T(8,128)(2,1)}, bf16[128,1024]...) fusion(bf16[128,8192]{1,0:T(8,128)(2,1)} %bitcast.43, ...), kind=kLoop, calls=%fused_computation.94 | loop fusion | bytes 4194336 | tf_op jit(solution)/shard_map/dynamic_slice | solution.py:183
  148.3 5.5 %collective-permute-done.38.tokens_ref = bf16[128,1024]{1,0:T(8,128)(2,1)S(1)} collective-permute-done((bf16[128,1024]{1,0:T(8,128)(2,1)S(1)}, bf16[128,1024]{1,0:T(8,128)(2,1)S(1)}, u32[]{:S(2)}, u32[]{:S(2)}) %collective-permute-start.38) | collective-permute-done | bytes 262176 | tf_op jit(solution)/shard_map/ppermute | solution.py:27
  153.8 2.1 collective-permute-done.36.tokens_ref
  155.8 2.9 %collective-permute-start.30 = (bf16[128,1024]{1,0:T(8,128)(2,1)}, bf16[128,1024]{1,0:T(8,128)(2,1)}, u32[]{:S(2)}, u32[]{:S(2)}) collective-permute-start(bf16[128,1024]{1,0:T(8,128)(2,1)} %get-tuple-element.20), channel_id=1, source_target_pairs={{0,6},{1,7},{2,0},{3,1},{4,2},{5,3},{6,4},{7,5},{8,14},{9,15},{10,... | collective-permute-start | bytes 786440 | tf_op jit(solution)/shard_map/ppermute | solution.py:27
  160.9 3.0 %collective-permute-done.28.tokens_ref = bf16[128,1024]{1,0:T(8,128)(2,1)S(1)} collective-permute-done((bf16[128,1024]{1,0:T(8,128)(2,1)}, bf16[128,1024]{1,0:T(8,128)(2,1)S(1)}, u32[]{:S(2)}, u32[]{:S(2)}) %collective-permute-start.28) | collective-permute-done | bytes 262176 | tf_op jit(solution)/shard_map/ppermute | solution.py:27
  166.0 3.0 %collective-permute-done.32.tokens_ref = bf16[128,1024]{1,0:T(8,128)(2,1)} collective-permute-done((bf16[128,1024]{1,0:T(8,128)(2,1)}, bf16[128,1024]{1,0:T(8,128)(2,1)}, u32[]{:S(2)}, u32[]{:S(2)}) %collective-permute-start.32) | collective-permute-done | bytes 262176 | tf_op jit(solution)/shard_map/ppermute | solution.py:27
  169.0 3.4 %collective-permute-start.12 = (bf16[128,3584]{1,0:T(8,128)(2,1)}, bf16[128,3584]{1,0:T(8,128)(2,1)}, u32[]{:S(2)}, u32[]{:S(2)}) collective-permute-start(bf16[128,3584]{1,0:T(8,128)(2,1)} %get-tuple-element.10), channel_id=1, source_target_pairs={{0,4},{1,5},{2,6},{3,7},{4,0},{5,1},{6,2},{7,3},{8,12},{9,13},{10,... | collective-permute-start | bytes 2752520 | tf_op jit(solution)/shard_map/ppermute | solution.py:27
  172.5 2.0 collective-permute-start.8
  174.5 4.7 %constant_dynamic-update-slice_fusion.22 = bf16[1024,4608]{1,0:T(8,128)(2,1)} fusion(bf16[1024,4608]{1,0:T(8,128)(2,1)} %get-tuple-element.40, bf16[512,4608]{1,0:T(8,128)(2,1)} %collective-permute-done.21), kind=kLoop, calls=%fused_computation.58 | loop fusion | bytes 9437184 | tf_op jit(solution)/shard_map/concatenate | solution.py:229
  179.2 2.3 project.31
  181.5 2.3 project.30
  183.8 2.6 %project.29 = bf16[320,128]{1,0:T(8,128)(2,1)S(1)} custom-call(s32[10]{0:T(128)S(1)} %get-tuple-element.73.where_ref, bf16[128,1024]{1,0:T(8,128)(2,1)S(1)} %collective-permute-done.34.tokens_ref, bf16[32,32,4608]{2,1,0:T(8,128)(2,1)} %bitcast.34.refs_0_.refs_1_.refs_2_.refs_3_.refs_4_.refs_5_.refs_6_.refs_7_.refs_8_.refs_9_, ...), custom_call_target="tpu_custom_call" | custom-call | flops 83886080 | bytes 917504 | tf_op jit(solution)/shard_map/project/pallas_call | solution.py:96
  186.4 4.8 %constant_dynamic-update-slice_fusion.7 = bf16[1024,4608]{1,0:T(8,128)(2,1)} fusion(bf16[1024,4608]{1,0:T(8,128)(2,1)} %get-tuple-element.44, bf16[512,4608]{1,0:T(8,128)(2,1)} %collective-permute-done.7), kind=kLoop, calls=%fused_computation.43 | loop fusion | bytes 9437184 | tf_op jit(solution)/shard_map/concatenate | solution.py:229
  191.2 2.3 project.25
  193.5 2.4 project.26
  195.9 2.4 project.27
  199.3 3.4 %collective-permute-start.37 = (bf16[320,128]{1,0:T(8,128)(2,1)S(1)}, bf16[320,128]{1,0:T(8,128)(2,1)S(1)}, u32[]{:S(2)}, u32[]{:S(2)}) collective-permute-start(bf16[320,128]{1,0:T(8,128)(2,1)S(1)} %project.30), channel_id=1, source_target_pairs={{0,8},{1,9},{2,10},{3,11},{4,12},{5,13},{6,14},{7,15},{8,16},{9,17... | collective-permute-start | bytes 245768 | tf_op jit(solution)/shard_map/ppermute | solution.py:27
  202.7 3.2 %project.23 = bf16[320,128]{1,0:T(8,128)(2,1)S(1)} custom-call(s32[10]{0:T(128)S(1)} %get-tuple-element.71.where_ref, bf16[128,3584]{1,0:T(8,128)(2,1)} %collective-permute-done.26.tokens_ref, bf16[32,32,4608]{2,1,0:T(8,128)(2,1)} %bitcast.34.refs_0_.refs_1_.refs_2_.refs_3_.refs_4_.refs_5_.refs_6_.refs_7_.refs_8_.refs_9_, ...), custom_call_target="tpu_custom_call" | custom-call | flops 293601280 | bytes 3211264 | tf_op jit(solution)/shard_map/project/pallas_call | solution.py:96
  205.9 3.2 %project.22 = bf16[320,128]{1,0:T(8,128)(2,1)S(1)} custom-call(s32[10]{0:T(128)S(1)} %get-tuple-element.72.where_ref, bf16[128,3584]{1,0:T(8,128)(2,1)} %collective-permute-done.24.tokens_ref, bf16[32,32,4608]{2,1,0:T(8,128)(2,1)} %bitcast.34.refs_0_.refs_1_.refs_2_.refs_3_.refs_4_.refs_5_.refs_6_.refs_7_.refs_8_.refs_9_, ...), custom_call_target="tpu_custom_call" | custom-call | flops 293601280 | bytes 3211264 | tf_op jit(solution)/shard_map/project/pallas_call | solution.py:96
  209.1 3.5 %project.21 = bf16[320,128]{1,0:T(8,128)(2,1)S(1)} custom-call(s32[10]{0:T(128)S(1)} %get-tuple-element.73.where_ref, bf16[128,3584]{1,0:T(8,128)(2,1)} %collective-permute-done.22.tokens_ref, bf16[32,32,4608]{2,1,0:T(8,128)(2,1)} %bitcast.34.refs_0_.refs_1_.refs_2_.refs_3_.refs_4_.refs_5_.refs_6_.refs_7_.refs_8_.refs_9_, ...), custom_call_target="tpu_custom_call" | custom-call | flops 293601280 | bytes 3211264 | tf_op jit(solution)/shard_map/project/pallas_call | solution.py:96
  212.7 2.3 collective-permute-start.27
  215.5 2.7 %collective-permute-start.23 = (bf16[320,128]{1,0:T(8,128)(2,1)S(1)}, bf16[320,128]{1,0:T(8,128)(2,1)S(1)}, u32[]{:S(2)}, u32[]{:S(2)}) collective-permute-start(bf16[320,128]{1,0:T(8,128)(2,1)S(1)} %project.21), channel_id=1, source_target_pairs={{0,24},{1,25},{2,26},{3,27},{4,28},{5,29},{6,30},{7,31},{8,0},{9,1... | collective-permute-start | bytes 245768 | tf_op jit(solution)/shard_map/ppermute | solution.py:27
  219.1 3.3 %project.19 = bf16[320,128]{1,0:T(8,128)(2,1)S(1)} custom-call(s32[10]{0:T(128)S(1)} %get-tuple-element.75.where_ref, bf16[128,3584]{1,0:T(8,128)(2,1)} %collective-permute-done.12.tokens_ref, bf16[32,32,4608]{2,1,0:T(8,128)(2,1)} %bitcast.17.refs_0_.refs_1_.refs_2_.refs_3_.refs_4_.refs_5_.refs_6_.refs_7_.refs_8_.refs_9_, ...), custom_call_target="tpu_custom_call" | custom-call | flops 293601280 | bytes 3211264 | tf_op jit(solution)/shard_map/project/pallas_call | solution.py:96
  222.5 3.2 %project.18 = bf16[320,128]{1,0:T(8,128)(2,1)S(1)} custom-call(s32[10]{0:T(128)S(1)} %get-tuple-element.76.where_ref, bf16[128,3584]{1,0:T(8,128)(2,1)} %collective-permute-done.10.tokens_ref, bf16[32,32,4608]{2,1,0:T(8,128)(2,1)} %bitcast.17.refs_0_.refs_1_.refs_2_.refs_3_.refs_4_.refs_5_.refs_6_.refs_7_.refs_8_.refs_9_, ...), custom_call_target="tpu_custom_call" | custom-call | flops 293601280 | bytes 3211264 | tf_op jit(solution)/shard_map/project/pallas_call | solution.py:96
  225.7 3.2 %project.17 = bf16[320,128]{1,0:T(8,128)(2,1)S(1)} custom-call(s32[10]{0:T(128)S(1)} %get-tuple-element.77.where_ref, bf16[128,3584]{1,0:T(8,128)(2,1)} %collective-permute-done.8.tokens_ref, bf16[32,32,4608]{2,1,0:T(8,128)(2,1)} %bitcast.17.refs_0_.refs_1_.refs_2_.refs_3_.refs_4_.refs_5_.refs_6_.refs_7_.refs_8_.refs_9_, ...), custom_call_target="tpu_custom_call" | custom-call | flops 293601280 | bytes 3211264 | tf_op jit(solution)/shard_map/project/pallas_call | solution.py:96
  230.6 3.0 %collective-permute-start.33 = (bf16[320,128]{1,0:T(8,128)(2,1)S(1)}, bf16[320,128]{1,0:T(8,128)(2,1)S(1)}, u32[]{:S(2)}, u32[]{:S(2)}) collective-permute-start(bf16[320,128]{1,0:T(8,128)(2,1)S(1)} %project.27), channel_id=1, source_target_pairs={{0,4},{1,5},{2,6},{3,7},{4,0},{5,1},{6,2},{7,3},{8,12},{9,13},{10,... | collective-permute-start | bytes 245768 | tf_op jit(solution)/shard_map/ppermute | solution.py:27
  236.7 2.3 project.28.refs_12_
  239.1 2.3 project.24.refs_8_
  241.4 3.2 %project.20.refs_4_ = f32[320,128]{1,0:T(8,128)S(1)} custom-call(s32[10]{0:T(128)S(1)} %get-tuple-element.74.where_ref, bf16[128,3584]{1,0:T(8,128)(2,1)S(1)} %get-tuple-element.9.tokens_ref, bf16[32,32,4608]{2,1,0:T(8,128)(2,1)} %bitcast.34.refs_0_.refs_1_.refs_2_.refs_3_.refs_4_.refs_5_.refs_6_.refs_7_.refs_8_.refs_9_, ...), custom_call_target="tpu_custom_call" | custom-call | flops 293601280 | bytes 3211264 | tf_op jit(solution)/shard_map/project/pallas_call | solution.py:96
  245.3 3.2 %project.16.refs_0_ = f32[320,128]{1,0:T(8,128)S(1)} custom-call(s32[10]{0:T(128)S(1)} %get-tuple-element.78.where_ref, bf16[128,3584]{1,0:T(8,128)(2,1)S(1)} %get-tuple-element.13.tokens_ref, bf16[32,32,4608]{2,1,0:T(8,128)(2,1)} %bitcast.17.refs_0_.refs_1_.refs_2_.refs_3_.refs_4_.refs_5_.refs_6_.refs_7_.refs_8_.refs_9_, ...), custom_call_target="tpu_custom_call" | custom-call | flops 293601280 | bytes 3211264 | tf_op jit(solution)/shard_map/project/pallas_call | solution.py:96
  250.5 2.4 scores.1
  (143 shorter events, 49.4 us)
Async XLA Ops:
  0.0 107.4 %copy-start = (bf16[128,8192]{1,0:T(8,128)(2,1)S(1)}, bf16[128,8192]{1,0:T(8,128)(2,1)}, u32[]{:S(2)}) copy-start(bf16[128,8192]{1,0:T(8,128)(2,1)} %param.12) | copy-start | bytes 6291460
  3.0 10.1 %collective-permute-start.14 = (bf16[32,4608]{1,0:T(8,128)(2,1)S(1)}, bf16[32,4608]{1,0:T(8,128)(2,1)S(1)}, u32[]{:S(2)}, u32[]{:S(2)}) collective-permute-start(bf16[32,4608]{1,0:T(8,128)(2,1)S(1)} %pad_maximum_fusion.6), channel_id=1, source_target_pairs={{0,8},{1,9},{2,10},{3,11},{4,12},{5,13},{6,14},{7,15},{8,16},{9,17... | collective-permute-start | bytes 884744 | tf_op jit(solution)/shard_map/ppermute | solution.py:27
  4.7 11.4 %collective-permute-start.15 = (bf16[32,4608]{1,0:T(8,128)(2,1)S(1)}, bf16[32,4608]{1,0:T(8,128)(2,1)S(1)}, u32[]{:S(2)}, u32[]{:S(2)}) collective-permute-start(bf16[32,4608]{1,0:T(8,128)(2,1)S(1)} %pad_maximum_fusion.7), channel_id=1, source_target_pairs={{0,24},{1,25},{2,26},{3,27},{4,28},{5,29},{6,30},{7,31},{8,0},{9,1... | collective-permute-start | bytes 884744 | tf_op jit(solution)/shard_map/ppermute | solution.py:27
  6.4 14.2 %collective-permute-start.16 = (bf16[32,4608]{1,0:T(8,128)(2,1)S(1)}, bf16[32,4608]{1,0:T(8,128)(2,1)S(1)}, u32[]{:S(2)}, u32[]{:S(2)}) collective-permute-start(bf16[32,4608]{1,0:T(8,128)(2,1)S(1)} %pad_maximum_fusion.8), channel_id=1, source_target_pairs={{0,16},{1,17},{2,18},{3,19},{4,20},{5,21},{6,22},{7,23},{8,24},{9,... | collective-permute-start | bytes 884744 | tf_op jit(solution)/shard_map/ppermute | solution.py:27
  8.5 14.3 %collective-permute-start = (bf16[32,4608]{1,0:T(8,128)(2,1)S(1)}, bf16[32,4608]{1,0:T(8,128)(2,1)S(1)}, u32[]{:S(2)}, u32[]{:S(2)}) collective-permute-start(bf16[32,4608]{1,0:T(8,128)(2,1)S(1)} %pad_maximum_fusion.2), channel_id=1, source_target_pairs={{0,2},{1,3},{2,4},{3,5},{4,6},{5,7},{6,0},{7,1},{8,10},{9,11},{10,... | collective-permute-start | bytes 884744 | tf_op jit(solution)/shard_map/ppermute | solution.py:27
  10.5 12.2 %collective-permute-start.1 = (bf16[32,4608]{1,0:T(8,128)(2,1)S(1)}, bf16[32,4608]{1,0:T(8,128)(2,1)S(1)}, u32[]{:S(2)}, u32[]{:S(2)}) collective-permute-start(bf16[32,4608]{1,0:T(8,128)(2,1)S(1)} %pad_maximum_fusion.3), channel_id=1, source_target_pairs={{0,6},{1,7},{2,0},{3,1},{4,2},{5,3},{6,4},{7,5},{8,14},{9,15},{10,... | collective-permute-start | bytes 884744 | tf_op jit(solution)/shard_map/ppermute | solution.py:27
  13.1 13.0 %collective-permute-start.2 = (bf16[32,4608]{1,0:T(8,128)(2,1)S(1)}, bf16[32,4608]{1,0:T(8,128)(2,1)S(1)}, u32[]{:S(2)}, u32[]{:S(2)}) collective-permute-start(bf16[32,4608]{1,0:T(8,128)(2,1)S(1)} %pad_maximum_fusion.4), channel_id=1, source_target_pairs={{0,4},{1,5},{2,6},{3,7},{4,0},{5,1},{6,2},{7,3},{8,12},{9,13},{10,... | collective-permute-start | bytes 884744 | tf_op jit(solution)/shard_map/ppermute | solution.py:27
  20.7 27.7 %collective-permute-start.17 = (bf16[128,4608]{1,0:T(8,128)(2,1)S(1)}, bf16[128,4608]{1,0:T(8,128)(2,1)S(1)}, u32[]{:S(2)}, u32[]{:S(2)}) collective-permute-start(bf16[128,4608]{1,0:T(8,128)(2,1)S(1)} %pad_maximum_fusion.1), channel_id=1, source_target_pairs={{0,2},{1,3},{2,4},{3,5},{4,6},{5,7},{6,0},{7,1},{8,10},{9,11},{10,... | collective-permute-start | bytes 3538952 | tf_op jit(solution)/shard_map/ppermute | solution.py:27
  22.6 28.2 %collective-permute-start.18 = (bf16[128,4608]{1,0:T(8,128)(2,1)S(1)}, bf16[128,4608]{1,0:T(8,128)(2,1)S(1)}, u32[]{:S(2)}, u32[]{:S(2)}) collective-permute-start(bf16[128,4608]{1,0:T(8,128)(2,1)S(1)} %pad_maximum_fusion.1), channel_id=1, source_target_pairs={{0,6},{1,7},{2,0},{3,1},{4,2},{5,3},{6,4},{7,5},{8,14},{9,15},{10,... | collective-permute-start | bytes 3538952 | tf_op jit(solution)/shard_map/ppermute | solution.py:27
  26.2 26.4 %collective-permute-start.3 = (bf16[128,4608]{1,0:T(8,128)(2,1)S(1)}, bf16[128,4608]{1,0:T(8,128)(2,1)S(1)}, u32[]{:S(2)}, u32[]{:S(2)}) collective-permute-start(bf16[128,4608]{1,0:T(8,128)(2,1)S(1)} %pad_maximum_fusion), channel_id=1, source_target_pairs={{0,8},{1,9},{2,10},{3,11},{4,12},{5,13},{6,14},{7,15},{8,16},{9,17... | collective-permute-start | bytes 3538952 | tf_op jit(solution)/shard_map/ppermute | solution.py:27
  26.7 26.0 %collective-permute-start.4 = (bf16[128,4608]{1,0:T(8,128)(2,1)S(1)}, bf16[128,4608]{1,0:T(8,128)(2,1)S(1)}, u32[]{:S(2)}, u32[]{:S(2)}) collective-permute-start(bf16[128,4608]{1,0:T(8,128)(2,1)S(1)} %pad_maximum_fusion), channel_id=1, source_target_pairs={{0,24},{1,25},{2,26},{3,27},{4,28},{5,29},{6,30},{7,31},{8,0},{9,1... | collective-permute-start | bytes 3538952 | tf_op jit(solution)/shard_map/ppermute | solution.py:27
  48.4 16.8 %collective-permute-start.19 = (bf16[64,4608]{1,0:T(8,128)(2,1)S(1)}, bf16[64,4608]{1,0:T(8,128)(2,1)S(1)}, u32[]{:S(2)}, u32[]{:S(2)}) collective-permute-start(bf16[64,4608]{1,0:T(8,128)(2,1)S(1)} %slice.28), channel_id=1, source_target_pairs={{0,2},{1,3},{2,4},{3,5},{4,6},{5,7},{6,0},{7,1},{8,10},{9,11},{10,... | collective-permute-start | bytes 1769480 | tf_op jit(solution)/shard_map/ppermute | solution.py:27
  50.9 15.3 %collective-permute-start.20 = (bf16[64,4608]{1,0:T(8,128)(2,1)S(1)}, bf16[64,4608]{1,0:T(8,128)(2,1)S(1)}, u32[]{:S(2)}, u32[]{:S(2)}) collective-permute-start(bf16[64,4608]{1,0:T(8,128)(2,1)S(1)} %slice.29), channel_id=1, source_target_pairs={{0,6},{1,7},{2,0},{3,1},{4,2},{5,3},{6,4},{7,5},{8,14},{9,15},{10,... | collective-permute-start | bytes 1769480 | tf_op jit(solution)/shard_map/ppermute | solution.py:27
  52.6 15.4 %collective-permute-start.5 = (bf16[64,4608]{1,0:T(8,128)(2,1)S(1)}, bf16[64,4608]{1,0:T(8,128)(2,1)S(1)}, u32[]{:S(2)}, u32[]{:S(2)}) collective-permute-start(bf16[64,4608]{1,0:T(8,128)(2,1)S(1)} %slice.26), channel_id=1, source_target_pairs={{0,8},{1,9},{2,10},{3,11},{4,12},{5,13},{6,14},{7,15},{8,16},{9,17... | collective-permute-start | bytes 1769480 | tf_op jit(solution)/shard_map/ppermute | solution.py:27
  52.8 16.4 %collective-permute-start.6 = (bf16[64,4608]{1,0:T(8,128)(2,1)S(1)}, bf16[64,4608]{1,0:T(8,128)(2,1)S(1)}, u32[]{:S(2)}, u32[]{:S(2)}) collective-permute-start(bf16[64,4608]{1,0:T(8,128)(2,1)S(1)} %slice.27), channel_id=1, source_target_pairs={{0,24},{1,25},{2,26},{3,27},{4,28},{5,29},{6,30},{7,31},{8,0},{9,1... | collective-permute-start | bytes 1769480 | tf_op jit(solution)/shard_map/ppermute | solution.py:27
  66.2 8.6 %copy-start.17 = (bf16[1,8192]{1,0:T(2,128)(2,1)S(1)}, bf16[1,8192]{1,0:T(2,128)(2,1)}, u32[]{:S(2)}) copy-start(bf16[1,8192]{1,0:T(2,128)(2,1)} %param.11) | copy-start | bytes 49156
  67.3 105.1 %collective-permute-start.21 = (bf16[512,4608]{1,0:T(8,128)(2,1)}, bf16[512,4608]{1,0:T(8,128)(2,1)}, u32[]{:S(2)}, u32[]{:S(2)}) collective-permute-start(bf16[512,4608]{1,0:T(8,128)(2,1)} %get-tuple-element.39), channel_id=1, source_target_pairs={{0,1},{1,0},{2,3},{3,2},{4,5},{5,4},{6,7},{7,6},{8,9},{9,8},{10,11... | collective-permute-start | bytes 14155784 | tf_op jit(solution)/shard_map/ppermute | solution.py:27
  70.3 102.1 %collective-permute-start.7 = (bf16[512,4608]{1,0:T(8,128)(2,1)}, bf16[512,4608]{1,0:T(8,128)(2,1)}, u32[]{:S(2)}, u32[]{:S(2)}) collective-permute-start(bf16[512,4608]{1,0:T(8,128)(2,1)} %get-tuple-element.43), channel_id=1, source_target_pairs={{0,1},{1,0},{2,3},{3,2},{4,5},{5,4},{6,7},{7,6},{8,9},{9,8},{10,11... | collective-permute-start | bytes 14155784 | tf_op jit(solution)/shard_map/ppermute | solution.py:27
  70.3 37.1 %all-to-all-start = ((bf16[4,32,8192]{2,1,0:T(8,128)(2,1)}), bf16[4,32,8192]{2,1,0:T(8,128)(2,1)}, u32[]{:S(2)}, u32[]{:S(2)}) async-start(bf16[4,32,8192]{2,1,0:T(8,128)(2,1)} %bitcast.96), calls=%async_computation | async-start | bytes 4194304 | tf_op jit(solution)/shard_map/all_to_all | solution.py:208
  112.0 29.4 %all-to-all-start.1 = ((bf16[4,32,8192]{2,1,0:T(8,128)(2,1)}), bf16[4,32,8192]{2,1,0:T(8,128)(2,1)}, u32[]{:S(2)}, u32[]{:S(2)}) async-start(bf16[4,32,8192]{2,1,0:T(8,128)(2,1)} %cotangent_chain.1), calls=%async_computation.1 | async-start | bytes 4194304 | tf_op jit(solution)/shard_map/all_to_all | solution.py:214
  122.1 23.9 %collective-permute-start.26 = (bf16[128,3584]{1,0:T(8,128)(2,1)}, bf16[128,3584]{1,0:T(8,128)(2,1)}, u32[]{:S(2)}, u32[]{:S(2)}) collective-permute-start(bf16[128,3584]{1,0:T(8,128)(2,1)} %get-tuple-element.7), channel_id=1, source_target_pairs={{0,16},{1,17},{2,18},{3,19},{4,20},{5,21},{6,22},{7,23},{8,24},{9,... | collective-permute-start | bytes 2752520 | tf_op jit(solution)/shard_map/ppermute | solution.py:27
  144.0 9.7 %collective-permute-start.38 = (bf16[128,1024]{1,0:T(8,128)(2,1)S(1)}, bf16[128,1024]{1,0:T(8,128)(2,1)S(1)}, u32[]{:S(2)}, u32[]{:S(2)}) collective-permute-start(bf16[128,1024]{1,0:T(8,128)(2,1)S(1)} %get-tuple-element.15), channel_id=1, source_target_pairs={{0,16},{1,17},{2,18},{3,19},{4,20},{5,21},{6,22},{7,23},{8,24},{9,... | collective-permute-start | bytes 786440 | tf_op jit(solution)/shard_map/ppermute | solution.py:27
  144.5 11.4 %collective-permute-start.36 = (bf16[128,1024]{1,0:T(8,128)(2,1)}, bf16[128,1024]{1,0:T(8,128)(2,1)S(1)}, u32[]{:S(2)}, u32[]{:S(2)}) collective-permute-start(bf16[128,1024]{1,0:T(8,128)(2,1)} %get-tuple-element.16), channel_id=1, source_target_pairs={{0,24},{1,25},{2,26},{3,27},{4,28},{5,29},{6,30},{7,31},{8,0},{9,1... | collective-permute-start | bytes 786440 | tf_op jit(solution)/shard_map/ppermute | solution.py:27
  146.0 12.8 %collective-permute-start.34 = (bf16[128,1024]{1,0:T(8,128)(2,1)}, bf16[128,1024]{1,0:T(8,128)(2,1)S(1)}, u32[]{:S(2)}, u32[]{:S(2)}) collective-permute-start(bf16[128,1024]{1,0:T(8,128)(2,1)} %get-tuple-element.17), channel_id=1, source_target_pairs={{0,8},{1,9},{2,10},{3,11},{4,12},{5,13},{6,14},{7,15},{8,16},{9,17... | collective-permute-start | bytes 786440 | tf_op jit(solution)/shard_map/ppermute | solution.py:27
  153.8 10.2 %collective-permute-start.28 = (bf16[128,1024]{1,0:T(8,128)(2,1)}, bf16[128,1024]{1,0:T(8,128)(2,1)S(1)}, u32[]{:S(2)}, u32[]{:S(2)}) collective-permute-start(bf16[128,1024]{1,0:T(8,128)(2,1)} %get-tuple-element.21), channel_id=1, source_target_pairs={{0,2},{1,3},{2,4},{3,5},{4,6},{5,7},{6,0},{7,1},{8,10},{9,11},{10,... | collective-permute-start | bytes 786440 | tf_op jit(solution)/shard_map/ppermute | solution.py:27
  155.8 9.8 %collective-permute-start.30 = (bf16[128,1024]{1,0:T(8,128)(2,1)}, bf16[128,1024]{1,0:T(8,128)(2,1)}, u32[]{:S(2)}, u32[]{:S(2)}) collective-permute-start(bf16[128,1024]{1,0:T(8,128)(2,1)} %get-tuple-element.20), channel_id=1, source_target_pairs={{0,6},{1,7},{2,0},{3,1},{4,2},{5,3},{6,4},{7,5},{8,14},{9,15},{10,... | collective-permute-start | bytes 786440 | tf_op jit(solution)/shard_map/ppermute | solution.py:27
  158.8 10.3 %collective-permute-start.32 = (bf16[128,1024]{1,0:T(8,128)(2,1)}, bf16[128,1024]{1,0:T(8,128)(2,1)}, u32[]{:S(2)}, u32[]{:S(2)}) collective-permute-start(bf16[128,1024]{1,0:T(8,128)(2,1)} %get-tuple-element.19), channel_id=1, source_target_pairs={{0,4},{1,5},{2,6},{3,7},{4,0},{5,1},{6,2},{7,3},{8,12},{9,13},{10,... | collective-permute-start | bytes 786440 | tf_op jit(solution)/shard_map/ppermute | solution.py:27
  163.9 34.3 %collective-permute-start.24 = (bf16[128,3584]{1,0:T(8,128)(2,1)}, bf16[128,3584]{1,0:T(8,128)(2,1)}, u32[]{:S(2)}, u32[]{:S(2)}) collective-permute-start(bf16[128,3584]{1,0:T(8,128)(2,1)} %get-tuple-element.14), channel_id=1, source_target_pairs={{0,24},{1,25},{2,26},{3,27},{4,28},{5,29},{6,30},{7,31},{8,0},{9,1... | collective-permute-start | bytes 2752520 | tf_op jit(solution)/shard_map/ppermute | solution.py:27
  165.7 33.6 %collective-permute-start.22 = (bf16[128,3584]{1,0:T(8,128)(2,1)}, bf16[128,3584]{1,0:T(8,128)(2,1)}, u32[]{:S(2)}, u32[]{:S(2)}) collective-permute-start(bf16[128,3584]{1,0:T(8,128)(2,1)} %get-tuple-element.8), channel_id=1, source_target_pairs={{0,8},{1,9},{2,10},{3,11},{4,12},{5,13},{6,14},{7,15},{8,16},{9,17... | collective-permute-start | bytes 2752520 | tf_op jit(solution)/shard_map/ppermute | solution.py:27
  169.0 43.6 %collective-permute-start.12 = (bf16[128,3584]{1,0:T(8,128)(2,1)}, bf16[128,3584]{1,0:T(8,128)(2,1)}, u32[]{:S(2)}, u32[]{:S(2)}) collective-permute-start(bf16[128,3584]{1,0:T(8,128)(2,1)} %get-tuple-element.10), channel_id=1, source_target_pairs={{0,4},{1,5},{2,6},{3,7},{4,0},{5,1},{6,2},{7,3},{8,12},{9,13},{10,... | collective-permute-start | bytes 2752520 | tf_op jit(solution)/shard_map/ppermute | solution.py:27
  172.5 40.3 %collective-permute-start.10 = (bf16[128,3584]{1,0:T(8,128)(2,1)}, bf16[128,3584]{1,0:T(8,128)(2,1)}, u32[]{:S(2)}, u32[]{:S(2)}) collective-permute-start(bf16[128,3584]{1,0:T(8,128)(2,1)} %get-tuple-element.11), channel_id=1, source_target_pairs={{0,6},{1,7},{2,0},{3,1},{4,2},{5,3},{6,4},{7,5},{8,14},{9,15},{10,... | collective-permute-start | bytes 2752520 | tf_op jit(solution)/shard_map/ppermute | solution.py:27
  172.5 42.5 %collective-permute-start.8 = (bf16[128,3584]{1,0:T(8,128)(2,1)}, bf16[128,3584]{1,0:T(8,128)(2,1)}, u32[]{:S(2)}, u32[]{:S(2)}) collective-permute-start(bf16[128,3584]{1,0:T(8,128)(2,1)} %get-tuple-element.12), channel_id=1, source_target_pairs={{0,2},{1,3},{2,4},{3,5},{4,6},{5,7},{6,0},{7,1},{8,10},{9,11},{10,... | collective-permute-start | bytes 2752520 | tf_op jit(solution)/shard_map/ppermute | solution.py:27
  198.3 17.2 %collective-permute-start.39 = (bf16[320,128]{1,0:T(8,128)(2,1)S(1)}, bf16[320,128]{1,0:T(8,128)(2,1)S(1)}, u32[]{:S(2)}, u32[]{:S(2)}) collective-permute-start(bf16[320,128]{1,0:T(8,128)(2,1)S(1)} %project.31), channel_id=1, source_target_pairs={{0,16},{1,17},{2,18},{3,19},{4,20},{5,21},{6,22},{7,23},{8,24},{9,... | collective-permute-start | bytes 245768 | tf_op jit(solution)/shard_map/ppermute | solution.py:27
  199.3 18.9 %collective-permute-start.37 = (bf16[320,128]{1,0:T(8,128)(2,1)S(1)}, bf16[320,128]{1,0:T(8,128)(2,1)S(1)}, u32[]{:S(2)}, u32[]{:S(2)}) collective-permute-start(bf16[320,128]{1,0:T(8,128)(2,1)S(1)} %project.30), channel_id=1, source_target_pairs={{0,8},{1,9},{2,10},{3,11},{4,12},{5,13},{6,14},{7,15},{8,16},{9,17... | collective-permute-start | bytes 245768 | tf_op jit(solution)/shard_map/ppermute | solution.py:27
  212.6 16.2 %collective-permute-start.35 = (bf16[320,128]{1,0:T(8,128)(2,1)S(1)}, bf16[320,128]{1,0:T(8,128)(2,1)S(1)}, u32[]{:S(2)}, u32[]{:S(2)}) collective-permute-start(bf16[320,128]{1,0:T(8,128)(2,1)S(1)} %project.29), channel_id=1, source_target_pairs={{0,24},{1,25},{2,26},{3,27},{4,28},{5,29},{6,30},{7,31},{8,0},{9,1... | collective-permute-start | bytes 245768 | tf_op jit(solution)/shard_map/ppermute | solution.py:27
  212.7 17.9 %collective-permute-start.27 = (bf16[320,128]{1,0:T(8,128)(2,1)S(1)}, bf16[320,128]{1,0:T(8,128)(2,1)S(1)}, u32[]{:S(2)}, u32[]{:S(2)}) collective-permute-start(bf16[320,128]{1,0:T(8,128)(2,1)S(1)} %project.23), channel_id=1, source_target_pairs={{0,16},{1,17},{2,18},{3,19},{4,20},{5,21},{6,22},{7,23},{8,24},{9,... | collective-permute-start | bytes 245768 | tf_op jit(solution)/shard_map/ppermute | solution.py:27
  215.0 18.6 %collective-permute-start.25 = (bf16[320,128]{1,0:T(8,128)(2,1)S(1)}, bf16[320,128]{1,0:T(8,128)(2,1)S(1)}, u32[]{:S(2)}, u32[]{:S(2)}) collective-permute-start(bf16[320,128]{1,0:T(8,128)(2,1)S(1)} %project.22), channel_id=1, source_target_pairs={{0,8},{1,9},{2,10},{3,11},{4,12},{5,13},{6,14},{7,15},{8,16},{9,17... | collective-permute-start | bytes 245768 | tf_op jit(solution)/shard_map/ppermute | solution.py:27
  215.5 6.9 %copy-start.6 = (bf16[320,128]{1,0:T(8,128)(2,1)}, bf16[320,128]{1,0:T(8,128)(2,1)S(1)}, u32[]{:S(2)}) copy-start(bf16[320,128]{1,0:T(8,128)(2,1)S(1)} %collective-permute-done.39.refs_15_) | copy-start | bytes 245764
  215.5 18.6 %collective-permute-start.23 = (bf16[320,128]{1,0:T(8,128)(2,1)S(1)}, bf16[320,128]{1,0:T(8,128)(2,1)S(1)}, u32[]{:S(2)}, u32[]{:S(2)}) collective-permute-start(bf16[320,128]{1,0:T(8,128)(2,1)S(1)} %project.21), channel_id=1, source_target_pairs={{0,24},{1,25},{2,26},{3,27},{4,28},{5,29},{6,30},{7,31},{8,0},{9,1... | collective-permute-start | bytes 245768 | tf_op jit(solution)/shard_map/ppermute | solution.py:27
  218.9 15.8 %collective-permute-start.29 = (bf16[320,128]{1,0:T(8,128)(2,1)S(1)}, bf16[320,128]{1,0:T(8,128)(2,1)S(1)}, u32[]{:S(2)}, u32[]{:S(2)}) collective-permute-start(bf16[320,128]{1,0:T(8,128)(2,1)S(1)} %project.25), channel_id=1, source_target_pairs={{0,6},{1,7},{2,0},{3,1},{4,2},{5,3},{6,4},{7,5},{8,14},{9,15},{10,... | collective-permute-start | bytes 245768 | tf_op jit(solution)/shard_map/ppermute | solution.py:27
  228.9 10.1 %copy-start.8 = (bf16[320,128]{1,0:T(8,128)(2,1)}, bf16[320,128]{1,0:T(8,128)(2,1)S(1)}, u32[]{:S(2)}) copy-start(bf16[320,128]{1,0:T(8,128)(2,1)S(1)} %collective-permute-done.35.refs_13_) | copy-start | bytes 245764
  228.9 20.3 %collective-permute-start.31 = (bf16[320,128]{1,0:T(8,128)(2,1)S(1)}, bf16[320,128]{1,0:T(8,128)(2,1)S(1)}, u32[]{:S(2)}, u32[]{:S(2)}) collective-permute-start(bf16[320,128]{1,0:T(8,128)(2,1)S(1)} %project.26), channel_id=1, source_target_pairs={{0,2},{1,3},{2,4},{3,5},{4,6},{5,7},{6,0},{7,1},{8,10},{9,11},{10,... | collective-permute-start | bytes 245768 | tf_op jit(solution)/shard_map/ppermute | solution.py:27
  230.6 8.4 %copy-start.9 = (bf16[320,128]{1,0:T(8,128)(2,1)}, bf16[320,128]{1,0:T(8,128)(2,1)S(1)}, u32[]{:S(2)}) copy-start(bf16[320,128]{1,0:T(8,128)(2,1)S(1)} %collective-permute-done.27.refs_7_) | copy-start | bytes 245764
  230.6 18.6 %collective-permute-start.33 = (bf16[320,128]{1,0:T(8,128)(2,1)S(1)}, bf16[320,128]{1,0:T(8,128)(2,1)S(1)}, u32[]{:S(2)}, u32[]{:S(2)}) collective-permute-start(bf16[320,128]{1,0:T(8,128)(2,1)S(1)} %project.27), channel_id=1, source_target_pairs={{0,4},{1,5},{2,6},{3,7},{4,0},{5,1},{6,2},{7,3},{8,12},{9,13},{10,... | collective-permute-start | bytes 245768 | tf_op jit(solution)/shard_map/ppermute | solution.py:27
  233.6 15.6 %collective-permute-start.13 = (bf16[320,128]{1,0:T(8,128)(2,1)S(1)}, bf16[320,128]{1,0:T(8,128)(2,1)S(1)}, u32[]{:S(2)}, u32[]{:S(2)}) collective-permute-start(bf16[320,128]{1,0:T(8,128)(2,1)S(1)} %project.19), channel_id=1, source_target_pairs={{0,4},{1,5},{2,6},{3,7},{4,0},{5,1},{6,2},{7,3},{8,12},{9,13},{10,... | collective-permute-start | bytes 245768 | tf_op jit(solution)/shard_map/ppermute | solution.py:27
  234.1 15.1 %collective-permute-start.11 = (bf16[320,128]{1,0:T(8,128)(2,1)S(1)}, bf16[320,128]{1,0:T(8,128)(2,1)S(1)}, u32[]{:S(2)}, u32[]{:S(2)}) collective-permute-start(bf16[320,128]{1,0:T(8,128)(2,1)S(1)} %project.18), channel_id=1, source_target_pairs={{0,2},{1,3},{2,4},{3,5},{4,6},{5,7},{6,0},{7,1},{8,10},{9,11},{10,... | collective-permute-start | bytes 245768 | tf_op jit(solution)/shard_map/ppermute | solution.py:27
  234.7 15.8 %collective-permute-start.9 = (bf16[320,128]{1,0:T(8,128)(2,1)S(1)}, bf16[320,128]{1,0:T(8,128)(2,1)}, u32[]{:S(2)}, u32[]{:S(2)}) collective-permute-start(bf16[320,128]{1,0:T(8,128)(2,1)S(1)} %project.17), channel_id=1, source_target_pairs={{0,6},{1,7},{2,0},{3,1},{4,2},{5,3},{6,4},{7,5},{8,14},{9,15},{10,... | collective-permute-start | bytes 245768 | tf_op jit(solution)/shard_map/ppermute | solution.py:27
  245.3 9.1 %copy-start.1 = (bf16[128,8192]{1,0:T(8,128)(2,1)S(1)}, bf16[128,8192]{1,0:T(8,128)(2,1)}, u32[]{:S(2)}) copy-start(bf16[128,8192]{1,0:T(8,128)(2,1)} %param.12) | copy-start | bytes 6291460
  (13 other events, 31.6 us)

commit v2 on v0

v2 whole, which is shorter than its diff:
```python
import functools

import jax
import jax.numpy as jnp
from jax import lax
from jax.experimental import pallas as pl
from jax.experimental.pallas import tpu as pltpu
from jax.sharding import Mesh
from jax.sharding import PartitionSpec as P

EPSILON = 1e-05
SIDE = 4
CORES = 2
RELATIVE = (0, 3, 1, 2)
HBM = pl.BlockSpec(memory_space=pltpu.HBM)
SMEM = pl.BlockSpec(memory_space=pltpu.SMEM)
TOKEN = jax.ShapeDtypeStruct((8, 128), jnp.float32)
VMEM_BYTES = 48 << 20


def shifted(block, axis, distance):
    size = lax.axis_size(axis)
    return lax.ppermute(block, axis, [(i, (i + distance) % size) for i in range(size)])


def moved(copies):
    for into, _ in copies:
        for copy in into:
            copy.start()
    for into, out in copies:
        for copy in into:
            copy.wait()
        out.start()
    for _, out in copies:
        out.wait()


def joined_kernel(groups, arrays, *refs):
    sources, held, sems = refs[:arrays], refs[-2], refs[-1]
    outs = refs[-3 - len(groups) : -3]
    copies, row = [], 0
    for group, out_ref in zip(groups, outs):
        to = 0
        for source, first, rows in group:
            here, i = held.at[pl.ds(row + to, rows)], len(copies)
            into = pltpu.make_async_copy(sources[source].at[pl.ds(first, rows)], here, sems.at[0, i])
            out = pltpu.make_async_copy(here, out_ref.at[pl.ds(to, rows)], sems.at[1, i])
            copies.append(([into], out))
            to += rows
        row += to
    moved(copies)


def joined(groups, after):
    arrays = []
    listed = []
    for group in groups:
        for array, _, _ in group:
            if not any(array is known for known in arrays):
                arrays.append(array)
        index = lambda array: [array is known for known in arrays].index(True)
        listed.append([(index(array), first, rows) for array, first, rows in group])
    sizes = [sum(rows for _, _, rows in group) for group in listed]
    wide, dtype = arrays[0].shape[1], arrays[0].dtype
    *outs, token = pl.pallas_call(
        functools.partial(joined_kernel, listed, len(arrays)),
        in_specs=[HBM] * (len(arrays) + len(after)),
        out_specs=[HBM] * (len(sizes) + 1),
        out_shape=[jax.ShapeDtypeStruct((size, wide), dtype) for size in sizes] + [TOKEN],
        scratch_shapes=[
            pltpu.VMEM((sum(sizes), wide), dtype),
            pltpu.SemaphoreType.DMA((2, sum(len(group) for group in listed))),
        ],
        compiler_params=pltpu.CompilerParams(vmem_limit_bytes=VMEM_BYTES),
        name="joined",
    )(*arrays, *after)
    return outs, token


def cut_kernel(wides, halves, steps, place_ref, *refs):
    arrays = refs[: len(wides)]
    held, sems = refs[-2:]
    outs = refs[-3 - halves * len(steps) : -3]
    copies = []
    for half in range(halves):
        for i, step in enumerate(steps):
            at = half * len(steps) + i
            place = (place_ref[half] + step) % SIDE
            to, into = 0, []
            for array, (array_ref, wide) in enumerate(zip(arrays, wides)):
                start = pl.multiple_of((half * SIDE + place) * wide, 128)
                into.append(
                    pltpu.make_async_copy(
                        array_ref.at[:, pl.ds(start, wide)],
                        held.at[at, :, pl.ds(to, wide)],
                        sems.at[array, at],
                    )
                )
                to += wide
            out = pltpu.make_async_copy(held.at[at], outs[at], sems.at[len(wides), at])
            copies.append((into, out))
    moved(copies)


def cut(arrays, places, steps, after):
    halves = 2
    wides = tuple(array.shape[1] // (halves * SIDE) for array in arrays)
    rows, wide = arrays[0].shape[0], sum(wides)
    count = halves * len(steps)
    dtype = arrays[0].dtype
    *pieces, token = pl.pallas_call(
        functools.partial(cut_kernel, wides, halves, steps),
        in_specs=[SMEM] + [HBM] * (len(arrays) + len(after)),
        out_specs=[HBM] * (count + 1),
        out_shape=[jax.ShapeDtypeStruct((rows, wide), dtype)] * count + [TOKEN],
        scratch_shapes=[
            pltpu.VMEM((count, rows, wide), dtype),
            pltpu.SemaphoreType.DMA((len(arrays) + 1, count)),
        ],
        compiler_params=pltpu.CompilerParams(vmem_limit_bytes=VMEM_BYTES),
        name="cut",
    )(places, *arrays, *after)
    return pieces[: len(steps)], pieces[len(steps) :], token


def chain_kernel(section_ref, inputs_ref, top_ref, *refs):
    gain_refs, out_refs = refs[:SIDE], refs[-3:-1]
    sections = inputs_ref.shape[0]
    wide = out_refs[0].shape[-1]

    def give(layer, values):
        for half, out_ref in enumerate(out_refs):
            for place in range(SIDE):
                start = (half * SIDE + place) * wide
                out_ref[layer, place] = values[:, start : start + wide]

    cotangent = top_ref[...].astype(jnp.float32)
    give(sections - 1, top_ref[...])
    for layer in range(sections - 1, 0, -1):
        distance = lax.rem(layer - section_ref[0] + sections, sections)
        gain = gain_refs[0][...]
        for kept, far in enumerate(RELATIVE):
            gain = jnp.where(distance == far, gain_refs[kept][...], gain)
        values = inputs_ref[layer].astype(jnp.float32)
        inverse = lax.rsqrt(jnp.mean(values * values, axis=-1, keepdims=True) + EPSILON)
        normed = values * inverse
        scaled = gain.astype(jnp.float32) * cotangent
        pulled = jnp.mean(normed * scaled, axis=-1, keepdims=True)
        cotangent = cotangent + scaled * inverse - normed * inverse * pulled
        give(layer - 1, cotangent.astype(jnp.bfloat16))


def chain(section, inputs, top, gains, after):
    sections, rows, width = inputs.shape
    step = 16
    steps = rows // step
    wide = width // (2 * SIDE)
    out = jax.ShapeDtypeStruct((sections, SIDE, rows, wide), jnp.bfloat16)
    first, second, token = pl.pallas_call(
        chain_kernel,
        grid_spec=pltpu.PrefetchScalarGridSpec(
            num_scalar_prefetch=1,
            grid=(steps,),
            in_specs=[
                pl.BlockSpec((sections, step, width), lambda i, section_ref: (0, i, 0)),
                pl.BlockSpec((step, width), lambda i, section_ref: (section_ref[0] * steps + i, 0)),
            ]
            + [pl.BlockSpec((1, width), lambda i, section_ref: (0, 0))] * len(gains)
            + [HBM] * len(after),
            out_specs=[
                pl.BlockSpec((sections, SIDE, step, wide), lambda i, section_ref: (0, 0, i, 0))
            ]
            * 2
            + [HBM],
        ),
        out_shape=[out, out, TOKEN],
        compiler_params=pltpu.CompilerParams(vmem_limit_bytes=VMEM_BYTES),
        name="cotangent_chain",
    )(section, inputs, top, *gains, *after)
    return (first, second), token


def project_kernel(groups, up_wide, at_ref, where_ref, up_ref, down_ref, mine_ref, theirs_ref, *refs):
    out_ref, _, factor_ref, token_ref, sems = refs[-5:]
    capacity = where_ref.shape[0]
    rank = factor_ref.shape[0] // capacity
    held = mine_ref.shape[0] // rank
    blocks, rows, down_wide = down_ref.shape[0], down_ref.shape[2], down_ref.shape[3]

    def slot_copy(source, row, slot):
        return pltpu.make_async_copy(
            source.at[pl.ds(pl.multiple_of(row * rank, rank), rank)],
            factor_ref.at[pl.ds(slot * rank, rank)],
            sems.at[slot],
        )

    copies = [
        pltpu.make_async_copy(
            up_ref.at[:, pl.ds(pl.multiple_of(at_ref[0], 128), up_wide)],
            token_ref.at[:, pl.ds(0, up_wide)],
            sems.at[capacity],
        )
    ] + [
        pltpu.make_async_copy(
            down_ref.at[block, at_ref[1]],
            token_ref.at[pl.ds(block * rows, rows), pl.ds(up_wide, down_wide)],
            sems.at[capacity + 1 + block],
        )
        for block in range(blocks)
    ]
    for copy in copies:
        copy.start()
    for slot in range(capacity):
        row = where_ref[slot]

        @pl.when(row < held)
        def _(row=row, slot=slot):
            slot_copy(mine_ref, row, slot).start()

        @pl.when(row >= held)
        def _(row=row, slot=slot):
            slot_copy(theirs_ref, row - held, slot).start()

    for copy in copies:
        copy.wait()
    size = capacity * rank
    slots = capacity // groups
    for group in range(groups):
        for slot in range(group * slots, (group + 1) * slots):
            slot_copy(mine_ref, 0, slot).wait()
        first, last = group * slots * rank, (group + 1) * slots * rank
        for side, columns in enumerate((slice(0, up_wide), slice(up_wide, up_wide + down_wide))):
            part = lax.dot_general(
                factor_ref[first:last, columns],
                token_ref[:, columns],
                (((1,), (1,)), ((), ())),
                preferred_element_type=jnp.float32,
            )
            out_ref[side * size + first : side * size + last] = part.astype(out_ref.dtype)


def project(at, where, up_tokens, down_tokens, mine, theirs, rank, up_wide, dtype, after, groups=2):
    capacity = where.shape[0]
    rows = up_tokens.shape[0]
    wide = mine.shape[1]
    return pl.pallas_call(
        functools.partial(project_kernel, groups, up_wide),
        in_specs=[SMEM, SMEM] + [HBM] * (4 + len(after)),
        out_specs=[pl.BlockSpec(memory_space=pltpu.VMEM), HBM],
        out_shape=[jax.ShapeDtypeStruct((2 * capacity * rank, rows), dtype), TOKEN],
        scratch_shapes=[
            pltpu.VMEM((capacity * rank, wide), jnp.bfloat16),
            pltpu.VMEM((rows, wide), jnp.bfloat16),
            pltpu.SemaphoreType.DMA((capacity + 1 + down_tokens.shape[0],)),
        ],
        compiler_params=pltpu.CompilerParams(vmem_limit_bytes=VMEM_BYTES),
        name="project",
    )(at, where, up_tokens, down_tokens, mine, theirs, *after)


def score_kernel(hits_ref, live_ref, *refs):
    part_refs, out_ref = refs[:-1], refs[-1]
    capacity = hits_ref.shape[1]
    size = part_refs[0].shape[0] // 2
    rank = size // capacity
    total = sum(ref[...].astype(jnp.float32) for ref in part_refs)
    products = total[:size] * total[size:]
    dense = jnp.zeros((hits_ref.shape[0], products.shape[1]), jnp.float32)
    for slot in range(capacity):
        row = jnp.sum(products[slot * rank : (slot + 1) * rank], axis=0, keepdims=True)
        dense = dense + hits_ref[:, slot : slot + 1] * row
    out_ref[...] = dense * live_ref[...]


def scores_of(hits, live, parts):
    return pl.pallas_call(
        score_kernel,
        out_shape=jax.ShapeDtypeStruct((hits.shape[0], live.shape[1]), jnp.float32),
        name="scores",
    )(hits, live, *parts).T


def spread(pieces, axis):
    return [shifted(piece, axis, distance) for piece, distance in zip(pieces, (1, -1, 2))]


def body(
    hidden_acts,
    layer_inputs,
    norm_gains,
    top_cotangent,
    up_factors,
    down_factors,
    candidates,
    counts,
):
    sections = lax.axis_size("x")
    section, y, z, c = (lax.axis_index(axis) for axis in ("x", "y", "z", "c"))
    me = (y * SIDE + z) * CORES + c
    shards = SIDE * SIDE * CORES
    rows, width = layer_inputs.shape[1:]
    hidden = hidden_acts[0]
    up, down = up_factors[0, 0], down_factors[0, 0]
    rank, ff = up.shape
    up_wide = ff // (2 * SIDE)
    places = jnp.stack([z, y]).astype(jnp.int32)
    axes, other_axes = ("z", "y"), ("y", "z")
    halves = range(2)

    def whole(array):
        return (array, 0, array.shape[0])

    *pieces, token = cut([up, down], places, (0, 1, -1, 2), [])
    near, token = joined(
        [
            [whole(pieces[half][0])] + [whole(p) for p in spread(pieces[half][1:], axes[half])]
            for half in halves
        ],
        [token],
    )
    size = near[0].shape[0]
    before = [shifted(near[half], other_axes[half], 1) for half in halves]
    after = [shifted(near[half], other_axes[half], -1) for half in halves]
    *sent, token = cut([hidden], places, (1, -1, 2), [token])

    block = rows // sections
    gains = [norm_gains] + [shifted(norm_gains, "x", distance) for distance in (1, -1, 2)]
    inputs = lax.all_to_all(
        layer_inputs[0].reshape(sections, block, width), "x", 0, 0, tiled=True
    )
    cotangents, token = chain(
        section.reshape(1).astype(jnp.int32), inputs, top_cotangent, gains, [token]
    )
    down_tokens = [
        lax.all_to_all(
            cotangents[half].reshape(sections * SIDE, block, -1), ("x", axes[half]), 0, 0, tiled=True
        ).reshape(sections, SIDE, block, -1)
        for half in halves
    ]

    forward, token = joined(
        [[(array, half * size // 2, size // 2)] for half in halves for array in (before, after)[half]],
        [token],
    )
    far = [
        (shifted(forward[half], other_axes[half], 1), shifted(forward[2 + half], other_axes[half], -1))
        for half in halves
    ]
    arrived = [spread(sent[half], axes[half]) for half in halves]
    mine, token = joined(
        [
            [whole(near[half]), whole(before[half]), whole(after[half])]
            + [whole(part) for part in far[half]]
            for half in halves
        ],
        [token, arrived[0][2], down_tokens[0]],
    )
    theirs = [shifted(mine[half], "c", 1) for half in halves]

    queries, listed = candidates.shape
    capacity = listed + listed // 4
    member = jnp.any(
        candidates[:, :, None] == jnp.arange(shards, dtype=jnp.int32)[None, None, :], axis=1
    ).astype(jnp.int32)
    position = jnp.cumsum(member, axis=0) - member
    hits = (
        (member.T[:, None, :] == 1)
        & (position.T[:, None, :] == jnp.arange(capacity, dtype=jnp.int32)[None, :, None])
    )
    query = jnp.arange(queries, dtype=jnp.int32)
    order = jnp.array([0, 2, 3, 1], jnp.int32)
    far_y = order[(query // (CORES * SIDE) - y) % SIDE]
    far_z = order[(query // CORES % SIDE - z) % SIDE]
    other = (query % CORES != c).astype(jnp.int32) * SIDE * SIDE
    kept = (other + far_y * SIDE + far_z, other + far_z * SIDE + far_y)
    where = [jnp.sum(jnp.where(hits, place[None, None, :], 0), axis=2) for place in kept]
    own_hits = lax.dynamic_index_in_dim(hits, me, 0, keepdims=False).astype(jnp.float32).T
    live = (jnp.arange(rows, dtype=jnp.int32) < counts[0]).astype(jnp.float32)[None, :]

    parts = []
    for kept_at in range(SIDE):
        for half in halves:
            distance = RELATIVE[kept_at]
            place = (places[half] + distance) % SIDE
            shard = (
                (y * SIDE + place) * CORES + c if half == 0 else (place * SIDE + z) * CORES + c
            )
            column = jnp.int32(0) if distance else (half * SIDE + place) * up_wide
            part, token = project(
                jnp.stack([column, place]).astype(jnp.int32),
                lax.dynamic_index_in_dim(where[half], shard, 0, keepdims=False),
                arrived[half][kept_at - 1] if distance else hidden,
                down_tokens[half],
                mine[half],
                theirs[half],
                rank,
                up_wide,
                jnp.bfloat16 if distance else jnp.float32,
                [token],
            )
            parts.append(shifted(part, axes[half], distance) if distance else part)
    return scores_of(own_hits, live, parts)[None]


def solution(mesh):
    grid = Mesh(mesh.devices.reshape(-1, SIDE, SIDE, CORES), ("x", "y", "z", "c"))
    dp = ("y", "z", "c")
    return jax.shard_map(
        body,
        mesh=grid,
        in_specs=(
            P("x", dp, None),
            P("x", dp, None),
            P("x", None),
            P(dp, None),
            P(dp, "x", None, None),
            P(dp, "x", None, None),
            P(),
            P(dp),
        ),
        out_specs=P("x", dp, None),
        check_vma=False,
    )
```

time: 736 us -> 216 us (0.29); the launches traced: 727 us -> 215 us
  waiting for transfers between devices: 557 us -> 59.6 us
  Pallas kernels: 0 us -> 54.9 us
  starting transfers between devices: 33.7 us -> 81.6 us
  matrix products: 43 us -> 0 us
  other arithmetic: 41.4 us -> 2.79 us
  local copies, waits for them, and re-layouts: 50.1 us -> 14.5 us
    all_to_all x4 -> x3, waiting for transfers between devices: 383 us -> 0.96 us  [the longest x2 0.96 us: body(): lax.all_to_all(cotangents[half].reshape(sections * SIDE, block, -1), ('x'...]
    ppermute x3 -> x31, waiting for transfers between devices: 174 us -> 58.7 us  [shifted(): lax.ppermute(block, axis, [(i, (i + distance) % size) for i in range(size)])]
    ppermute x3 -> x31, starting transfers between devices: 4.36 us -> 64.6 us  [shifted(): lax.ppermute(block, axis, [(i, (i + distance) % size) for i in range(size)])]
    pallas_call x0 -> x15, Pallas kernels: none -> 54.9 us  [the longest x8 31 us: project(): pl.pallas_call(functools.partial(project_kernel, groups, up_wide), in_spe...]
    dot_general x5 -> x0, matrix products: 43 us -> none  [the longest x1 21.7 us: body(): jnp.einsum('tf,srf->tsr', hidden_acts[0], arrived_up[0], preferred_elemen...]
    convert_element_type x2 -> x0, local copies, waits for them, and re-layouts: 26.6 us -> none  [the longest x1 20.2 us: body(): outgoing_up = jnp.einsum('dsq,qrf->dsrf', slot_hits, spread_up, preferred...]
    unnamed x2 -> x0, other arithmetic: 16.2 us -> none
    sub x3 -> x0, other arithmetic: 14.6 us -> none  [transition(): cotangent + scaled * inverse]
  transfers between devices with their start and end apart: 7 -> 34, of which waited for: 5 -> 11; matrix products, arithmetic and copies ran while one was open for 14% -> 1% of each run, Pallas kernels for 0% -> 21%
where the time goes in v2:
time: 216 us; the launch traced here: 215 us
  starting transfers between devices  81.6 us (38%)
  waiting for transfers between devices  59.6 us (28%)
  Pallas kernels  54.9 us (25%)
  local copies, waits for them, and re-layouts  14.5 us (7%)
  other arithmetic  2.79 us (1%)
    ppermute x31, starting transfers between devices, shifted(): lax.ppermute(block, axis, [(i, (i + distance) % size) for i in range(size)])  64.6 us
    ppermute x31, waiting for transfers between devices, shifted(): lax.ppermute(block, axis, [(i, (i + distance) % size) for i in range(size)])  58.7 us
    pallas_call x8, Pallas kernels, project(): pl.pallas_call(functools.partial(project_kernel, groups, up_wide), in_spe...  31 us
    unnamed x49, local copies, waits for them, and re-layouts  14.3 us
    all_to_all x2, starting transfers between devices, body(): lax.all_to_all(cotangents[half].reshape(sections * SIDE, block, -1), ('x'...  12.5 us
    pallas_call x3, Pallas kernels, joined(): pl.pallas_call(functools.partial(joined_kernel, listed, len(arrays)), in_...  10.9 us
    pallas_call x2, Pallas kernels, cut(): pl.pallas_call(functools.partial(cut_kernel, wides, halves, steps), in_sp...  6.55 us
    all_to_all x1, starting transfers between devices, body(): lax.all_to_all(layer_inputs[0].reshape(sections, block, width), 'x', 0, 0...  4.42 us
  transfers between devices with their start and end apart: 34, of which 11 were waited for; matrix products, arithmetic and copies ran while one was open for 1% of the time, Pallas kernels for 21%

profile of v2, /device:TPU:32, one launch (start us, length us, event | category | flops | bytes accessed | tf_op | source)
XLA Modules:
  0.0 214.5 jit_solution(5093924452683814705)
XLA Ops:
  0.0 4.4 %all-to-all-start = ((bf16[4,32,8192]{2,1,0:T(8,128)(2,1)}), bf16[4,32,8192]{2,1,0:T(8,128)(2,1)S(1)}, u32[]{:S(2)}, u32[]{:S(2)}) async-start(bf16[4,32,8192]{2,1,0:T(8,128)(2,1)} %bitcast.77), calls=%async_computation | async-start | bytes 4194304 | tf_op jit(solution)/shard_map/all_to_all | solution.py:328
  4.5 1.5 copy-done.5
  6.0 2.1 cut.2
  8.1 2.0 collective-permute-start.3
  10.2 3.0 %collective-permute-start.5 = (bf16[32,4608]{1,0:T(8,128)(2,1)S(1)}, bf16[32,4608]{1,0:T(8,128)(2,1)S(1)}, u32[]{:S(2)}, u32[]{:S(2)}) collective-permute-start(bf16[32,4608]{1,0:T(8,128)(2,1)S(1)} %get-tuple-element.53), channel_id=1, source_target_pairs={{0,4},{2,6},{4,0},{6,2},{1,5},{3,7},{5,1},{7,3},{8,12},{10,14},{12... | collective-permute-start | bytes 884744 | tf_op jit(solution)/shard_map/ppermute | solution.py:23
  13.2 1.6 collective-permute-start.6
  14.8 1.7 collective-permute-start.7
  16.4 6.0 %collective-permute-done.3.refs_1_ = bf16[32,4608]{1,0:T(8,128)(2,1)S(1)} collective-permute-done((bf16[32,4608]{1,0:T(8,128)(2,1)S(1)}, bf16[32,4608]{1,0:T(8,128)(2,1)S(1)}, u32[]{:S(2)}, u32[]{:S(2)}) %collective-permute-start.3) | collective-permute-done | bytes 294944 | tf_op jit(solution)/shard_map/ppermute | solution.py:23
  22.5 3.2 %collective-permute-start.8 = (bf16[32,4608]{1,0:T(8,128)(2,1)S(1)}, bf16[32,4608]{1,0:T(8,128)(2,1)S(1)}, u32[]{:S(2)}, u32[]{:S(2)}) collective-permute-start(bf16[32,4608]{1,0:T(8,128)(2,1)S(1)} %get-tuple-element.57), channel_id=1, source_target_pairs={{0,16},{8,24},{16,0},{24,8},{1,17},{9,25},{17,1},{25,9},{2,18},{10... | collective-permute-start | bytes 884744 | tf_op jit(solution)/shard_map/ppermute | solution.py:23
  25.7 5.0 %collective-permute-done.8.refs_7_ = bf16[32,4608]{1,0:T(8,128)(2,1)S(1)} collective-permute-done((bf16[32,4608]{1,0:T(8,128)(2,1)S(1)}, bf16[32,4608]{1,0:T(8,128)(2,1)S(1)}, u32[]{:S(2)}, u32[]{:S(2)}) %collective-permute-start.8) | collective-permute-done | bytes 294944 | tf_op jit(solution)/shard_map/ppermute | solution.py:23
  30.7 2.0 joined.3
  32.7 3.1 %collective-permute-start.10 = (bf16[128,4608]{1,0:T(8,128)(2,1)}, bf16[128,4608]{1,0:T(8,128)(2,1)S(1)}, u32[]{:S(2)}, u32[]{:S(2)}) collective-permute-start(bf16[128,4608]{1,0:T(8,128)(2,1)} %get-tuple-element.62.refs_0_), channel_id=1, source_target_pairs={{0,24},{8,0},{16,8},{24,16},{1,25},{9,1},{17,9},{25,17},{2,26},{10... | collective-permute-start | bytes 3538952 | tf_op jit(solution)/shard_map/ppermute | solution.py:23
  35.8 3.4 %collective-permute-start.11 = (bf16[128,4608]{1,0:T(8,128)(2,1)}, bf16[128,4608]{1,0:T(8,128)(2,1)}, u32[]{:S(2)}, u32[]{:S(2)}) collective-permute-start(bf16[128,4608]{1,0:T(8,128)(2,1)} %get-tuple-element.63.refs_5_), channel_id=1, source_target_pairs={{0,2},{2,4},{4,6},{6,0},{1,3},{3,5},{5,7},{7,1},{8,10},{10,12},{12... | collective-permute-start | bytes 3538952 | tf_op jit(solution)/shard_map/ppermute | solution.py:23
  39.2 3.0 %collective-permute-start.1 = (bf16[1,8192]{1,0:T(2,128)(2,1)S(1)}, bf16[1,8192]{1,0:T(2,128)(2,1)S(1)}, u32[]{:S(2)}, u32[]{:S(2)}) collective-permute-start(bf16[1,8192]{1,0:T(2,128)(2,1)S(1)} %copy-done.14), channel_id=1, source_target_pairs={{0,96},{32,0},{64,32},{96,64},{1,97},{33,1},{65,33},{97,65},{2,98}... | collective-permute-start | bytes 49160 | tf_op jit(solution)/shard_map/ppermute | solution.py:23
  42.2 1.6 collective-permute-done.1.refs_2_
  45.2 4.0 %collective-permute-done.refs_1_ = bf16[1,8192]{1,0:T(2,128)(2,1)S(1)} collective-permute-done((bf16[1,8192]{1,0:T(2,128)(2,1)S(1)}, bf16[1,8192]{1,0:T(2,128)(2,1)S(1)}, u32[]{:S(2)}, u32[]{:S(2)}) %collective-permute-start) | collective-permute-done | bytes 16416 | tf_op jit(solution)/shard_map/ppermute | solution.py:23
  50.6 4.4 %cut.3 = (bf16[128,3584]{1,0:T(8,128)(2,1)}, bf16[128,3584]{1,0:T(8,128)(2,1)}, bf16[128,3584]{1,0:T(8,128)(2,1)S(1)}, bf16[128,3584]{1,0:T(8,128)(2,1)}, bf16[1...) custom-call(s32[2]{0:T(128)S(1)} %pad_add_fusion.7.place_ref, ...), custom_call_target="tpu_custom_call" | custom-call | tf_op jit(solution)/shard_map/cut/pallas_call | solution.py:111
  56.9 4.3 %cotangent_chain.1 = (bf16[4,4,32,1024]{3,2,1,0:T(8,128)(2,1)S(1)}, bf16[4,4,32,1024]{3,2,1,0:T(8,128)(2,1)}, f32[8,128]{1,0:T(8,128)S(1)}) custom-call(s32[1]{0:T(128)} %bitcast.11.section_ref, bf16[4,32,8192]{2,1,0:T(8,128)(2,1)S(1)} %all-to-all-done.inputs_ref, bf16[128,8192]{1,0:T(8,128)(2,1)} %top_ref.1, bf16[1,8192]{1,0:T(2,128)(2,1)S(1)} %copy-done.14, ...), custom_call_target="tpu_custom_call" | custom-call | tf_op jit(solution)/shard_map/cotangent_chain/pallas_call | solution.py:159
  62.2 6.9 %all-to-all-start.1 = ((bf16[16,32,1024]{2,1,0:T(8,128)(2,1)}), bf16[16,32,1024]{2,1,0:T(8,128)(2,1)S(1)}, u32[]{:S(2)}, u32[]{:S(2)}) async-start(bf16[16,32,1024]{2,1,0:T(8,128)(2,1)} %bitcast.72), calls=%async_computation.1 | async-start | bytes 2097152 | tf_op jit(solution)/shard_map/all_to_all | solution.py:335
  69.2 2.1 collective-permute-start.17
  71.3 2.1 joined.4
  74.6 2.2 %collective-permute-start.14 = (bf16[64,4608]{1,0:T(8,128)(2,1)S(1)}, bf16[64,4608]{1,0:T(8,128)(2,1)S(1)}, u32[]{:S(2)}, u32[]{:S(2)}) collective-permute-start(bf16[64,4608]{1,0:T(8,128)(2,1)S(1)} %get-tuple-element.66), channel_id=1, source_target_pairs={{0,24},{8,0},{16,8},{24,16},{1,25},{9,1},{17,9},{25,17},{2,26},{10... | collective-permute-start | bytes 1769480 | tf_op jit(solution)/shard_map/ppermute | solution.py:23
  76.8 2.0 collective-permute-start.16
  78.8 20.9 %collective-permute-done.17.refs_11_.up_ref = bf16[128,3584]{1,0:T(8,128)(2,1)S(1)} collective-permute-done((bf16[128,3584]{1,0:T(8,128)(2,1)}, bf16[128,3584]{1,0:T(8,128)(2,1)S(1)}, u32[]{:S(2)}, u32[]{:S(2)}) %collective-permute-start.17) | collective-permute-done | bytes 917536 | tf_op jit(solution)/shard_map/ppermute | solution.py:23
  99.7 6.8 %collective-permute-done.15.refs_8_ = bf16[64,4608]{1,0:T(8,128)(2,1)S(1)} collective-permute-done((bf16[64,4608]{1,0:T(8,128)(2,1)S(1)}, bf16[64,4608]{1,0:T(8,128)(2,1)S(1)}, u32[]{:S(2)}, u32[]{:S(2)}) %collective-permute-start.15) | collective-permute-done | bytes 589856 | tf_op jit(solution)/shard_map/ppermute | solution.py:23
  110.2 6.8 %joined.5 = (bf16[512,4608]{1,0:T(8,128)(2,1)}, bf16[512,4608]{1,0:T(8,128)(2,1)}, f32[8,128]{1,0:T(8,128)S(1)}) custom-call(bf16[128,4608]{1,0:T(8,128)(2,1)} %get-tuple-element.62.refs_0_, bf16[128,4608]{1,0:T(8,128)(2,1)} %collective-permute-done.9.refs_0_.refs_1_, bf16[128,4608]{1,0:T(8,128)(2,1)} %copy-done.2, ...), custom_call_target="tpu_custom_call" | custom-call | tf_op jit(solution)/shard_map/joined/pallas_call | solution.py:65
  118.1 5.6 %all-to-all-start.2 = ((bf16[16,32,1024]{2,1,0:T(8,128)(2,1)}), bf16[16,32,1024]{2,1,0:T(8,128)(2,1)S(1)}, u32[]{:S(2)}, u32[]{:S(2)}) async-start(bf16[16,32,1024]{2,1,0:T(8,128)(2,1)} %bitcast.22), calls=%async_computation.2 | async-start | bytes 2097152 | tf_op jit(solution)/shard_map/all_to_all | solution.py:335
  124.8 1.9 collective-permute-start.22
  129.5 2.6 %collective-permute-done.19.theirs_ref = bf16[512,4608]{1,0:T(8,128)(2,1)} collective-permute-done((bf16[512,4608]{1,0:T(8,128)(2,1)}, bf16[512,4608]{1,0:T(8,128)(2,1)}, u32[]{:S(2)}, u32[]{:S(2)}) %collective-permute-start.19) | collective-permute-done | bytes 4718624 | tf_op jit(solution)/shard_map/ppermute | solution.py:23
  132.1 1.4 collective-permute-start.29
  134.1 2.3 %copy-done.1 = bf16[512,4608]{1,0:T(8,128)(2,1)S(1)} copy-done((bf16[512,4608]{1,0:T(8,128)(2,1)S(1)}, bf16[512,4608]{1,0:T(8,128)(2,1)}, u32[]{:S(2)}) %copy-start.1) | copy-done | bytes 4718616
  136.4 3.6 %project.8 = (f32[640,128]{1,0:T(8,128)S(1)}, f32[8,128]{1,0:T(8,128)S(1)}) custom-call(s32[2]{0:T(128)S(1)} %pad_add_fusion.6.at_ref, s32[10]{0:T(128)S(1)} %get-tuple-element.104.where_ref, bf16[128,28672]{1,0:T(8,128)(2,1)} %bitcast.75, bf16[4,4,32,1024]{3,2,1,0:T(8,128)(2,1)S(1)} %bitcast.63, bf16[512,4608]{1,0:T(8,128)(2,1)S(1)} %copy-done.1, ...), custom_call_target="tpu_custom_call" | custom-call | tf_op jit(solution)/shard_map/project/pallas_call | solution.py:246
  141.8 2.3 %copy-done = bf16[512,4608]{1,0:T(8,128)(2,1)S(1)} copy-done((bf16[512,4608]{1,0:T(8,128)(2,1)S(1)}, bf16[512,4608]{1,0:T(8,128)(2,1)}, u32[]{:S(2)}) %copy-start) | copy-done | bytes 4718616
  144.1 3.6 %project.9 = (f32[640,128]{1,0:T(8,128)S(1)}, f32[8,128]{1,0:T(8,128)S(1)}) custom-call(s32[2]{0:T(128)S(1)} %pad_add_fusion.8.at_ref, s32[10]{0:T(128)S(1)} %get-tuple-element.100.where_ref, bf16[128,28672]{1,0:T(8,128)(2,1)} %bitcast.76, bf16[4,4,32,1024]{3,2,1,0:T(8,128)(2,1)S(1)} %bitcast.67, bf16[512,4608]{1,0:T(8,128)(2,1)S(1)} %copy-done, ...), custom_call_target="tpu_custom_call" | custom-call | tf_op jit(solution)/shard_map/project/pallas_call | solution.py:246
  147.8 3.8 %project.10 = (bf16[640,128]{1,0:T(8,128)(2,1)S(1)}, f32[8,128]{1,0:T(8,128)S(1)}) custom-call(s32[2]{0:T(128)S(1)} %pad_add_fusion.5.at_ref, s32[10]{0:T(128)S(1)} %get-tuple-element.103.where_ref, bf16[128,3584]{1,0:T(8,128)(2,1)} %collective-permute-done.20.up_ref, bf16[4,4,32,1024]{3,2,1,0:T(8,128)(2,1)S(1)} %bitcast.64, ...), custom_call_target="tpu_custom_call" | custom-call | tf_op jit(solution)/shard_map/project/pallas_call | solution.py:246
  151.6 7.6 %collective-permute-done.22.up_ref = bf16[128,3584]{1,0:T(8,128)(2,1)} collective-permute-done((bf16[128,3584]{1,0:T(8,128)(2,1)}, bf16[128,3584]{1,0:T(8,128)(2,1)}, u32[]{:S(2)}, u32[]{:S(2)}) %collective-permute-start.22) | collective-permute-done | bytes 917536 | tf_op jit(solution)/shard_map/ppermute | solution.py:23
  159.1 3.8 %project.11 = (bf16[640,128]{1,0:T(8,128)(2,1)S(1)}, f32[8,128]{1,0:T(8,128)S(1)}) custom-call(s32[2]{0:T(128)S(1)} %pad_add_fusion.4.at_ref, s32[10]{0:T(128)S(1)} %get-tuple-element.99.where_ref, bf16[128,3584]{1,0:T(8,128)(2,1)} %collective-permute-done.22.up_ref, bf16[4,4,32,1024]{3,2,1,0:T(8,128)(2,1)S(1)} %bitcast.68, ...), custom_call_target="tpu_custom_call" | custom-call | tf_op jit(solution)/shard_map/project/pallas_call | solution.py:246
  162.9 4.4 %project.12 = (bf16[640,128]{1,0:T(8,128)(2,1)}, f32[8,128]{1,0:T(8,128)S(1)}) custom-call(s32[2]{0:T(128)S(1)} %pad_add_fusion.3.at_ref, s32[10]{0:T(128)S(1)} %get-tuple-element.102.where_ref, bf16[128,3584]{1,0:T(8,128)(2,1)} %collective-permute-done.24.up_ref, bf16[4,4,32,1024]{3,2,1,0:T(8,128)(2,1)S(1)} %bitcast.65, ...), custom_call_target="tpu_custom_call" | custom-call | tf_op jit(solution)/shard_map/project/pallas_call | solution.py:246
  167.4 4.4 %project.13 = (bf16[640,128]{1,0:T(8,128)(2,1)}, f32[8,128]{1,0:T(8,128)S(1)}) custom-call(s32[2]{0:T(128)S(1)} %pad_add_fusion.2.at_ref, s32[10]{0:T(128)S(1)} %get-tuple-element.98.where_ref, bf16[128,3584]{1,0:T(8,128)(2,1)} %collective-permute-done.26.up_ref, bf16[4,4,32,1024]{3,2,1,0:T(8,128)(2,1)S(1)} %bitcast.69, ...), custom_call_target="tpu_custom_call" | custom-call | tf_op jit(solution)/shard_map/project/pallas_call | solution.py:246
  171.9 3.6 %project.14 = (bf16[640,128]{1,0:T(8,128)(2,1)S(1)}, f32[8,128]{1,0:T(8,128)S(1)}) custom-call(s32[2]{0:T(128)S(1)} %pad_add_fusion.1.at_ref, s32[10]{0:T(128)S(1)} %get-tuple-element.101.where_ref, bf16[128,3584]{1,0:T(8,128)(2,1)S(1)} %copy-done.4, bf16[4,4,32,1024]{3,2,1,0:T(8,128)(2,1)S(1)} %bitcast.66, bf16[512,4608]{1,0:T(8,128)(2,1)} %get-tuple-element.71.mine_ref, ...), custom_call_target="tpu_custom_call" | custom-call | tf_op jit(solution)/shard_map/project/pallas_call | solution.py:246
  175.5 10.3 %collective-permute-start.28 = (bf16[640,128]{1,0:T(8,128)(2,1)S(1)}, bf16[640,128]{1,0:T(8,128)(2,1)S(1)}, u32[]{:S(2)}, u32[]{:S(2)}) collective-permute-start(bf16[640,128]{1,0:T(8,128)(2,1)S(1)} %get-tuple-element.91), channel_id=1, source_target_pairs={{0,4},{2,6},{4,0},{6,2},{1,5},{3,7},{5,1},{7,3},{8,12},{10,14},{12... | collective-permute-start | bytes 491528 | tf_op jit(solution)/shard_map/ppermute | solution.py:23
  186.9 3.6 %project.15 = (bf16[640,128]{1,0:T(8,128)(2,1)S(1)}, f32[8,128]{1,0:T(8,128)}) custom-call(s32[2]{0:T(128)S(1)} %pad_add_fusion.at_ref, s32[10]{0:T(128)S(1)} %get-tuple-element.97.where_ref, bf16[128,3584]{1,0:T(8,128)(2,1)S(1)} %collective-permute-done.29.up_ref, bf16[4,4,32,1024]{3,2,1,0:T(8,128)(2,1)S(1)} %bitcast.70, ...), custom_call_target="tpu_custom_call" | custom-call | tf_op jit(solution)/shard_map/project/pallas_call | solution.py:246
  190.5 9.7 %collective-permute-start.30 = (bf16[640,128]{1,0:T(8,128)(2,1)S(1)}, bf16[640,128]{1,0:T(8,128)(2,1)S(1)}, u32[]{:S(2)}, u32[]{:S(2)}) collective-permute-start(bf16[640,128]{1,0:T(8,128)(2,1)S(1)} %get-tuple-element.94), channel_id=1, source_target_pairs={{0,16},{8,24},{16,0},{24,8},{1,17},{9,25},{17,1},{25,9},{2,18},{10... | collective-permute-start | bytes 491528 | tf_op jit(solution)/shard_map/ppermute | solution.py:23
  200.2 2.9 %collective-permute-start.25 = (bf16[640,128]{1,0:T(8,128)(2,1)}, bf16[640,128]{1,0:T(8,128)(2,1)S(1)}, u32[]{:S(2)}, u32[]{:S(2)}) collective-permute-start(bf16[640,128]{1,0:T(8,128)(2,1)} %get-tuple-element.86), channel_id=1, source_target_pairs={{0,2},{2,4},{4,6},{6,0},{1,3},{3,5},{5,7},{7,1},{8,10},{10,12},{12... | collective-permute-start | bytes 491528 | tf_op jit(solution)/shard_map/ppermute | solution.py:23
  203.1 3.2 %collective-permute-start.23 = (bf16[640,128]{1,0:T(8,128)(2,1)S(1)}, bf16[640,128]{1,0:T(8,128)(2,1)S(1)}, u32[]{:S(2)}, u32[]{:S(2)}) collective-permute-start(bf16[640,128]{1,0:T(8,128)(2,1)S(1)} %get-tuple-element.83), channel_id=1, source_target_pairs={{0,24},{8,0},{16,8},{24,16},{1,25},{9,1},{17,9},{25,17},{2,26},{10... | collective-permute-start | bytes 491528 | tf_op jit(solution)/shard_map/ppermute | solution.py:23
  207.5 1.6 collective-permute-done.23.refs_3_
  209.2 2.5 %collective-permute-done.21.refs_2_ = bf16[640,128]{1,0:T(8,128)(2,1)S(1)} collective-permute-done((bf16[640,128]{1,0:T(8,128)(2,1)S(1)}, bf16[640,128]{1,0:T(8,128)(2,1)S(1)}, u32[]{:S(2)}, u32[]{:S(2)}) %collective-permute-start.21) | collective-permute-done | bytes 163872 | tf_op jit(solution)/shard_map/ppermute | solution.py:23
  212.3 2.2 %scores.1 = f32[32,128]{1,0:T(8,128)} custom-call(f32[32,10]{1,0:T(8,128)} %convert_bitcast_fusion.hits_ref, f32[1,128]{1,0:T(1,128)} %compare_convert_fusion.live_ref, f32[640,128]{1,0:T(8,128)} %copy-done.12, f32[640,128]{1,0:T(8,128)} %copy-done.13, bf16[640,128]{1,0:T(8,128)(2,1)} %copy-done.22, bf16[640,128]{1,0:T(8,128)(2,1)} %copy-done.21, ...), custom_call_target="tpu_custom_call" | custom-call | tf_op jit(solution)/shard_map/scores/pallas_call | solution.py:276
  (106 shorter events, 20.3 us)
Async XLA Ops:
  0.0 4.5 %copy-start.11 = (bf16[1,1,32,8192]{3,2,1,0:T(8,128)(2,1)S(1)}, bf16[1,1,32,8192]{3,2,1,0:T(8,128)(2,1)}, u32[]{:S(2)}) copy-start(bf16[1,1,32,8192]{3,2,1,0:T(8,128)(2,1)} %param.14) | copy-start | bytes 1572868
  0.0 56.9 %all-to-all-start = ((bf16[4,32,8192]{2,1,0:T(8,128)(2,1)}), bf16[4,32,8192]{2,1,0:T(8,128)(2,1)S(1)}, u32[]{:S(2)}, u32[]{:S(2)}) async-start(bf16[4,32,8192]{2,1,0:T(8,128)(2,1)} %bitcast.77), calls=%async_computation | async-start | bytes 4194304 | tf_op jit(solution)/shard_map/all_to_all | solution.py:328
  6.0 33.2 %copy-start.14 = (bf16[1,8192]{1,0:T(2,128)(2,1)S(1)}, bf16[1,8192]{1,0:T(2,128)(2,1)}, u32[]{:S(2)}) copy-start(bf16[1,8192]{1,0:T(2,128)(2,1)} %refs_0_.1) | copy-start | bytes 49156
  8.1 14.3 %collective-permute-start.3 = (bf16[32,4608]{1,0:T(8,128)(2,1)S(1)}, bf16[32,4608]{1,0:T(8,128)(2,1)S(1)}, u32[]{:S(2)}, u32[]{:S(2)}) collective-permute-start(bf16[32,4608]{1,0:T(8,128)(2,1)S(1)} %get-tuple-element.51), channel_id=1, source_target_pairs={{0,2},{2,4},{4,6},{6,0},{1,3},{3,5},{5,7},{7,1},{8,10},{10,12},{12... | collective-permute-start | bytes 884744 | tf_op jit(solution)/shard_map/ppermute | solution.py:23
  10.1 15.5 %collective-permute-start.4 = (bf16[32,4608]{1,0:T(8,128)(2,1)S(1)}, bf16[32,4608]{1,0:T(8,128)(2,1)S(1)}, u32[]{:S(2)}, u32[]{:S(2)}) collective-permute-start(bf16[32,4608]{1,0:T(8,128)(2,1)S(1)} %get-tuple-element.52), channel_id=1, source_target_pairs={{0,6},{2,0},{4,2},{6,4},{1,7},{3,1},{5,3},{7,5},{8,14},{10,8},{12,... | collective-permute-start | bytes 884744 | tf_op jit(solution)/shard_map/ppermute | solution.py:23
  10.2 15.5 %collective-permute-start.5 = (bf16[32,4608]{1,0:T(8,128)(2,1)S(1)}, bf16[32,4608]{1,0:T(8,128)(2,1)S(1)}, u32[]{:S(2)}, u32[]{:S(2)}) collective-permute-start(bf16[32,4608]{1,0:T(8,128)(2,1)S(1)} %get-tuple-element.53), channel_id=1, source_target_pairs={{0,4},{2,6},{4,0},{6,2},{1,5},{3,7},{5,1},{7,3},{8,12},{10,14},{12... | collective-permute-start | bytes 884744 | tf_op jit(solution)/shard_map/ppermute | solution.py:23
  13.2 12.5 %collective-permute-start.6 = (bf16[32,4608]{1,0:T(8,128)(2,1)S(1)}, bf16[32,4608]{1,0:T(8,128)(2,1)S(1)}, u32[]{:S(2)}, u32[]{:S(2)}) collective-permute-start(bf16[32,4608]{1,0:T(8,128)(2,1)S(1)} %get-tuple-element.55), channel_id=1, source_target_pairs={{0,8},{8,16},{16,24},{24,0},{1,9},{9,17},{17,25},{25,1},{2,10},{10... | collective-permute-start | bytes 884744 | tf_op jit(solution)/shard_map/ppermute | solution.py:23
  14.8 10.9 %collective-permute-start.7 = (bf16[32,4608]{1,0:T(8,128)(2,1)S(1)}, bf16[32,4608]{1,0:T(8,128)(2,1)S(1)}, u32[]{:S(2)}, u32[]{:S(2)}) collective-permute-start(bf16[32,4608]{1,0:T(8,128)(2,1)S(1)} %get-tuple-element.56), channel_id=1, source_target_pairs={{0,24},{8,0},{16,8},{24,16},{1,25},{9,1},{17,9},{25,17},{2,26},{10... | collective-permute-start | bytes 884744 | tf_op jit(solution)/shard_map/ppermute | solution.py:23
  22.5 8.2 %collective-permute-start.8 = (bf16[32,4608]{1,0:T(8,128)(2,1)S(1)}, bf16[32,4608]{1,0:T(8,128)(2,1)S(1)}, u32[]{:S(2)}, u32[]{:S(2)}) collective-permute-start(bf16[32,4608]{1,0:T(8,128)(2,1)S(1)} %get-tuple-element.57), channel_id=1, source_target_pairs={{0,16},{8,24},{16,0},{24,8},{1,17},{9,25},{17,1},{25,9},{2,18},{10... | collective-permute-start | bytes 884744 | tf_op jit(solution)/shard_map/ppermute | solution.py:23
  32.7 38.5 %collective-permute-start.10 = (bf16[128,4608]{1,0:T(8,128)(2,1)}, bf16[128,4608]{1,0:T(8,128)(2,1)S(1)}, u32[]{:S(2)}, u32[]{:S(2)}) collective-permute-start(bf16[128,4608]{1,0:T(8,128)(2,1)} %get-tuple-element.62.refs_0_), channel_id=1, source_target_pairs={{0,24},{8,0},{16,8},{24,16},{1,25},{9,1},{17,9},{25,17},{2,26},{10... | collective-permute-start | bytes 3538952 | tf_op jit(solution)/shard_map/ppermute | solution.py:23
  35.8 35.4 %collective-permute-start.9 = (bf16[128,4608]{1,0:T(8,128)(2,1)}, bf16[128,4608]{1,0:T(8,128)(2,1)}, u32[]{:S(2)}, u32[]{:S(2)}) collective-permute-start(bf16[128,4608]{1,0:T(8,128)(2,1)} %get-tuple-element.62.refs_0_), channel_id=1, source_target_pairs={{0,8},{8,16},{16,24},{24,0},{1,9},{9,17},{17,25},{25,1},{2,10},{10... | collective-permute-start | bytes 3538952 | tf_op jit(solution)/shard_map/ppermute | solution.py:23
  35.8 35.4 %collective-permute-start.12 = (bf16[128,4608]{1,0:T(8,128)(2,1)}, bf16[128,4608]{1,0:T(8,128)(2,1)}, u32[]{:S(2)}, u32[]{:S(2)}) collective-permute-start(bf16[128,4608]{1,0:T(8,128)(2,1)} %get-tuple-element.63.refs_5_), channel_id=1, source_target_pairs={{0,6},{2,0},{4,2},{6,4},{1,7},{3,1},{5,3},{7,5},{8,14},{10,8},{12,... | collective-permute-start | bytes 3538952 | tf_op jit(solution)/shard_map/ppermute | solution.py:23
  35.8 35.4 %collective-permute-start.11 = (bf16[128,4608]{1,0:T(8,128)(2,1)}, bf16[128,4608]{1,0:T(8,128)(2,1)}, u32[]{:S(2)}, u32[]{:S(2)}) collective-permute-start(bf16[128,4608]{1,0:T(8,128)(2,1)} %get-tuple-element.63.refs_5_), channel_id=1, source_target_pairs={{0,2},{2,4},{4,6},{6,0},{1,3},{3,5},{5,7},{7,1},{8,10},{10,12},{12... | collective-permute-start | bytes 3538952 | tf_op jit(solution)/shard_map/ppermute | solution.py:23
  39.2 4.6 %collective-permute-start.1 = (bf16[1,8192]{1,0:T(2,128)(2,1)S(1)}, bf16[1,8192]{1,0:T(2,128)(2,1)S(1)}, u32[]{:S(2)}, u32[]{:S(2)}) collective-permute-start(bf16[1,8192]{1,0:T(2,128)(2,1)S(1)} %copy-done.14), channel_id=1, source_target_pairs={{0,96},{32,0},{64,32},{96,64},{1,97},{33,1},{65,33},{97,65},{2,98}... | collective-permute-start | bytes 49160 | tf_op jit(solution)/shard_map/ppermute | solution.py:23
  43.8 5.4 %collective-permute-start = (bf16[1,8192]{1,0:T(2,128)(2,1)S(1)}, bf16[1,8192]{1,0:T(2,128)(2,1)S(1)}, u32[]{:S(2)}, u32[]{:S(2)}) collective-permute-start(bf16[1,8192]{1,0:T(2,128)(2,1)S(1)} %copy-done.14), channel_id=1, source_target_pairs={{0,32},{32,64},{64,96},{96,0},{1,33},{33,65},{65,97},{97,1},{2,34}... | collective-permute-start | bytes 49160 | tf_op jit(solution)/shard_map/ppermute | solution.py:23
  49.2 7.7 %collective-permute-start.2 = (bf16[1,8192]{1,0:T(2,128)(2,1)S(1)}, bf16[1,8192]{1,0:T(2,128)(2,1)S(1)}, u32[]{:S(2)}, u32[]{:S(2)}) collective-permute-start(bf16[1,8192]{1,0:T(2,128)(2,1)S(1)} %copy-done.14), channel_id=1, source_target_pairs={{0,64},{32,96},{64,0},{96,32},{1,65},{33,97},{65,1},{97,33},{2,66}... | collective-permute-start | bytes 49160 | tf_op jit(solution)/shard_map/ppermute | solution.py:23
  62.2 45.9 %all-to-all-start.1 = ((bf16[16,32,1024]{2,1,0:T(8,128)(2,1)}), bf16[16,32,1024]{2,1,0:T(8,128)(2,1)S(1)}, u32[]{:S(2)}, u32[]{:S(2)}) async-start(bf16[16,32,1024]{2,1,0:T(8,128)(2,1)} %bitcast.72), calls=%async_computation.1 | async-start | bytes 2097152 | tf_op jit(solution)/shard_map/all_to_all | solution.py:335
  69.2 30.5 %collective-permute-start.17 = (bf16[128,3584]{1,0:T(8,128)(2,1)}, bf16[128,3584]{1,0:T(8,128)(2,1)S(1)}, u32[]{:S(2)}, u32[]{:S(2)}) collective-permute-start(bf16[128,3584]{1,0:T(8,128)(2,1)} %copy-done.16), channel_id=1, source_target_pairs={{0,4},{2,6},{4,0},{6,2},{1,5},{3,7},{5,1},{7,3},{8,12},{10,14},{12... | collective-permute-start | bytes 2752520 | tf_op jit(solution)/shard_map/ppermute | solution.py:23
  71.2 2.1 copy-start.2
  73.4 26.3 %collective-permute-start.13 = (bf16[64,4608]{1,0:T(8,128)(2,1)S(1)}, bf16[64,4608]{1,0:T(8,128)(2,1)S(1)}, u32[]{:S(2)}, u32[]{:S(2)}) collective-permute-start(bf16[64,4608]{1,0:T(8,128)(2,1)S(1)} %get-tuple-element.65), channel_id=1, source_target_pairs={{0,8},{8,16},{16,24},{24,0},{1,9},{9,17},{17,25},{25,1},{2,10},{10... | collective-permute-start | bytes 1769480 | tf_op jit(solution)/shard_map/ppermute | solution.py:23
  74.6 25.1 %collective-permute-start.14 = (bf16[64,4608]{1,0:T(8,128)(2,1)S(1)}, bf16[64,4608]{1,0:T(8,128)(2,1)S(1)}, u32[]{:S(2)}, u32[]{:S(2)}) collective-permute-start(bf16[64,4608]{1,0:T(8,128)(2,1)S(1)} %get-tuple-element.66), channel_id=1, source_target_pairs={{0,24},{8,0},{16,8},{24,16},{1,25},{9,1},{17,9},{25,17},{2,26},{10... | collective-permute-start | bytes 1769480 | tf_op jit(solution)/shard_map/ppermute | solution.py:23
  76.8 29.7 %collective-permute-start.15 = (bf16[64,4608]{1,0:T(8,128)(2,1)S(1)}, bf16[64,4608]{1,0:T(8,128)(2,1)S(1)}, u32[]{:S(2)}, u32[]{:S(2)}) collective-permute-start(bf16[64,4608]{1,0:T(8,128)(2,1)S(1)} %get-tuple-element.67), channel_id=1, source_target_pairs={{0,2},{2,4},{4,6},{6,0},{1,3},{3,5},{5,7},{7,1},{8,10},{10,12},{12... | collective-permute-start | bytes 1769480 | tf_op jit(solution)/shard_map/ppermute | solution.py:23
  76.8 30.5 %collective-permute-start.16 = (bf16[64,4608]{1,0:T(8,128)(2,1)S(1)}, bf16[64,4608]{1,0:T(8,128)(2,1)S(1)}, u32[]{:S(2)}, u32[]{:S(2)}) collective-permute-start(bf16[64,4608]{1,0:T(8,128)(2,1)S(1)} %get-tuple-element.68), channel_id=1, source_target_pairs={{0,6},{2,0},{4,2},{6,4},{1,7},{3,1},{5,3},{7,5},{8,14},{10,8},{12,... | collective-permute-start | bytes 1769480 | tf_op jit(solution)/shard_map/ppermute | solution.py:23
  99.7 17.3 %copy-start.3 = (bf16[128,3584]{1,0:T(8,128)(2,1)}, bf16[128,3584]{1,0:T(8,128)(2,1)S(1)}, u32[]{:S(2)}) copy-start(bf16[128,3584]{1,0:T(8,128)(2,1)S(1)} %collective-permute-done.17.refs_11_.up_ref) | copy-start | bytes 2752516
  110.2 7.4 %copy-start.23 = (s32[32,8]{0,1:T(8,128)S(1)}, s32[32,8]{0,1:T(8,128)}, u32[]{:S(2)}) copy-start(s32[32,8]{0,1:T(8,128)} %param.15) | copy-start | bytes 3076
  117.0 10.9 %collective-permute-start.18 = (bf16[512,4608]{1,0:T(8,128)(2,1)}, bf16[512,4608]{1,0:T(8,128)(2,1)}, u32[]{:S(2)}, u32[]{:S(2)}) collective-permute-start(bf16[512,4608]{1,0:T(8,128)(2,1)} %get-tuple-element.71.mine_ref), channel_id=1, source_target_pairs={{0,1},{1,0},{2,3},{3,2},{4,5},{5,4},{6,7},{7,6},{8,9},{9,8},{10,11... | collective-permute-start | bytes 14155784 | tf_op jit(solution)/shard_map/ppermute | solution.py:23
  117.1 15.0 %collective-permute-start.19 = (bf16[512,4608]{1,0:T(8,128)(2,1)}, bf16[512,4608]{1,0:T(8,128)(2,1)}, u32[]{:S(2)}, u32[]{:S(2)}) collective-permute-start(bf16[512,4608]{1,0:T(8,128)(2,1)} %get-tuple-element.75.mine_ref), channel_id=1, source_target_pairs={{0,1},{1,0},{2,3},{3,2},{4,5},{5,4},{6,7},{7,6},{8,9},{9,8},{10,11... | collective-permute-start | bytes 14155784 | tf_op jit(solution)/shard_map/ppermute | solution.py:23
  118.1 23.7 %all-to-all-start.2 = ((bf16[16,32,1024]{2,1,0:T(8,128)(2,1)}), bf16[16,32,1024]{2,1,0:T(8,128)(2,1)S(1)}, u32[]{:S(2)}, u32[]{:S(2)}) async-start(bf16[16,32,1024]{2,1,0:T(8,128)(2,1)} %bitcast.22), calls=%async_computation.2 | async-start | bytes 2097152 | tf_op jit(solution)/shard_map/all_to_all | solution.py:335
  123.9 23.8 %collective-permute-start.20 = (bf16[128,3584]{1,0:T(8,128)(2,1)}, bf16[128,3584]{1,0:T(8,128)(2,1)}, u32[]{:S(2)}, u32[]{:S(2)}) collective-permute-start(bf16[128,3584]{1,0:T(8,128)(2,1)} %get-tuple-element.78), channel_id=1, source_target_pairs={{0,2},{2,4},{4,6},{6,0},{1,3},{3,5},{5,7},{7,1},{8,10},{10,12},{12... | collective-permute-start | bytes 2752520 | tf_op jit(solution)/shard_map/ppermute | solution.py:23
  124.8 34.4 %collective-permute-start.22 = (bf16[128,3584]{1,0:T(8,128)(2,1)}, bf16[128,3584]{1,0:T(8,128)(2,1)}, u32[]{:S(2)}, u32[]{:S(2)}) collective-permute-start(bf16[128,3584]{1,0:T(8,128)(2,1)} %get-tuple-element.81), channel_id=1, source_target_pairs={{0,8},{8,16},{16,24},{24,0},{1,9},{9,17},{17,25},{25,1},{2,10},{10... | collective-permute-start | bytes 2752520 | tf_op jit(solution)/shard_map/ppermute | solution.py:23
  126.7 36.2 %collective-permute-start.24 = (bf16[128,3584]{1,0:T(8,128)(2,1)}, bf16[128,3584]{1,0:T(8,128)(2,1)}, u32[]{:S(2)}, u32[]{:S(2)}) collective-permute-start(bf16[128,3584]{1,0:T(8,128)(2,1)} %get-tuple-element.84), channel_id=1, source_target_pairs={{0,6},{2,0},{4,2},{6,4},{1,7},{3,1},{5,3},{7,5},{8,14},{10,8},{12,... | collective-permute-start | bytes 2752520 | tf_op jit(solution)/shard_map/ppermute | solution.py:23
  127.9 39.4 %collective-permute-start.26 = (bf16[128,3584]{1,0:T(8,128)(2,1)}, bf16[128,3584]{1,0:T(8,128)(2,1)}, u32[]{:S(2)}, u32[]{:S(2)}) collective-permute-start(bf16[128,3584]{1,0:T(8,128)(2,1)} %get-tuple-element.87), channel_id=1, source_target_pairs={{0,24},{8,0},{16,8},{24,16},{1,25},{9,1},{17,9},{25,17},{2,26},{10... | collective-permute-start | bytes 2752520 | tf_op jit(solution)/shard_map/ppermute | solution.py:23
  132.1 54.8 %collective-permute-start.29 = (bf16[128,3584]{1,0:T(8,128)(2,1)}, bf16[128,3584]{1,0:T(8,128)(2,1)S(1)}, u32[]{:S(2)}, u32[]{:S(2)}) collective-permute-start(bf16[128,3584]{1,0:T(8,128)(2,1)} %copy-done.15), channel_id=1, source_target_pairs={{0,16},{8,24},{16,0},{24,8},{1,17},{9,25},{17,1},{25,9},{2,18},{10... | collective-permute-start | bytes 2752520 | tf_op jit(solution)/shard_map/ppermute | solution.py:23
  134.1 2.3 %copy-start.1 = (bf16[512,4608]{1,0:T(8,128)(2,1)S(1)}, bf16[512,4608]{1,0:T(8,128)(2,1)}, u32[]{:S(2)}) copy-start(bf16[512,4608]{1,0:T(8,128)(2,1)} %get-tuple-element.71.mine_ref) | copy-start | bytes 14155780
  141.8 2.3 %copy-start = (bf16[512,4608]{1,0:T(8,128)(2,1)S(1)}, bf16[512,4608]{1,0:T(8,128)(2,1)}, u32[]{:S(2)}) copy-start(bf16[512,4608]{1,0:T(8,128)(2,1)} %get-tuple-element.75.mine_ref) | copy-start | bytes 14155780
  147.7 3.8 %copy-start.13 = (f32[640,128]{1,0:T(8,128)}, f32[640,128]{1,0:T(8,128)S(1)}, u32[]{:S(2)}) copy-start(f32[640,128]{1,0:T(8,128)S(1)} %get-tuple-element.77.refs_1_) | copy-start | bytes 983044
  167.4 4.5 %copy-start.4 = (bf16[128,3584]{1,0:T(8,128)(2,1)S(1)}, bf16[128,3584]{1,0:T(8,128)(2,1)}, u32[]{:S(2)}) copy-start(bf16[128,3584]{1,0:T(8,128)(2,1)} %copy-done.3) | copy-start | bytes 2752516
  175.5 30.8 %collective-permute-start.28 = (bf16[640,128]{1,0:T(8,128)(2,1)S(1)}, bf16[640,128]{1,0:T(8,128)(2,1)S(1)}, u32[]{:S(2)}, u32[]{:S(2)}) collective-permute-start(bf16[640,128]{1,0:T(8,128)(2,1)S(1)} %get-tuple-element.91), channel_id=1, source_target_pairs={{0,4},{2,6},{4,0},{6,2},{1,5},{3,7},{5,1},{7,3},{8,12},{10,14},{12... | collective-permute-start | bytes 491528 | tf_op jit(solution)/shard_map/ppermute | solution.py:23
  190.5 16.9 %collective-permute-start.30 = (bf16[640,128]{1,0:T(8,128)(2,1)S(1)}, bf16[640,128]{1,0:T(8,128)(2,1)S(1)}, u32[]{:S(2)}, u32[]{:S(2)}) collective-permute-start(bf16[640,128]{1,0:T(8,128)(2,1)S(1)} %get-tuple-element.94), channel_id=1, source_target_pairs={{0,16},{8,24},{16,0},{24,8},{1,17},{9,25},{17,1},{25,9},{2,18},{10... | collective-permute-start | bytes 491528 | tf_op jit(solution)/shard_map/ppermute | solution.py:23
  200.2 7.3 %collective-permute-start.27 = (bf16[640,128]{1,0:T(8,128)(2,1)}, bf16[640,128]{1,0:T(8,128)(2,1)S(1)}, u32[]{:S(2)}, u32[]{:S(2)}) collective-permute-start(bf16[640,128]{1,0:T(8,128)(2,1)} %get-tuple-element.89), channel_id=1, source_target_pairs={{0,8},{8,16},{16,24},{24,0},{1,9},{9,17},{17,25},{25,1},{2,10},{10... | collective-permute-start | bytes 491528 | tf_op jit(solution)/shard_map/ppermute | solution.py:23
  200.2 7.3 %collective-permute-start.25 = (bf16[640,128]{1,0:T(8,128)(2,1)}, bf16[640,128]{1,0:T(8,128)(2,1)S(1)}, u32[]{:S(2)}, u32[]{:S(2)}) collective-permute-start(bf16[640,128]{1,0:T(8,128)(2,1)} %get-tuple-element.86), channel_id=1, source_target_pairs={{0,2},{2,4},{4,6},{6,0},{1,3},{3,5},{5,7},{7,1},{8,10},{10,12},{12... | collective-permute-start | bytes 491528 | tf_op jit(solution)/shard_map/ppermute | solution.py:23
  203.1 6.1 %collective-permute-start.23 = (bf16[640,128]{1,0:T(8,128)(2,1)S(1)}, bf16[640,128]{1,0:T(8,128)(2,1)S(1)}, u32[]{:S(2)}, u32[]{:S(2)}) collective-permute-start(bf16[640,128]{1,0:T(8,128)(2,1)S(1)} %get-tuple-element.83), channel_id=1, source_target_pairs={{0,24},{8,0},{16,8},{24,16},{1,25},{9,1},{17,9},{25,17},{2,26},{10... | collective-permute-start | bytes 491528 | tf_op jit(solution)/shard_map/ppermute | solution.py:23
  206.3 5.3 %copy-start.17 = (bf16[640,128]{1,0:T(8,128)(2,1)}, bf16[640,128]{1,0:T(8,128)(2,1)S(1)}, u32[]{:S(2)}) copy-start(bf16[640,128]{1,0:T(8,128)(2,1)S(1)} %collective-permute-done.28.refs_6_) | copy-start | bytes 491524
  206.3 5.3 %collective-permute-start.21 = (bf16[640,128]{1,0:T(8,128)(2,1)S(1)}, bf16[640,128]{1,0:T(8,128)(2,1)S(1)}, u32[]{:S(2)}, u32[]{:S(2)}) collective-permute-start(bf16[640,128]{1,0:T(8,128)(2,1)S(1)} %get-tuple-element.80), channel_id=1, source_target_pairs={{0,6},{2,0},{4,2},{6,4},{1,7},{3,1},{5,3},{7,5},{8,14},{10,8},{12,... | collective-permute-start | bytes 491528 | tf_op jit(solution)/shard_map/ppermute | solution.py:23
  207.5 4.2 %copy-start.18 = (bf16[640,128]{1,0:T(8,128)(2,1)}, bf16[640,128]{1,0:T(8,128)(2,1)S(1)}, u32[]{:S(2)}) copy-start(bf16[640,128]{1,0:T(8,128)(2,1)S(1)} %collective-permute-done.30.refs_7_) | copy-start | bytes 491524
  207.5 4.2 %copy-start.19 = (bf16[640,128]{1,0:T(8,128)(2,1)}, bf16[640,128]{1,0:T(8,128)(2,1)S(1)}, u32[]{:S(2)}) copy-start(bf16[640,128]{1,0:T(8,128)(2,1)S(1)} %collective-permute-done.27.refs_5_) | copy-start | bytes 491524
  207.5 4.2 %copy-start.20 = (bf16[640,128]{1,0:T(8,128)(2,1)}, bf16[640,128]{1,0:T(8,128)(2,1)S(1)}, u32[]{:S(2)}) copy-start(bf16[640,128]{1,0:T(8,128)(2,1)S(1)} %collective-permute-done.25.refs_4_) | copy-start | bytes 491524
  209.1 2.5 %copy-start.21 = (bf16[640,128]{1,0:T(8,128)(2,1)}, bf16[640,128]{1,0:T(8,128)(2,1)S(1)}, u32[]{:S(2)}) copy-start(bf16[640,128]{1,0:T(8,128)(2,1)S(1)} %collective-permute-done.23.refs_3_) | copy-start | bytes 491524
  (10 other events, 9.6 us)

commit v3 on v2

v3 whole, which is shorter than its diff:
```python
import functools

import jax
import jax.numpy as jnp
from jax import lax
from jax.experimental import pallas as pl
from jax.experimental.pallas import tpu as pltpu
from jax.sharding import Mesh
from jax.sharding import PartitionSpec as P

EPSILON = 1e-05
SIDE = 4
CORES = 2
RELATIVE = (0, 3, 1, 2)
ANY = pl.BlockSpec(memory_space=pl.ANY)
SMEM = pl.BlockSpec(memory_space=pltpu.SMEM)
TOKEN = jax.ShapeDtypeStruct((8, 128), jnp.float32)
VMEM_BYTES = 60 << 20


def shifted(block, axis, distance):
    size = lax.axis_size(axis)
    return lax.ppermute(block, axis, [(i, (i + distance) % size) for i in range(size)])


def moved(copies):
    for into, _ in copies:
        for copy in into:
            copy.start()
    for into, out in copies:
        for copy in into:
            copy.wait()
        out.start()
    for _, out in copies:
        out.wait()


def joined_kernel(groups, arrays, *refs):
    sources, held, sems = refs[:arrays], refs[-2], refs[-1]
    outs = refs[-3 - len(groups) : -3]
    copies, row = [], 0
    for group, out_ref in zip(groups, outs):
        to = 0
        for source, first, rows in group:
            here, i = held.at[pl.ds(row + to, rows)], len(copies)
            into = pltpu.make_async_copy(sources[source].at[pl.ds(first, rows)], here, sems.at[0, i])
            out = pltpu.make_async_copy(here, out_ref.at[pl.ds(to, rows)], sems.at[1, i])
            copies.append(([into], out))
            to += rows
        row += to
    moved(copies)


def joined(groups, after):
    arrays = []
    listed = []
    for group in groups:
        for array, _, _ in group:
            if not any(array is known for known in arrays):
                arrays.append(array)
        index = lambda array: [array is known for known in arrays].index(True)
        listed.append([(index(array), first, rows) for array, first, rows in group])
    sizes = [sum(rows for _, _, rows in group) for group in listed]
    wide, dtype = arrays[0].shape[1], arrays[0].dtype
    *outs, token = pl.pallas_call(
        functools.partial(joined_kernel, listed, len(arrays)),
        in_specs=[ANY] * (len(arrays) + len(after)),
        out_specs=[ANY] * (len(sizes) + 1),
        out_shape=[jax.ShapeDtypeStruct((size, wide), dtype) for size in sizes] + [TOKEN],
        scratch_shapes=[
            pltpu.VMEM((sum(sizes), wide), dtype),
            pltpu.SemaphoreType.DMA((2, sum(len(group) for group in listed))),
        ],
        compiler_params=pltpu.CompilerParams(vmem_limit_bytes=VMEM_BYTES),
        name="joined",
    )(*arrays, *after)
    return outs, token


def cut_kernel(plan, arrays, *refs):
    sources = refs[:arrays]
    count = len(plan)
    outs, held, sems = refs[-2 - 2 * count : -2 - count], refs[-1 - count : -1], refs[-1]
    copies = []
    for at, (sources_of, out_ref, buffer) in enumerate(zip(plan, outs, held)):
        into = []
        for source, rows, to_row, to, first, wide, by, step in sources_of:
            start = first
            if by is not None:
                start = pl.multiple_of(first + (lax.axis_index(by) + step) % SIDE * wide, 128)
            into.append(
                pltpu.make_async_copy(
                    sources[source].at[pl.ds(*rows), pl.ds(start, wide)],
                    buffer.at[pl.ds(to_row, rows[1]), pl.ds(to, wide)],
                    sems.at[at, len(into)],
                )
            )
        copies.append((into, pltpu.make_async_copy(buffer, out_ref, sems.at[at, len(into)])))
    moved(copies)


def cut(arrays, plan, after):
    shapes = [
        (max(to_row + rows[1] for _, rows, to_row, *_ in item), max(to + wide for _, _, _, to, _, wide, *_ in item))
        for item in plan
    ]
    dtype = arrays[0].dtype
    *outs, token = pl.pallas_call(
        functools.partial(cut_kernel, plan, len(arrays)),
        in_specs=[ANY] * (len(arrays) + len(after)),
        out_specs=[ANY] * (len(plan) + 1),
        out_shape=[jax.ShapeDtypeStruct(shape, dtype) for shape in shapes] + [TOKEN],
        scratch_shapes=[pltpu.VMEM(shape, dtype) for shape in shapes]
        + [pltpu.SemaphoreType.DMA((len(plan), 1 + max(len(item) for item in plan)))],
        compiler_params=pltpu.CompilerParams(vmem_limit_bytes=VMEM_BYTES),
        name="cut",
    )(*arrays, *after)
    return outs, token


def chain_kernel(section_ref, inputs_ref, gains_ref, top_ref, *refs):
    out_ref = refs[-2]
    sections, width = inputs_ref.shape[0], top_ref.shape[1]
    cotangent = top_ref[...].astype(jnp.float32)
    out_ref[sections - 1] = top_ref[...]
    for layer in range(sections - 1, 0, -1):
        gain = gains_ref[layer : layer + 1, :].astype(jnp.float32)
        values = inputs_ref[layer, :, :width].astype(jnp.float32)
        inverse = lax.rsqrt(jnp.mean(values * values, axis=-1, keepdims=True) + EPSILON)
        normed = values * inverse
        scaled = gain * cotangent
        pulled = jnp.mean(normed * scaled, axis=-1, keepdims=True)
        cotangent = cotangent + scaled * inverse - normed * inverse * pulled
        out_ref[layer - 1] = cotangent.astype(out_ref.dtype)


def chain(section, inputs, gains, top, after):
    sections, rows, wide_in = inputs.shape
    width = top.shape[1]
    step = 16
    steps = rows // step
    return pl.pallas_call(
        chain_kernel,
        grid_spec=pltpu.PrefetchScalarGridSpec(
            num_scalar_prefetch=1,
            grid=(steps,),
            in_specs=[
                pl.BlockSpec((sections, step, wide_in), lambda i, section_ref: (0, i, 0)),
                pl.BlockSpec((sections, width), lambda i, section_ref: (0, 0)),
                pl.BlockSpec((step, width), lambda i, section_ref: (section_ref[0] * steps + i, 0)),
            ]
            + [ANY] * len(after),
            out_specs=[
                pl.BlockSpec((sections, step, width), lambda i, section_ref: (0, i, 0)),
                ANY,
            ],
        ),
        out_shape=[jax.ShapeDtypeStruct((sections, rows, width), jnp.bfloat16), TOKEN],
        compiler_params=pltpu.CompilerParams(vmem_limit_bytes=VMEM_BYTES),
        name="cotangent_chain",
    )(section, inputs, gains, top, *after)


def project_kernel(plan, sources, kept, up_wide, down_wide, where_ref, *refs):
    pieces = len(plan)
    factor_refs, token_refs = refs[:kept], refs[kept:]
    outs = refs[-4 - pieces : -4]
    factor_ref, token_ref, sems = refs[-3:]
    capacity = where_ref.shape[1]
    rank = factor_ref.shape[1] // capacity
    held = factor_refs[0].shape[0] // rank
    halves = 2
    y, z, c = (lax.axis_index(axis) for axis in ("y", "z", "c"))
    wides = up_wide, down_wide

    def place_of(piece):
        half, distance = plan[piece]
        return ((y if half else z) + distance) % SIDE

    def row_of(piece):
        half, _ = plan[piece]
        place = place_of(piece)
        shard = (place * SIDE + z) * CORES + c if half else (y * SIDE + place) * CORES + c
        return half * (where_ref.shape[0] // halves) + shard

    def slot_copy(source, row, piece, slot):
        return pltpu.make_async_copy(
            source.at[pl.ds(pl.multiple_of(row * rank, rank), rank)],
            factor_ref.at[piece, pl.ds(slot * rank, rank)],
            sems.at[piece, slot],
        )

    def token_copies(piece):
        to, copies = 0, []
        for part, wide in enumerate(wides):
            source, column = sources[piece][part]
            if column is None:
                column = pl.multiple_of((plan[piece][0] * SIDE + place_of(piece)) * wide, 128)
            copies.append(
                pltpu.make_async_copy(
                    token_refs[source].at[:, pl.ds(column, wide)],
                    token_ref.at[piece, :, pl.ds(to, wide)],
                    sems.at[piece, capacity + part],
                )
            )
            to += wide
        return copies

    def begin(piece):
        half, _ = plan[piece]
        for copy in token_copies(piece):
            copy.start()
        listed = row_of(piece)
        here = factor_refs[half * (kept // halves) : (half + 1) * (kept // halves)]
        for slot in range(capacity):
            row = where_ref[listed, slot]
            for at, source in enumerate(here):

                @pl.when((row >= at * held) & (row < (at + 1) * held))
                def _(source=source, row=row, at=at, slot=slot, piece=piece):
                    slot_copy(source, row - at * held, piece, slot).start()

    size = capacity * rank
    ahead = 2
    for piece in range(min(ahead, pieces)):
        begin(piece)
    for piece, out_ref in enumerate(outs):
        for copy in token_copies(piece):
            copy.wait()
        for slot in range(capacity):
            slot_copy(factor_refs[0], 0, piece, slot).wait()
        if piece + ahead < pieces:
            begin(piece + ahead)
        for side, columns in enumerate((slice(0, up_wide), slice(up_wide, up_wide + down_wide))):
            part = lax.dot_general(
                factor_ref[piece, :, columns],
                token_ref[piece, :, columns],
                (((1,), (1,)), ((), ())),
                preferred_element_type=jnp.float32,
            )
            out_ref[side * size : (side + 1) * size] = part.astype(out_ref.dtype)


def project(plan, where, tokens, factors, rank, up_wide, down_wide, after):
    pieces, capacity = len(plan), where.shape[1]
    rows = tokens[0][0][0].shape[0]
    arrays = []
    sources = []
    for pair in tokens:
        for array, _ in pair:
            if not any(array is known for known in arrays):
                arrays.append(array)
        sources.append(
            [([array is known for known in arrays].index(True), column) for array, column in pair]
        )
    vmem = pl.BlockSpec(memory_space=pltpu.VMEM)
    *outs, token = pl.pallas_call(
        functools.partial(project_kernel, plan, sources, len(factors), up_wide, down_wide),
        in_specs=[SMEM] + [ANY] * (len(factors) + len(arrays) + len(after)),
        out_specs=[vmem] * pieces + [ANY],
        out_shape=[
            jax.ShapeDtypeStruct(
                (2 * capacity * rank, rows), jnp.bfloat16 if distance else jnp.float32
            )
            for _, distance in plan
        ]
        + [TOKEN],
        scratch_shapes=[
            pltpu.VMEM((pieces, capacity * rank, up_wide + down_wide), jnp.bfloat16),
            pltpu.VMEM((pieces, rows, up_wide + down_wide), jnp.bfloat16),
            pltpu.SemaphoreType.DMA((pieces, capacity + 2)),
        ],
        compiler_params=pltpu.CompilerParams(vmem_limit_bytes=VMEM_BYTES),
        name="project",
    )(where, *factors, *arrays, *after)
    return outs, token


def score_kernel(hits_ref, live_ref, *refs):
    part_refs, out_ref = refs[:-1], refs[-1]
    capacity = hits_ref.shape[1]
    size = part_refs[0].shape[0] // 2
    rank = size // capacity
    total = sum(ref[...].astype(jnp.float32) for ref in part_refs)
    products = total[:size] * total[size:]
    dense = jnp.zeros((hits_ref.shape[0], products.shape[1]), jnp.float32)
    for slot in range(capacity):
        row = jnp.sum(products[slot * rank : (slot + 1) * rank], axis=0, keepdims=True)
        dense = dense + hits_ref[:, slot : slot + 1] * row
    out_ref[...] = dense * live_ref[...]


def scores_of(hits, live, parts):
    return pl.pallas_call(
        score_kernel,
        out_shape=jax.ShapeDtypeStruct((hits.shape[0], live.shape[1]), jnp.float32),
        name="scores",
    )(hits, live, *parts).T


def spread(pieces, axis):
    return [shifted(piece, axis, distance) for piece, distance in zip(pieces, (1, -1, 2))]


def body(
    hidden_acts,
    layer_inputs,
    norm_gains,
    top_cotangent,
    up_factors,
    down_factors,
    candidates,
    counts,
):
    sections = lax.axis_size("x")
    section, y, z, c = (lax.axis_index(axis) for axis in ("x", "y", "z", "c"))
    me = (y * SIDE + z) * CORES + c
    shards = SIDE * SIDE * CORES
    rows, width = layer_inputs.shape[1:]
    hidden = hidden_acts[0]
    up, down = up_factors[0, 0], down_factors[0, 0]
    rank, ff = up.shape
    up_wide = ff // (2 * SIDE)
    down_wide = width // (2 * SIDE)
    axes, other_axes = ("z", "y"), ("y", "z")
    halves = range(2)

    def whole(array):
        return (array, 0, array.shape[0])

    def slices(half, sources, wides, rows, steps):
        items = []
        for step in steps:
            to, item = 0, []
            for source, wide in zip(sources, wides):
                item.append((source, (0, rows), 0, to, half * SIDE * wide, wide, axes[half], step))
                to += wide
            items.append(item)
        return items

    queries, listed = candidates.shape
    capacity = listed + listed // 4
    member = jnp.any(
        candidates[:, :, None] == jnp.arange(shards, dtype=jnp.int32)[None, None, :], axis=1
    ).astype(jnp.int32)
    position = jnp.cumsum(member, axis=0) - member
    hits = (
        (member.T[:, None, :] == 1)
        & (position.T[:, None, :] == jnp.arange(capacity, dtype=jnp.int32)[None, :, None])
    )
    query = jnp.arange(queries, dtype=jnp.int32)
    order = jnp.array([0, 2, 3, 1], jnp.int32)
    far_y = order[(query // (CORES * SIDE) - y) % SIDE]
    far_z = order[(query // CORES % SIDE - z) % SIDE]
    other = (query % CORES != c).astype(jnp.int32) * SIDE * SIDE
    kept = (other + far_y * SIDE + far_z, other + far_z * SIDE + far_y)
    where = jnp.concatenate(
        [jnp.sum(jnp.where(hits, place[None, None, :], 0), axis=2) for place in kept]
    )
    own_hits = lax.dynamic_index_in_dim(hits, me, 0, keepdims=False).astype(jnp.float32).T
    live = (jnp.arange(rows, dtype=jnp.int32) < counts[0]).astype(jnp.float32)[None, :]

    outs, token = cut(
        [up, down, hidden],
        [item for half in halves for item in slices(half, (2,), (up_wide,), rows, (2,))]
        + [
            item
            for half in halves
            for item in slices(half, (0, 1), (up_wide, down_wide), rank, (0, 1, -1, 2))
        ],
        [],
    )
    far_up = [shifted(outs[half], axes[half], 2) for half in halves]
    pieces = outs[2 : 2 + SIDE], outs[2 + SIDE :]
    block = rows // sections
    extra = width // block
    (payload,), token = cut(
        [layer_inputs[0], norm_gains.reshape(block, extra)],
        [
            [
                item
                for part in range(sections)
                for item in (
                    (0, (part * block, block), part * block, 0, 0, width, None, 0),
                    (1, (0, block), part * block, width, 0, extra, None, 0),
                )
            ]
        ],
        [token],
    )
    inputs = lax.all_to_all(payload.reshape(sections, block, -1), "x", 0, 0, tiled=True)
    gains = inputs[:, :, width:].reshape(sections, width)

    near, token = joined(
        [
            [whole(pieces[half][0])] + [whole(p) for p in spread(pieces[half][1:], axes[half])]
            for half in halves
        ],
        [token],
    )
    size = near[0].shape[0]
    before = [shifted(near[half], other_axes[half], 1) for half in halves]
    after = [shifted(near[half], other_axes[half], -1) for half in halves]

    cotangents, token = chain(
        section.reshape(1).astype(jnp.int32),
        inputs,
        gains,
        top_cotangent,
        [token, where, own_hits, live],
    )
    cotangent = lax.all_to_all(cotangents, "x", 0, 0, tiled=True).reshape(rows, width)

    forward, token = joined(
        [[(array, half * size // 2, size // 2)] for half in halves for array in (before, after)[half]],
        [token],
    )
    far = [
        (shifted(forward[half], other_axes[half], 1), shifted(forward[2 + half], other_axes[half], -1))
        for half in halves
    ]
    sent, token = cut(
        [hidden, cotangent],
        [item for half in halves for item in slices(half, (1,), (down_wide,), rows, (2,))]
        + [
            item
            for half in halves
            for item in slices(half, (0, 1), (up_wide, down_wide), rows, (1, -1))
        ],
        [token],
    )
    far_down = [shifted(sent[half], axes[half], 2) for half in halves]
    beside = [
        [shifted(sent[2 + 2 * half], axes[half], 1), shifted(sent[3 + 2 * half], axes[half], -1)]
        for half in halves
    ]
    mine, token = joined(
        [
            [whole(part) for part in (near[half], before[half], after[half], *far[half])]
            for half in halves
        ],
        [token],
    )
    factors = [array for half in halves for array in (mine[half], shifted(mine[half], "c", 1))]

    parts = []
    for distances in ((0, 2), (3, 1)):
        plan = [(half, distance) for half in halves for distance in distances]
        tokens = []
        for half, distance in plan:
            if distance == 0:
                tokens.append(((hidden, None), (cotangent, None)))
            elif distance == 2:
                tokens.append(((far_up[half], 0), (far_down[half], 0)))
            else:
                piece = beside[half][RELATIVE.index(distance) - 1]
                tokens.append(((piece, 0), (piece, up_wide)))
        products, token = project(plan, where, tokens, factors, rank, up_wide, down_wide, [token])
        parts += [
            shifted(product, axes[half], distance) if distance else product
            for product, (half, distance) in zip(products, plan)
        ]
    return scores_of(own_hits, live, parts)[None]


def solution(mesh):
    grid = Mesh(mesh.devices.reshape(-1, SIDE, SIDE, CORES), ("x", "y", "z", "c"))
    dp = ("y", "z", "c")
    return jax.shard_map(
        body,
        mesh=grid,
        in_specs=(
            P("x", dp, None),
            P("x", dp, None),
            P("x", None),
            P(dp, None),
            P(dp, "x", None, None),
            P(dp, "x", None, None),
            P(),
            P(dp),
        ),
        out_specs=P("x", dp, None),
        check_vma=False,
    )
```

time: 216 us -> 184 us (0.85)
  starting transfers between devices: 81.6 us -> 53.8 us
  local copies, waits for them, and re-layouts: 14.5 us -> 5.35 us
  waiting for transfers between devices: 59.6 us -> 66.2 us
  Pallas kernels: 54.9 us -> 52.2 us
    ppermute x31 -> x30, starting transfers between devices: 64.6 us -> 44.8 us  [shifted(): lax.ppermute(block, axis, [(i, (i + distance) % size) for i in range(size)])]
    unnamed x49 -> x57, local copies, waits for them, and re-layouts: 14.3 us -> 4.57 us
    all_to_all x3 -> x2, starting transfers between devices: 16.9 us -> 9.01 us  [the longest x1 4.71 us: body(): lax.all_to_all(cotangents, 'x', 0, 0, tiled=True).reshape(rows, width)]
    ppermute x31 -> x30, waiting for transfers between devices: 58.7 us -> 65 us  [shifted(): lax.ppermute(block, axis, [(i, (i + distance) % size) for i in range(size)])]
    pallas_call x10 -> x5, Pallas kernels: 37.5 us -> 32.9 us  [the longest x2 21.6 us: project(): pl.pallas_call(functools.partial(project_kernel, plan, sources, len(facto...]
  transfers between devices with their start and end apart: 34 -> 32, of which waited for: 11 -> 19; matrix products, arithmetic and copies ran while one was open for 1% -> 2% of each run, Pallas kernels for 21% -> 20%
where the time goes in v3:
time: 184 us; the launch traced here: 182 us
  waiting for transfers between devices  66.2 us (36%)
  starting transfers between devices  53.8 us (29%)
  Pallas kernels  52.2 us (28%)
  local copies, waits for them, and re-layouts  5.35 us (3%)
  other arithmetic  3.62 us (2%)
    ppermute x30, waiting for transfers between devices, shifted(): lax.ppermute(block, axis, [(i, (i + distance) % size) for i in range(size)])  65 us
    ppermute x30, starting transfers between devices, shifted(): lax.ppermute(block, axis, [(i, (i + distance) % size) for i in range(size)])  44.8 us
    pallas_call x2, Pallas kernels, project(): pl.pallas_call(functools.partial(project_kernel, plan, sources, len(facto...  21.6 us
    pallas_call x3, Pallas kernels, joined(): pl.pallas_call(functools.partial(joined_kernel, listed, len(arrays)), in_...  12.4 us
    pallas_call x3, Pallas kernels, cut(): pl.pallas_call(functools.partial(cut_kernel, plan, len(arrays)), in_specs...  11.3 us
    all_to_all x1, starting transfers between devices, body(): lax.all_to_all(cotangents, 'x', 0, 0, tiled=True).reshape(rows, width)  4.71 us
    pallas_call x1, Pallas kernels, chain(): pl.pallas_call(chain_kernel, grid_spec=pltpu.PrefetchScalarGridSpec(num_s...  4.64 us
    unnamed x57, local copies, waits for them, and re-layouts  4.57 us
  transfers between devices with their start and end apart: 32, of which 19 were waited for; matrix products, arithmetic and copies ran while one was open for 2% of the time, Pallas kernels for 20%

profile of v3, /device:TPU:32, one launch (start us, length us, event | category | flops | bytes accessed | tf_op | source)
XLA Modules:
  0.0 182.1 jit_solution(5271416907156476925)
XLA Ops:
  1.5 3.5 %cut.3 = (bf16[128,3584]{1,0:T(8,128)(2,1)}, bf16[128,3584]{1,0:T(8,128)(2,1)}, bf16[32,4608]{1,0:T(8,128)(2,1)}, bf16[32,4608]{1,0:T(8,128)(2,1)}, bf16[32,4608...) custom-call(bf16[32,28672]{1,0:T(8,128)(2,1)} %bitcast.42, ...), custom_call_target="tpu_custom_call" | custom-call | tf_op jit(solution)/shard_map/cut/pallas_call | solution.py:108
  4.9 3.0 %cut.4 = (bf16[128,8448]{1,0:T(8,128)(2,1)}, f32[8,128]{1,0:T(8,128)}) custom-call(bf16[128,8192]{1,0:T(8,128)(2,1)} %bitcast.41, bf16[32,256]{1,0:T(8,128)(2,1)} %reshape.241.refs_1_, f32[8,128]{1,0:T(8,128)} %get-tuple-element.55.refs_2_), custom_call_target="tpu_custom_call" | custom-call | tf_op jit(solution)/shard_map/cut/pallas_call | solution.py:108
  8.0 4.3 %all-to-all-start = ((bf16[4,32,8448]{2,1,0:T(8,128)(2,1)}), bf16[4,32,8448]{2,1,0:T(8,128)(2,1)S(1)}, u32[]{:S(2)}, u32[]{:S(2)}) async-start(bf16[4,32,8448]{2,1,0:T(8,128)(2,1)} %bitcast.40), calls=%async_computation | async-start | bytes 4325376 | tf_op jit(solution)/shard_map/all_to_all | solution.py:391
  12.3 1.9 %collective-permute-start = (bf16[32,4608]{1,0:T(8,128)(2,1)}, bf16[32,4608]{1,0:T(8,128)(2,1)S(1)}, u32[]{:S(2)}, u32[]{:S(2)}) collective-permute-start(bf16[32,4608]{1,0:T(8,128)(2,1)} %get-tuple-element.48), channel_id=1, source_target_pairs={{0,2},{2,4},{4,6},{6,0},{1,3},{3,5},{5,7},{7,1},{8,10},{10,12},{12... | collective-permute-start | bytes 884744 | tf_op jit(solution)/shard_map/ppermute | solution.py:23
  14.3 3.0 %collective-permute-start.2 = (bf16[32,4608]{1,0:T(8,128)(2,1)}, bf16[32,4608]{1,0:T(8,128)(2,1)S(1)}, u32[]{:S(2)}, u32[]{:S(2)}) collective-permute-start(bf16[32,4608]{1,0:T(8,128)(2,1)} %get-tuple-element.50), channel_id=1, source_target_pairs={{0,4},{2,6},{4,0},{6,2},{1,5},{3,7},{5,1},{7,3},{8,12},{10,14},{12... | collective-permute-start | bytes 884744 | tf_op jit(solution)/shard_map/ppermute | solution.py:23
  17.3 1.6 collective-permute-start.3
  18.9 1.7 collective-permute-start.4
  22.6 4.2 %collective-permute-done.refs_1_ = bf16[32,4608]{1,0:T(8,128)(2,1)S(1)} collective-permute-done((bf16[32,4608]{1,0:T(8,128)(2,1)}, bf16[32,4608]{1,0:T(8,128)(2,1)S(1)}, u32[]{:S(2)}, u32[]{:S(2)}) %collective-permute-start) | collective-permute-done | bytes 294944 | tf_op jit(solution)/shard_map/ppermute | solution.py:23
  26.9 3.2 %collective-permute-start.5 = (bf16[32,4608]{1,0:T(8,128)(2,1)}, bf16[32,4608]{1,0:T(8,128)(2,1)}, u32[]{:S(2)}, u32[]{:S(2)}) collective-permute-start(bf16[32,4608]{1,0:T(8,128)(2,1)} %get-tuple-element.54), channel_id=1, source_target_pairs={{0,16},{8,24},{16,0},{24,8},{1,17},{9,25},{17,1},{25,9},{2,18},{10... | collective-permute-start | bytes 884744 | tf_op jit(solution)/shard_map/ppermute | solution.py:23
  31.7 3.7 %collective-permute-done.5.refs_7_ = bf16[32,4608]{1,0:T(8,128)(2,1)} collective-permute-done((bf16[32,4608]{1,0:T(8,128)(2,1)}, bf16[32,4608]{1,0:T(8,128)(2,1)}, u32[]{:S(2)}, u32[]{:S(2)}) %collective-permute-start.5) | collective-permute-done | bytes 294944 | tf_op jit(solution)/shard_map/ppermute | solution.py:23
  35.4 2.5 %joined.3 = (bf16[128,4608]{1,0:T(8,128)(2,1)}, bf16[128,4608]{1,0:T(8,128)(2,1)}, f32[8,128]{1,0:T(8,128)}) custom-call(bf16[32,4608]{1,0:T(8,128)(2,1)} %get-tuple-element.47.refs_0_, bf16[32,4608]{1,0:T(8,128)(2,1)} %copy-done.10, bf16[32,4608]{1,0:T(8,128)(2,1)} %copy-done.11, bf16[32,4608]{1,0:T(8,128)(2,1)} %copy-done.12, ...), custom_call_target="tpu_custom_call" | custom-call | tf_op jit(solution)/shard_map/joined/pallas_call | solution.py:65
  38.0 3.1 %collective-permute-start.7 = (bf16[128,4608]{1,0:T(8,128)(2,1)}, bf16[128,4608]{1,0:T(8,128)(2,1)S(1)}, u32[]{:S(2)}, u32[]{:S(2)}) collective-permute-start(bf16[128,4608]{1,0:T(8,128)(2,1)} %get-tuple-element.57.refs_0_), channel_id=1, source_target_pairs={{0,24},{8,0},{16,8},{24,16},{1,25},{9,1},{17,9},{25,17},{2,26},{10... | collective-permute-start | bytes 3538952 | tf_op jit(solution)/shard_map/ppermute | solution.py:23
  41.0 3.1 %collective-permute-start.8 = (bf16[128,4608]{1,0:T(8,128)(2,1)}, bf16[128,4608]{1,0:T(8,128)(2,1)}, u32[]{:S(2)}, u32[]{:S(2)}) collective-permute-start(bf16[128,4608]{1,0:T(8,128)(2,1)} %get-tuple-element.58.refs_5_), channel_id=1, source_target_pairs={{0,2},{2,4},{4,6},{6,0},{1,3},{3,5},{5,7},{7,1},{8,10},{10,12},{12... | collective-permute-start | bytes 3538952 | tf_op jit(solution)/shard_map/ppermute | solution.py:23
  45.5 4.6 %cotangent_chain.1 = (bf16[4,32,8192]{2,1,0:T(8,128)(2,1)}, f32[8,128]{1,0:T(8,128)}) custom-call(s32[1]{0:T(128)} %bitcast.11.section_ref, bf16[4,32,8448]{2,1,0:T(8,128)(2,1)} %copy-done.1, bf16[4,8192]{1,0:T(4,128)(2,1)} %bitcast.44, bf16[128,8192]{1,0:T(8,128)(2,1)} %top_ref.1, f32[8,128]{1,0:T(8,128)} %get-tuple-element.60.refs_0_, ...), custom_call_target="tpu_custom_call" | custom-call | tf_op jit(solution)/shard_map/cotangent_chain/pallas_call | solution.py:142
  50.2 4.7 %all-to-all-start.1 = ((bf16[4,32,8192]{2,1,0:T(8,128)(2,1)}), bf16[4,32,8192]{2,1,0:T(8,128)(2,1)S(1)}, u32[]{:S(2)}, u32[]{:S(2)}) async-start(bf16[4,32,8192]{2,1,0:T(8,128)(2,1)} %get-tuple-element.66), calls=%async_computation.1 | async-start | bytes 4194304 | tf_op jit(solution)/shard_map/all_to_all | solution.py:412
  54.9 6.7 %collective-permute-done.7.refs_2_ = bf16[128,4608]{1,0:T(8,128)(2,1)S(1)} collective-permute-done((bf16[128,4608]{1,0:T(8,128)(2,1)}, bf16[128,4608]{1,0:T(8,128)(2,1)S(1)}, u32[]{:S(2)}, u32[]{:S(2)}) %collective-permute-start.7) | collective-permute-done | bytes 1179680 | tf_op jit(solution)/shard_map/ppermute | solution.py:23
  61.6 2.6 %collective-permute-done.6.refs_0_.refs_1_ = bf16[128,4608]{1,0:T(8,128)(2,1)} collective-permute-done((bf16[128,4608]{1,0:T(8,128)(2,1)}, bf16[128,4608]{1,0:T(8,128)(2,1)}, u32[]{:S(2)}, u32[]{:S(2)}) %collective-permute-start.6) | collective-permute-done | bytes 1179680 | tf_op jit(solution)/shard_map/ppermute | solution.py:23
  64.2 1.1 collective-permute-done.8.refs_1_.refs_6_
  65.2 2.6 %joined.4 = (bf16[64,4608]{1,0:T(8,128)(2,1)}, bf16[64,4608]{1,0:T(8,128)(2,1)}, bf16[64,4608]{1,0:T(8,128)(2,1)}, bf16[64,4608]{1,0:T(8,128)(2,1)}, f32[8,128]{1,0:T(8,128)}) custom-call(bf16[128,4608]{1,0:T(8,128)(2,1)} %collective-permute-done.6.refs_0_.refs_1_, bf16[128,4608]{1,0:T(8,128)(2,1)} %collective-permute-done.8.refs_1_.refs_6_, ...), custom_call_target="tpu_custom_call" | custom-call | tf_op jit(solution)/shard_map/joined/pallas_call | solution.py:65
  67.8 1.6 collective-permute-start.10
  69.5 1.7 collective-permute-start.11
  71.4 1.7 collective-permute-start.13
  73.1 1.2 all-to-all-done.1
  74.4 1.4 copy-done
  75.7 4.8 %cut.5 = (bf16[128,1024]{1,0:T(8,128)(2,1)}, bf16[128,1024]{1,0:T(8,128)(2,1)}, bf16[128,4608]{1,0:T(8,128)(2,1)}, bf16[128,4608]{1,0:T(8,128)(2,1)}, bf16[128,4...) custom-call(bf16[128,28672]{1,0:T(8,128)(2,1)} %bitcast.36, bf16[128,8192]{1,0:T(8,128)(2,1)} %bitcast.38, ...), custom_call_target="tpu_custom_call" | custom-call | tf_op jit(solution)/shard_map/cut/pallas_call | solution.py:108
  80.7 1.8 %collective-permute-done.12.refs_8_ = bf16[64,4608]{1,0:T(8,128)(2,1)} collective-permute-done((bf16[64,4608]{1,0:T(8,128)(2,1)}, bf16[64,4608]{1,0:T(8,128)(2,1)}, u32[]{:S(2)}, u32[]{:S(2)}) %collective-permute-start.12) | collective-permute-done | bytes 589856 | tf_op jit(solution)/shard_map/ppermute | solution.py:23
  82.6 7.3 %joined.5 = (bf16[512,4608]{1,0:T(8,128)(2,1)}, bf16[512,4608]{1,0:T(8,128)(2,1)}, f32[8,128]{1,0:T(8,128)}) custom-call(bf16[128,4608]{1,0:T(8,128)(2,1)} %get-tuple-element.57.refs_0_, bf16[128,4608]{1,0:T(8,128)(2,1)} %collective-permute-done.6.refs_0_.refs_1_, bf16[128,4608]{1,0:T(8,128)(2,1)} %copy-done.2, bf16[64,4608]{1,0:T(8,128)(2,1)} %copy-done.8, ...), custom_call_target="tpu_custom_call" | custom-call | tf_op jit(solution)/shard_map/joined/pallas_call | solution.py:65
  90.5 4.7 %collective-permute-start.16 = (bf16[128,3584]{1,0:T(8,128)(2,1)S(1)}, bf16[128,3584]{1,0:T(8,128)(2,1)S(1)}, u32[]{:S(2)}, u32[]{:S(2)}) collective-permute-start(bf16[128,3584]{1,0:T(8,128)(2,1)S(1)} %copy-done.24), channel_id=1, source_target_pairs={{0,4},{2,6},{4,0},{6,2},{1,5},{3,7},{5,1},{7,3},{8,12},{10,14},{12... | collective-permute-start | bytes 2752520 | tf_op jit(solution)/shard_map/ppermute | solution.py:23
  96.2 20.2 %collective-permute-done.16.refs_6_ = bf16[128,3584]{1,0:T(8,128)(2,1)S(1)} collective-permute-done((bf16[128,3584]{1,0:T(8,128)(2,1)S(1)}, bf16[128,3584]{1,0:T(8,128)(2,1)S(1)}, u32[]{:S(2)}, u32[]{:S(2)}) %collective-permute-start.16) | collective-permute-done | bytes 917536 | tf_op jit(solution)/shard_map/ppermute | solution.py:23
  116.4 1.0 collective-permute-start.19
  117.4 1.4 collective-permute-done.18.refs_8_
  119.3 2.1 %collective-permute-done.17.refs_7_ = bf16[128,1024]{1,0:T(8,128)(2,1)S(1)} collective-permute-done((bf16[128,1024]{1,0:T(8,128)(2,1)S(1)}, bf16[128,1024]{1,0:T(8,128)(2,1)S(1)}, u32[]{:S(2)}, u32[]{:S(2)}) %collective-permute-start.17) | collective-permute-done | bytes 262176 | tf_op jit(solution)/shard_map/ppermute | solution.py:23
  121.4 2.3 %collective-permute-start.23 = (bf16[128,4608]{1,0:T(8,128)(2,1)}, bf16[128,4608]{1,0:T(8,128)(2,1)S(1)}, u32[]{:S(2)}, u32[]{:S(2)}) collective-permute-start(bf16[128,4608]{1,0:T(8,128)(2,1)} %get-tuple-element.81), channel_id=1, source_target_pairs={{0,6},{2,0},{4,2},{6,4},{1,7},{3,1},{5,3},{7,5},{8,14},{10,8},{12,... | collective-permute-start | bytes 3538952 | tf_op jit(solution)/shard_map/ppermute | solution.py:23
  123.8 1.4 collective-permute-done.19.refs_9_
  125.2 3.2 %collective-permute-start.25 = (bf16[128,4608]{1,0:T(8,128)(2,1)}, bf16[128,4608]{1,0:T(8,128)(2,1)}, u32[]{:S(2)}, u32[]{:S(2)}) collective-permute-start(bf16[128,4608]{1,0:T(8,128)(2,1)} %get-tuple-element.83), channel_id=1, source_target_pairs={{0,24},{8,0},{16,8},{24,16},{1,25},{9,1},{17,9},{25,17},{2,26},{10... | collective-permute-start | bytes 3538952 | tf_op jit(solution)/shard_map/ppermute | solution.py:23
  128.4 10.9 %project.2 = (f32[640,128]{1,0:T(8,128)}, bf16[640,128]{1,0:T(8,128)(2,1)}, f32[640,128]{1,0:T(8,128)}, bf16[640,128]{1,0:T(8,128)(2,1)}, f32[8,128]{1,0:T(8,128)}) custom-call(s32[64,10]{1,0:T(8,128)} %pad_add_fusion.refs_1_.where_ref, bf16[512,4608]{1,0:T(8,128)(2,1)} %get-tuple-element.69.refs_0_, bf16[512,4608]{1,0:T(8,128)(2,1)} %collective-permute-done.14.refs_1_, ...), custom_call_target="tpu_custom_call" | custom-call | tf_op jit(solution)/shard_map/project/pallas_call | solution.py:257
  139.4 2.8 %collective-permute-start.20 = (bf16[640,128]{1,0:T(8,128)(2,1)}, bf16[640,128]{1,0:T(8,128)(2,1)S(1)}, u32[]{:S(2)}, u32[]{:S(2)}) collective-permute-start(bf16[640,128]{1,0:T(8,128)(2,1)} %get-tuple-element.77), channel_id=1, source_target_pairs={{0,4},{2,6},{4,0},{6,2},{1,5},{3,7},{5,1},{7,3},{8,12},{10,14},{12... | collective-permute-start | bytes 491528 | tf_op jit(solution)/shard_map/ppermute | solution.py:23
  142.1 5.8 %collective-permute-done.22.refs_4_ = bf16[128,4608]{1,0:T(8,128)(2,1)S(1)} collective-permute-done((bf16[128,4608]{1,0:T(8,128)(2,1)}, bf16[128,4608]{1,0:T(8,128)(2,1)S(1)}, u32[]{:S(2)}, u32[]{:S(2)}) %collective-permute-start.22) | collective-permute-done | bytes 1179680 | tf_op jit(solution)/shard_map/ppermute | solution.py:23
  147.9 1.1 collective-permute-start.21
  149.6 6.5 %collective-permute-done.24.refs_6_ = bf16[128,4608]{1,0:T(8,128)(2,1)S(1)} collective-permute-done((bf16[128,4608]{1,0:T(8,128)(2,1)}, bf16[128,4608]{1,0:T(8,128)(2,1)S(1)}, u32[]{:S(2)}, u32[]{:S(2)}) %collective-permute-start.24) | collective-permute-done | bytes 1179680 | tf_op jit(solution)/shard_map/ppermute | solution.py:23
  156.1 1.0 copy-done.5
  157.2 10.7 %project.3 = (bf16[640,128]{1,0:T(8,128)(2,1)}, bf16[640,128]{1,0:T(8,128)(2,1)}, bf16[640,128]{1,0:T(8,128)(2,1)}, bf16[640,128]{1,0:T(8,128)(2,1)}, f32[8,128]{1,0:T(8,128)}) custom-call(s32[64,10]{1,0:T(8,128)} %pad_add_fusion.refs_1_.where_ref, bf16[512,4608]{1,0:T(8,128)(2,1)} %get-tuple-element.69.refs_0_, ...), custom_call_target="tpu_custom_call" | custom-call | tf_op jit(solution)/shard_map/project/pallas_call | solution.py:257
  167.9 1.7 collective-permute-start.26
  170.0 2.4 %collective-permute-start.28 = (bf16[640,128]{1,0:T(8,128)(2,1)}, bf16[640,128]{1,0:T(8,128)(2,1)S(1)}, u32[]{:S(2)}, u32[]{:S(2)}) collective-permute-start(bf16[640,128]{1,0:T(8,128)(2,1)} %get-tuple-element.87), channel_id=1, source_target_pairs={{0,24},{8,0},{16,8},{24,16},{1,25},{9,1},{17,9},{25,17},{2,26},{10... | collective-permute-start | bytes 491528 | tf_op jit(solution)/shard_map/ppermute | solution.py:23
  172.5 1.0 collective-permute-done.26.refs_4_
  173.5 1.6 collective-permute-done.27.refs_5_
  175.6 3.6 %collective-permute-done.29.refs_7_ = bf16[640,128]{1,0:T(8,128)(2,1)S(1)} collective-permute-done((bf16[640,128]{1,0:T(8,128)(2,1)}, bf16[640,128]{1,0:T(8,128)(2,1)S(1)}, u32[]{:S(2)}, u32[]{:S(2)}) %collective-permute-start.29) | collective-permute-done | bytes 163872 | tf_op jit(solution)/shard_map/ppermute | solution.py:23
  179.9 2.3 %scores.1 = f32[32,128]{1,0:T(8,128)} custom-call(f32[32,10]{1,0:T(8,128)} %convert_bitcast_fusion.refs_2_.hits_ref, f32[1,128]{1,0:T(1,128)} %compare_convert_fusion.refs_3_.live_ref, f32[640,128]{1,0:T(8,128)} %get-tuple-element.76.refs_0_, bf16[640,128]{1,0:T(8,128)(2,1)} %copy-done.16, f32[640,128]{1,0:T(8,128)} %get-tuple-element.78.refs_2_, ...), custom_call_target="tpu_custom_call" | custom-call | tf_op jit(solution)/shard_map/scores/pallas_call | solution.py:294
  (97 shorter events, 10.9 us)
Async XLA Ops:
  8.0 13.2 %copy-start.22 = (s32[32,8]{0,1:T(8,128)S(1)}, s32[32,8]{0,1:T(8,128)}, u32[]{:S(2)}) copy-start(s32[32,8]{0,1:T(8,128)} %param.15) | copy-start | bytes 3076
  8.0 36.2 %all-to-all-start = ((bf16[4,32,8448]{2,1,0:T(8,128)(2,1)}), bf16[4,32,8448]{2,1,0:T(8,128)(2,1)S(1)}, u32[]{:S(2)}, u32[]{:S(2)}) async-start(bf16[4,32,8448]{2,1,0:T(8,128)(2,1)} %bitcast.40), calls=%async_computation | async-start | bytes 4325376 | tf_op jit(solution)/shard_map/all_to_all | solution.py:391
  12.3 14.6 %collective-permute-start = (bf16[32,4608]{1,0:T(8,128)(2,1)}, bf16[32,4608]{1,0:T(8,128)(2,1)S(1)}, u32[]{:S(2)}, u32[]{:S(2)}) collective-permute-start(bf16[32,4608]{1,0:T(8,128)(2,1)} %get-tuple-element.48), channel_id=1, source_target_pairs={{0,2},{2,4},{4,6},{6,0},{1,3},{3,5},{5,7},{7,1},{8,10},{10,12},{12... | collective-permute-start | bytes 884744 | tf_op jit(solution)/shard_map/ppermute | solution.py:23
  14.2 17.5 %collective-permute-start.1 = (bf16[32,4608]{1,0:T(8,128)(2,1)}, bf16[32,4608]{1,0:T(8,128)(2,1)S(1)}, u32[]{:S(2)}, u32[]{:S(2)}) collective-permute-start(bf16[32,4608]{1,0:T(8,128)(2,1)} %get-tuple-element.49), channel_id=1, source_target_pairs={{0,6},{2,0},{4,2},{6,4},{1,7},{3,1},{5,3},{7,5},{8,14},{10,8},{12,... | collective-permute-start | bytes 884744 | tf_op jit(solution)/shard_map/ppermute | solution.py:23
  14.3 17.4 %collective-permute-start.2 = (bf16[32,4608]{1,0:T(8,128)(2,1)}, bf16[32,4608]{1,0:T(8,128)(2,1)S(1)}, u32[]{:S(2)}, u32[]{:S(2)}) collective-permute-start(bf16[32,4608]{1,0:T(8,128)(2,1)} %get-tuple-element.50), channel_id=1, source_target_pairs={{0,4},{2,6},{4,0},{6,2},{1,5},{3,7},{5,1},{7,3},{8,12},{10,14},{12... | collective-permute-start | bytes 884744 | tf_op jit(solution)/shard_map/ppermute | solution.py:23
  17.3 14.4 %collective-permute-start.3 = (bf16[32,4608]{1,0:T(8,128)(2,1)}, bf16[32,4608]{1,0:T(8,128)(2,1)S(1)}, u32[]{:S(2)}, u32[]{:S(2)}) collective-permute-start(bf16[32,4608]{1,0:T(8,128)(2,1)} %get-tuple-element.52), channel_id=1, source_target_pairs={{0,8},{8,16},{16,24},{24,0},{1,9},{9,17},{17,25},{25,1},{2,10},{10... | collective-permute-start | bytes 884744 | tf_op jit(solution)/shard_map/ppermute | solution.py:23
  18.9 12.8 %collective-permute-start.4 = (bf16[32,4608]{1,0:T(8,128)(2,1)}, bf16[32,4608]{1,0:T(8,128)(2,1)}, u32[]{:S(2)}, u32[]{:S(2)}) collective-permute-start(bf16[32,4608]{1,0:T(8,128)(2,1)} %get-tuple-element.53), channel_id=1, source_target_pairs={{0,24},{8,0},{16,8},{24,16},{1,25},{9,1},{17,9},{25,17},{2,26},{10... | collective-permute-start | bytes 884744 | tf_op jit(solution)/shard_map/ppermute | solution.py:23
  26.9 8.5 %copy-start.10 = (bf16[32,4608]{1,0:T(8,128)(2,1)}, bf16[32,4608]{1,0:T(8,128)(2,1)S(1)}, u32[]{:S(2)}) copy-start(bf16[32,4608]{1,0:T(8,128)(2,1)S(1)} %collective-permute-done.refs_1_) | copy-start | bytes 884740
  26.9 8.5 %collective-permute-start.5 = (bf16[32,4608]{1,0:T(8,128)(2,1)}, bf16[32,4608]{1,0:T(8,128)(2,1)}, u32[]{:S(2)}, u32[]{:S(2)}) collective-permute-start(bf16[32,4608]{1,0:T(8,128)(2,1)} %get-tuple-element.54), channel_id=1, source_target_pairs={{0,16},{8,24},{16,0},{24,8},{1,17},{9,25},{17,1},{25,9},{2,18},{10... | collective-permute-start | bytes 884744 | tf_op jit(solution)/shard_map/ppermute | solution.py:23
  31.7 3.8 %copy-start.11 = (bf16[32,4608]{1,0:T(8,128)(2,1)}, bf16[32,4608]{1,0:T(8,128)(2,1)S(1)}, u32[]{:S(2)}) copy-start(bf16[32,4608]{1,0:T(8,128)(2,1)S(1)} %collective-permute-done.1.refs_2_) | copy-start | bytes 884740
  38.0 23.6 %collective-permute-start.7 = (bf16[128,4608]{1,0:T(8,128)(2,1)}, bf16[128,4608]{1,0:T(8,128)(2,1)S(1)}, u32[]{:S(2)}, u32[]{:S(2)}) collective-permute-start(bf16[128,4608]{1,0:T(8,128)(2,1)} %get-tuple-element.57.refs_0_), channel_id=1, source_target_pairs={{0,24},{8,0},{16,8},{24,16},{1,25},{9,1},{17,9},{25,17},{2,26},{10... | collective-permute-start | bytes 3538952 | tf_op jit(solution)/shard_map/ppermute | solution.py:23
  41.0 23.1 %collective-permute-start.6 = (bf16[128,4608]{1,0:T(8,128)(2,1)}, bf16[128,4608]{1,0:T(8,128)(2,1)}, u32[]{:S(2)}, u32[]{:S(2)}) collective-permute-start(bf16[128,4608]{1,0:T(8,128)(2,1)} %get-tuple-element.57.refs_0_), channel_id=1, source_target_pairs={{0,8},{8,16},{16,24},{24,0},{1,9},{9,17},{17,25},{25,1},{2,10},{10... | collective-permute-start | bytes 3538952 | tf_op jit(solution)/shard_map/ppermute | solution.py:23
  41.0 23.1 %collective-permute-start.9 = (bf16[128,4608]{1,0:T(8,128)(2,1)}, bf16[128,4608]{1,0:T(8,128)(2,1)}, u32[]{:S(2)}, u32[]{:S(2)}) collective-permute-start(bf16[128,4608]{1,0:T(8,128)(2,1)} %get-tuple-element.58.refs_5_), channel_id=1, source_target_pairs={{0,6},{2,0},{4,2},{6,4},{1,7},{3,1},{5,3},{7,5},{8,14},{10,8},{12,... | collective-permute-start | bytes 3538952 | tf_op jit(solution)/shard_map/ppermute | solution.py:23
  41.0 24.2 %collective-permute-start.8 = (bf16[128,4608]{1,0:T(8,128)(2,1)}, bf16[128,4608]{1,0:T(8,128)(2,1)}, u32[]{:S(2)}, u32[]{:S(2)}) collective-permute-start(bf16[128,4608]{1,0:T(8,128)(2,1)} %get-tuple-element.58.refs_5_), channel_id=1, source_target_pairs={{0,2},{2,4},{4,6},{6,0},{1,3},{3,5},{5,7},{7,1},{8,10},{10,12},{12... | collective-permute-start | bytes 3538952 | tf_op jit(solution)/shard_map/ppermute | solution.py:23
  50.2 24.2 %all-to-all-start.1 = ((bf16[4,32,8192]{2,1,0:T(8,128)(2,1)}), bf16[4,32,8192]{2,1,0:T(8,128)(2,1)S(1)}, u32[]{:S(2)}, u32[]{:S(2)}) async-start(bf16[4,32,8192]{2,1,0:T(8,128)(2,1)} %get-tuple-element.66), calls=%async_computation.1 | async-start | bytes 4194304 | tf_op jit(solution)/shard_map/all_to_all | solution.py:412
  67.8 12.7 %collective-permute-start.10 = (bf16[64,4608]{1,0:T(8,128)(2,1)}, bf16[64,4608]{1,0:T(8,128)(2,1)S(1)}, u32[]{:S(2)}, u32[]{:S(2)}) collective-permute-start(bf16[64,4608]{1,0:T(8,128)(2,1)} %get-tuple-element.62), channel_id=1, source_target_pairs={{0,8},{8,16},{16,24},{24,0},{1,9},{9,17},{17,25},{25,1},{2,10},{10... | collective-permute-start | bytes 1769480 | tf_op jit(solution)/shard_map/ppermute | solution.py:23
  69.5 11.2 %collective-permute-start.11 = (bf16[64,4608]{1,0:T(8,128)(2,1)}, bf16[64,4608]{1,0:T(8,128)(2,1)S(1)}, u32[]{:S(2)}, u32[]{:S(2)}) collective-permute-start(bf16[64,4608]{1,0:T(8,128)(2,1)} %get-tuple-element.63), channel_id=1, source_target_pairs={{0,24},{8,0},{16,8},{24,16},{1,25},{9,1},{17,9},{25,17},{2,26},{10... | collective-permute-start | bytes 1769480 | tf_op jit(solution)/shard_map/ppermute | solution.py:23
  71.1 11.4 %collective-permute-start.12 = (bf16[64,4608]{1,0:T(8,128)(2,1)}, bf16[64,4608]{1,0:T(8,128)(2,1)}, u32[]{:S(2)}, u32[]{:S(2)}) collective-permute-start(bf16[64,4608]{1,0:T(8,128)(2,1)} %get-tuple-element.64), channel_id=1, source_target_pairs={{0,2},{2,4},{4,6},{6,0},{1,3},{3,5},{5,7},{7,1},{8,10},{10,12},{12... | collective-permute-start | bytes 1769480 | tf_op jit(solution)/shard_map/ppermute | solution.py:23
  71.4 11.1 %collective-permute-start.13 = (bf16[64,4608]{1,0:T(8,128)(2,1)}, bf16[64,4608]{1,0:T(8,128)(2,1)}, u32[]{:S(2)}, u32[]{:S(2)}) collective-permute-start(bf16[64,4608]{1,0:T(8,128)(2,1)} %get-tuple-element.65), channel_id=1, source_target_pairs={{0,6},{2,0},{4,2},{6,4},{1,7},{3,1},{5,3},{7,5},{8,14},{10,8},{12,... | collective-permute-start | bytes 1769480 | tf_op jit(solution)/shard_map/ppermute | solution.py:23
  82.5 7.9 %copy-start.24 = (bf16[128,3584]{1,0:T(8,128)(2,1)S(1)}, bf16[128,3584]{1,0:T(8,128)(2,1)}, u32[]{:S(2)}) copy-start(bf16[128,3584]{1,0:T(8,128)(2,1)} %get-tuple-element.71) | copy-start | bytes 2752516
  82.6 12.7 %copy-start.23 = (bf16[128,3584]{1,0:T(8,128)(2,1)S(1)}, bf16[128,3584]{1,0:T(8,128)(2,1)}, u32[]{:S(2)}) copy-start(bf16[128,3584]{1,0:T(8,128)(2,1)} %get-tuple-element.73) | copy-start | bytes 2752516
  82.6 13.1 %copy-start.26 = (bf16[128,1024]{1,0:T(8,128)(2,1)S(1)}, bf16[128,1024]{1,0:T(8,128)(2,1)}, u32[]{:S(2)}) copy-start(bf16[128,1024]{1,0:T(8,128)(2,1)} %get-tuple-element.72) | copy-start | bytes 786436
  82.6 33.8 %copy-start.25 = (bf16[128,1024]{1,0:T(8,128)(2,1)S(1)}, bf16[128,1024]{1,0:T(8,128)(2,1)}, u32[]{:S(2)}) copy-start(bf16[128,1024]{1,0:T(8,128)(2,1)} %get-tuple-element.74) | copy-start | bytes 786436
  89.9 35.3 %collective-permute-start.14 = (bf16[512,4608]{1,0:T(8,128)(2,1)}, bf16[512,4608]{1,0:T(8,128)(2,1)}, u32[]{:S(2)}, u32[]{:S(2)}) collective-permute-start(bf16[512,4608]{1,0:T(8,128)(2,1)} %get-tuple-element.69.refs_0_), channel_id=1, source_target_pairs={{0,1},{1,0},{2,3},{3,2},{4,5},{5,4},{6,7},{7,6},{8,9},{9,8},{10,11... | collective-permute-start | bytes 14155784 | tf_op jit(solution)/shard_map/ppermute | solution.py:23
  90.0 38.4 %collective-permute-start.15 = (bf16[512,4608]{1,0:T(8,128)(2,1)}, bf16[512,4608]{1,0:T(8,128)(2,1)}, u32[]{:S(2)}, u32[]{:S(2)}) collective-permute-start(bf16[512,4608]{1,0:T(8,128)(2,1)} %get-tuple-element.70.refs_2_), channel_id=1, source_target_pairs={{0,1},{1,0},{2,3},{3,2},{4,5},{5,4},{6,7},{7,6},{8,9},{9,8},{10,11... | collective-permute-start | bytes 14155784 | tf_op jit(solution)/shard_map/ppermute | solution.py:23
  90.5 25.9 %collective-permute-start.16 = (bf16[128,3584]{1,0:T(8,128)(2,1)S(1)}, bf16[128,3584]{1,0:T(8,128)(2,1)S(1)}, u32[]{:S(2)}, u32[]{:S(2)}) collective-permute-start(bf16[128,3584]{1,0:T(8,128)(2,1)S(1)} %copy-done.24), channel_id=1, source_target_pairs={{0,4},{2,6},{4,0},{6,2},{1,5},{3,7},{5,1},{7,3},{8,12},{10,14},{12... | collective-permute-start | bytes 2752520 | tf_op jit(solution)/shard_map/ppermute | solution.py:23
  95.2 23.6 %collective-permute-start.18 = (bf16[128,3584]{1,0:T(8,128)(2,1)S(1)}, bf16[128,3584]{1,0:T(8,128)(2,1)S(1)}, u32[]{:S(2)}, u32[]{:S(2)}) collective-permute-start(bf16[128,3584]{1,0:T(8,128)(2,1)S(1)} %copy-done.23), channel_id=1, source_target_pairs={{0,16},{8,24},{16,0},{24,8},{1,17},{9,25},{17,1},{25,9},{2,18},{10... | collective-permute-start | bytes 2752520 | tf_op jit(solution)/shard_map/ppermute | solution.py:23
  95.6 25.8 %collective-permute-start.17 = (bf16[128,1024]{1,0:T(8,128)(2,1)S(1)}, bf16[128,1024]{1,0:T(8,128)(2,1)S(1)}, u32[]{:S(2)}, u32[]{:S(2)}) collective-permute-start(bf16[128,1024]{1,0:T(8,128)(2,1)S(1)} %copy-done.26), channel_id=1, source_target_pairs={{0,4},{2,6},{4,0},{6,2},{1,5},{3,7},{5,1},{7,3},{8,12},{10,14},{12... | collective-permute-start | bytes 786440 | tf_op jit(solution)/shard_map/ppermute | solution.py:23
  116.4 8.8 %copy-start.6 = (bf16[128,3584]{1,0:T(8,128)(2,1)}, bf16[128,3584]{1,0:T(8,128)(2,1)S(1)}, u32[]{:S(2)}) copy-start(bf16[128,3584]{1,0:T(8,128)(2,1)S(1)} %collective-permute-done.16.refs_6_) | copy-start | bytes 2752516
  116.4 8.8 %collective-permute-start.19 = (bf16[128,1024]{1,0:T(8,128)(2,1)S(1)}, bf16[128,1024]{1,0:T(8,128)(2,1)S(1)}, u32[]{:S(2)}, u32[]{:S(2)}) collective-permute-start(bf16[128,1024]{1,0:T(8,128)(2,1)S(1)} %copy-done.25), channel_id=1, source_target_pairs={{0,16},{8,24},{16,0},{24,8},{1,17},{9,25},{17,1},{25,9},{2,18},{10... | collective-permute-start | bytes 786440 | tf_op jit(solution)/shard_map/ppermute | solution.py:23
  118.8 6.3 %copy-start.7 = (bf16[128,3584]{1,0:T(8,128)(2,1)}, bf16[128,3584]{1,0:T(8,128)(2,1)S(1)}, u32[]{:S(2)}) copy-start(bf16[128,3584]{1,0:T(8,128)(2,1)S(1)} %collective-permute-done.18.refs_8_) | copy-start | bytes 2752516
  118.8 29.1 %collective-permute-start.22 = (bf16[128,4608]{1,0:T(8,128)(2,1)}, bf16[128,4608]{1,0:T(8,128)(2,1)S(1)}, u32[]{:S(2)}, u32[]{:S(2)}) collective-permute-start(bf16[128,4608]{1,0:T(8,128)(2,1)} %get-tuple-element.80), channel_id=1, source_target_pairs={{0,2},{2,4},{4,6},{6,0},{1,3},{3,5},{5,7},{7,1},{8,10},{10,12},{12... | collective-permute-start | bytes 3538952 | tf_op jit(solution)/shard_map/ppermute | solution.py:23
  121.4 7.0 %copy-start.14 = (bf16[128,1024]{1,0:T(8,128)(2,1)}, bf16[128,1024]{1,0:T(8,128)(2,1)S(1)}, u32[]{:S(2)}) copy-start(bf16[128,1024]{1,0:T(8,128)(2,1)S(1)} %collective-permute-done.17.refs_7_) | copy-start | bytes 786436
  121.4 28.2 %collective-permute-start.23 = (bf16[128,4608]{1,0:T(8,128)(2,1)}, bf16[128,4608]{1,0:T(8,128)(2,1)S(1)}, u32[]{:S(2)}, u32[]{:S(2)}) collective-permute-start(bf16[128,4608]{1,0:T(8,128)(2,1)} %get-tuple-element.81), channel_id=1, source_target_pairs={{0,6},{2,0},{4,2},{6,4},{1,7},{3,1},{5,3},{7,5},{8,14},{10,8},{12,... | collective-permute-start | bytes 3538952 | tf_op jit(solution)/shard_map/ppermute | solution.py:23
  125.1 31.0 %collective-permute-start.24 = (bf16[128,4608]{1,0:T(8,128)(2,1)}, bf16[128,4608]{1,0:T(8,128)(2,1)S(1)}, u32[]{:S(2)}, u32[]{:S(2)}) collective-permute-start(bf16[128,4608]{1,0:T(8,128)(2,1)} %get-tuple-element.82), channel_id=1, source_target_pairs={{0,8},{8,16},{16,24},{24,0},{1,9},{9,17},{17,25},{25,1},{2,10},{10... | collective-permute-start | bytes 3538952 | tf_op jit(solution)/shard_map/ppermute | solution.py:23
  125.2 30.9 %collective-permute-start.25 = (bf16[128,4608]{1,0:T(8,128)(2,1)}, bf16[128,4608]{1,0:T(8,128)(2,1)}, u32[]{:S(2)}, u32[]{:S(2)}) collective-permute-start(bf16[128,4608]{1,0:T(8,128)(2,1)} %get-tuple-element.83), channel_id=1, source_target_pairs={{0,24},{8,0},{16,8},{24,16},{1,25},{9,1},{17,9},{25,17},{2,26},{10... | collective-permute-start | bytes 3538952 | tf_op jit(solution)/shard_map/ppermute | solution.py:23
  139.4 33.1 %collective-permute-start.20 = (bf16[640,128]{1,0:T(8,128)(2,1)}, bf16[640,128]{1,0:T(8,128)(2,1)S(1)}, u32[]{:S(2)}, u32[]{:S(2)}) collective-permute-start(bf16[640,128]{1,0:T(8,128)(2,1)} %get-tuple-element.77), channel_id=1, source_target_pairs={{0,4},{2,6},{4,0},{6,2},{1,5},{3,7},{5,1},{7,3},{8,12},{10,14},{12... | collective-permute-start | bytes 491528 | tf_op jit(solution)/shard_map/ppermute | solution.py:23
  147.9 8.3 %copy-start.3 = (bf16[128,4608]{1,0:T(8,128)(2,1)}, bf16[128,4608]{1,0:T(8,128)(2,1)S(1)}, u32[]{:S(2)}) copy-start(bf16[128,4608]{1,0:T(8,128)(2,1)S(1)} %collective-permute-done.22.refs_4_) | copy-start | bytes 3538948
  147.9 24.6 %collective-permute-start.21 = (bf16[640,128]{1,0:T(8,128)(2,1)}, bf16[640,128]{1,0:T(8,128)(2,1)S(1)}, u32[]{:S(2)}, u32[]{:S(2)}) collective-permute-start(bf16[640,128]{1,0:T(8,128)(2,1)} %get-tuple-element.79), channel_id=1, source_target_pairs={{0,16},{8,24},{16,0},{24,8},{1,17},{9,25},{17,1},{25,9},{2,18},{10... | collective-permute-start | bytes 491528 | tf_op jit(solution)/shard_map/ppermute | solution.py:23
  149.6 6.5 %copy-start.4 = (bf16[128,4608]{1,0:T(8,128)(2,1)}, bf16[128,4608]{1,0:T(8,128)(2,1)S(1)}, u32[]{:S(2)}) copy-start(bf16[128,4608]{1,0:T(8,128)(2,1)S(1)} %collective-permute-done.23.refs_5_) | copy-start | bytes 3538948
  167.9 5.6 %collective-permute-start.26 = (bf16[640,128]{1,0:T(8,128)(2,1)}, bf16[640,128]{1,0:T(8,128)(2,1)S(1)}, u32[]{:S(2)}, u32[]{:S(2)}) collective-permute-start(bf16[640,128]{1,0:T(8,128)(2,1)} %get-tuple-element.85), channel_id=1, source_target_pairs={{0,6},{2,0},{4,2},{6,4},{1,7},{3,1},{5,3},{7,5},{8,14},{10,8},{12,... | collective-permute-start | bytes 491528 | tf_op jit(solution)/shard_map/ppermute | solution.py:23
  169.6 5.6 %collective-permute-start.27 = (bf16[640,128]{1,0:T(8,128)(2,1)}, bf16[640,128]{1,0:T(8,128)(2,1)S(1)}, u32[]{:S(2)}, u32[]{:S(2)}) collective-permute-start(bf16[640,128]{1,0:T(8,128)(2,1)} %get-tuple-element.86), channel_id=1, source_target_pairs={{0,2},{2,4},{4,6},{6,0},{1,3},{3,5},{5,7},{7,1},{8,10},{10,12},{12... | collective-permute-start | bytes 491528 | tf_op jit(solution)/shard_map/ppermute | solution.py:23
  170.0 5.6 %collective-permute-start.28 = (bf16[640,128]{1,0:T(8,128)(2,1)}, bf16[640,128]{1,0:T(8,128)(2,1)S(1)}, u32[]{:S(2)}, u32[]{:S(2)}) collective-permute-start(bf16[640,128]{1,0:T(8,128)(2,1)} %get-tuple-element.87), channel_id=1, source_target_pairs={{0,24},{8,0},{16,8},{24,16},{1,25},{9,1},{17,9},{25,17},{2,26},{10... | collective-permute-start | bytes 491528 | tf_op jit(solution)/shard_map/ppermute | solution.py:23
  172.5 6.7 %copy-start.16 = (bf16[640,128]{1,0:T(8,128)(2,1)}, bf16[640,128]{1,0:T(8,128)(2,1)S(1)}, u32[]{:S(2)}) copy-start(bf16[640,128]{1,0:T(8,128)(2,1)S(1)} %collective-permute-done.20.refs_1_) | copy-start | bytes 491524
  172.5 6.7 %collective-permute-start.29 = (bf16[640,128]{1,0:T(8,128)(2,1)}, bf16[640,128]{1,0:T(8,128)(2,1)S(1)}, u32[]{:S(2)}, u32[]{:S(2)}) collective-permute-start(bf16[640,128]{1,0:T(8,128)(2,1)} %get-tuple-element.88), channel_id=1, source_target_pairs={{0,8},{8,16},{16,24},{24,0},{1,9},{9,17},{17,25},{25,1},{2,10},{10... | collective-permute-start | bytes 491528 | tf_op jit(solution)/shard_map/ppermute | solution.py:23
  172.5 6.7 %copy-start.17 = (bf16[640,128]{1,0:T(8,128)(2,1)}, bf16[640,128]{1,0:T(8,128)(2,1)S(1)}, u32[]{:S(2)}) copy-start(bf16[640,128]{1,0:T(8,128)(2,1)S(1)} %collective-permute-done.21.refs_3_) | copy-start | bytes 491524
  173.5 5.7 %copy-start.18 = (bf16[640,128]{1,0:T(8,128)(2,1)}, bf16[640,128]{1,0:T(8,128)(2,1)S(1)}, u32[]{:S(2)}) copy-start(bf16[640,128]{1,0:T(8,128)(2,1)S(1)} %collective-permute-done.26.refs_4_) | copy-start | bytes 491524
  175.2 4.1 %copy-start.19 = (bf16[640,128]{1,0:T(8,128)(2,1)}, bf16[640,128]{1,0:T(8,128)(2,1)S(1)}, u32[]{:S(2)}) copy-start(bf16[640,128]{1,0:T(8,128)(2,1)S(1)} %collective-permute-done.27.refs_5_) | copy-start | bytes 491524
  (11 other events, 26.4 us)

commit v4 on v3

--- a/solution.py
+++ b/solution.py
@@ -35,49 +35,47 @@
         out.wait()
 
 
-def joined_kernel(groups, arrays, *refs):
+def joined_kernel(blocks, arrays, *refs):
     sources, held, sems = refs[:arrays], refs[-2], refs[-1]
-    outs = refs[-3 - len(groups) : -3]
+    outs = refs[-4 - max(out for out, *_ in blocks) : -3]
     copies, row = [], 0
-    for group, out_ref in zip(groups, outs):
-        to = 0
-        for source, first, rows in group:
-            here, i = held.at[pl.ds(row + to, rows)], len(copies)
-            into = pltpu.make_async_copy(sources[source].at[pl.ds(first, rows)], here, sems.at[0, i])
-            out = pltpu.make_async_copy(here, out_ref.at[pl.ds(to, rows)], sems.at[1, i])
-            copies.append(([into], out))
-            to += rows
-        row += to
+    for i, (out, to, source, first, rows) in enumerate(blocks):
+        here = held.at[pl.ds(row, rows)]
+        into = pltpu.make_async_copy(sources[source].at[pl.ds(first, rows)], here, sems.at[0, i])
+        copies.append(
+            ([into], pltpu.make_async_copy(here, outs[out].at[pl.ds(to, rows)], sems.at[1, i]))
+        )
+        row += rows
     moved(copies)
 
 
-def joined(groups, after):
-    arrays = []
-    listed = []
-    for group in groups:
-        for array, _, _ in group:
+def joined(groups, after, into=None):
+    arrays, blocks = [], []
+    for out, (_, *group) in enumerate(groups):
+        for to, array, first, rows in group:
             if not any(array is known for known in arrays):
                 arrays.append(array)
-        index = lambda array: [array is known for known in arrays].index(True)
-        listed.append([(index(array), first, rows) for array, first, rows in group])
-    sizes = [sum(rows for _, _, rows in group) for group in listed]
+            source = [array is known for known in arrays].index(True)
+            blocks.append((out, to, source, first, rows))
     wide, dtype = arrays[0].shape[1], arrays[0].dtype
+    into = [] if into is None else [into]
     *outs, token = pl.pallas_call(
-        functools.partial(joined_kernel, listed, len(arrays)),
-        in_specs=[ANY] * (len(arrays) + len(after)),
-        out_specs=[ANY] * (len(sizes) + 1),
-        out_shape=[jax.ShapeDtypeStruct((size, wide), dtype) for size in sizes] + [TOKEN],
+        functools.partial(joined_kernel, blocks, len(arrays)),
+        in_specs=[ANY] * (len(arrays) + len(into) + len(after)),
+        out_specs=[ANY] * (len(groups) + 1),
+        out_shape=[jax.ShapeDtypeStruct((size, wide), dtype) for size, *_ in groups] + [TOKEN],
         scratch_shapes=[
-            pltpu.VMEM((sum(sizes), wide), dtype),
-            pltpu.SemaphoreType.DMA((2, sum(len(group) for group in listed))),
-        ],
+            pltpu.VMEM((sum(block[-1] for block in blocks), wide), dtype),
+            pltpu.SemaphoreType.DMA((2, len(blocks))),
+        ],
+        input_output_aliases={len(arrays) + i: i for i in range(len(into))},
         compiler_params=pltpu.CompilerParams(vmem_limit_bytes=VMEM_BYTES),
         name="joined",
-    )(*arrays, *after)
+    )(*arrays, *into, *after)
     return outs, token
 
 
-def cut_kernel(plan, arrays, *refs):
+def cut_kernel(plan, arrays, starts, *refs):
     sources = refs[:arrays]
     count = len(plan)
     outs, held, sems = refs[-2 - 2 * count : -2 - count], refs[-1 - count : -1], refs[-1]
@@ -95,26 +93,30 @@
                     sems.at[at, len(into)],
                 )
             )
-        copies.append((into, pltpu.make_async_copy(buffer, out_ref, sems.at[at, len(into)])))
+        target = out_ref.at[:, pl.ds(starts[at], buffer.shape[1])]
+        copies.append((into, pltpu.make_async_copy(buffer, target, sems.at[at, len(into)])))
     moved(copies)
 
 
-def cut(arrays, plan, after):
+def cut(arrays, plan, after, wide=None, into=None, start=0):
     shapes = [
-        (max(to_row + rows[1] for _, rows, to_row, *_ in item), max(to + wide for _, _, _, to, _, wide, *_ in item))
+        (max(to_row + rows[1] for _, rows, to_row, *_ in item), max(to + columns for _, _, _, to, _, columns, *_ in item))
         for item in plan
     ]
     dtype = arrays[0].dtype
+    into = into or []
     *outs, token = pl.pallas_call(
-        functools.partial(cut_kernel, plan, len(arrays)),
-        in_specs=[ANY] * (len(arrays) + len(after)),
+        functools.partial(cut_kernel, plan, len(arrays), [start] * len(plan)),
+        in_specs=[ANY] * (len(arrays) + len(into) + len(after)),
         out_specs=[ANY] * (len(plan) + 1),
-        out_shape=[jax.ShapeDtypeStruct(shape, dtype) for shape in shapes] + [TOKEN],
+        out_shape=[jax.ShapeDtypeStruct((shape[0], wide or shape[1]), dtype) for shape in shapes]
+        + [TOKEN],
         scratch_shapes=[pltpu.VMEM(shape, dtype) for shape in shapes]
         + [pltpu.SemaphoreType.DMA((len(plan), 1 + max(len(item) for item in plan)))],
+        input_output_aliases={len(arrays) + i: i for i in range(len(into))},
         compiler_params=pltpu.CompilerParams(vmem_limit_bytes=VMEM_BYTES),
         name="cut",
-    )(*arrays, *after)
+    )(*arrays, *into, *after)
     return outs, token
 
 
@@ -161,14 +163,13 @@
     )(section, inputs, gains, top, *after)
 
 
-def project_kernel(plan, sources, kept, up_wide, down_wide, where_ref, *refs):
+def project_kernel(plan, sources, up_wide, down_wide, where_ref, *refs):
     pieces = len(plan)
-    factor_refs, token_refs = refs[:kept], refs[kept:]
+    factor_refs, token_refs = refs[:CORES], refs[CORES:]
     outs = refs[-4 - pieces : -4]
     factor_ref, token_ref, sems = refs[-3:]
     capacity = where_ref.shape[1]
     rank = factor_ref.shape[1] // capacity
-    held = factor_refs[0].shape[0] // rank
     halves = 2
     y, z, c = (lax.axis_index(axis) for axis in ("y", "z", "c"))
     wides = up_wide, down_wide
@@ -206,39 +207,46 @@
             to += wide
         return copies
 
-    def begin(piece):
+    groups = 2
+    slots = capacity // groups
+    chunks = [(piece, group) for piece in range(pieces) for group in range(groups)]
+
+    def begin(piece, group):
         half, _ = plan[piece]
-        for copy in token_copies(piece):
-            copy.start()
+        if group == 0:
+            for copy in token_copies(piece):
+                copy.start()
         listed = row_of(piece)
-        here = factor_refs[half * (kept // halves) : (half + 1) * (kept // halves)]
-        for slot in range(capacity):
+        held = SIDE * SIDE
+        for slot in range(group * slots, (group + 1) * slots):
             row = where_ref[listed, slot]
-            for at, source in enumerate(here):
-
-                @pl.when((row >= at * held) & (row < (at + 1) * held))
-                def _(source=source, row=row, at=at, slot=slot, piece=piece):
-                    slot_copy(source, row - at * held, piece, slot).start()
+            for core, source in enumerate(factor_refs):
+
+                @pl.when(row // held == core)
+                def _(source=source, row=half * held + row % held, slot=slot, piece=piece):
+                    slot_copy(source, row, piece, slot).start()
 
     size = capacity * rank
     ahead = 2
-    for piece in range(min(ahead, pieces)):
-        begin(piece)
-    for piece, out_ref in enumerate(outs):
-        for copy in token_copies(piece):
-            copy.wait()
-        for slot in range(capacity):
+    for chunk in chunks[:ahead]:
+        begin(*chunk)
+    for at, (piece, group) in enumerate(chunks):
+        if group == 0:
+            for copy in token_copies(piece):
+                copy.wait()
+        for slot in range(group * slots, (group + 1) * slots):
             slot_copy(factor_refs[0], 0, piece, slot).wait()
-        if piece + ahead < pieces:
-            begin(piece + ahead)
+        if at + ahead < len(chunks):
+            begin(*chunks[at + ahead])
+        first, last = group * slots * rank, (group + 1) * slots * rank
         for side, columns in enumerate((slice(0, up_wide), slice(up_wide, up_wide + down_wide))):
             part = lax.dot_general(
-                factor_ref[piece, :, columns],
+                factor_ref[piece, first:last, columns],
                 token_ref[piece, :, columns],
                 (((1,), (1,)), ((), ())),
                 preferred_element_type=jnp.float32,
             )
-            out_ref[side * size : (side + 1) * size] = part.astype(out_ref.dtype)
+            outs[piece][side * size + first : side * size + last] = part.astype(outs[piece].dtype)
 
 
 def project(plan, where, tokens, factors, rank, up_wide, down_wide, after):
@@ -255,7 +263,7 @@
         )
     vmem = pl.BlockSpec(memory_space=pltpu.VMEM)
     *outs, token = pl.pallas_call(
-        functools.partial(project_kernel, plan, sources, len(factors), up_wide, down_wide),
+        functools.partial(project_kernel, plan, sources, up_wide, down_wide),
         in_specs=[SMEM] + [ANY] * (len(factors) + len(arrays) + len(after)),
         out_specs=[vmem] * pieces + [ANY],
         out_shape=[
@@ -325,8 +333,12 @@
     axes, other_axes = ("z", "y"), ("y", "z")
     halves = range(2)
 
-    def whole(array):
-        return (array, 0, array.shape[0])
+    def stacked(first, pieces):
+        blocks = []
+        for piece in pieces:
+            blocks.append((first, piece, 0, piece.shape[0]))
+            first += piece.shape[0]
+        return blocks
 
     def slices(half, sources, wides, rows, steps):
         items = []
@@ -361,17 +373,18 @@
     live = (jnp.arange(rows, dtype=jnp.int32) < counts[0]).astype(jnp.float32)[None, :]
 
     outs, token = cut(
-        [up, down, hidden],
-        [item for half in halves for item in slices(half, (2,), (up_wide,), rows, (2,))]
-        + [
+        [up, down],
+        [
             item
             for half in halves
             for item in slices(half, (0, 1), (up_wide, down_wide), rank, (0, 1, -1, 2))
         ],
         [],
     )
-    far_up = [shifted(outs[half], axes[half], 2) for half in halves]
-    pieces = outs[2 : 2 + SIDE], outs[2 + SIDE :]
+    arrived = [
+        outs[half * SIDE : half * SIDE + 1] + spread(outs[half * SIDE + 1 : (half + 1) * SIDE], axes[half])
+        for half in halves
+    ]
     block = rows // sections
     extra = width // block
     (payload,), token = cut(
@@ -391,17 +404,17 @@
     inputs = lax.all_to_all(payload.reshape(sections, block, -1), "x", 0, 0, tiled=True)
     gains = inputs[:, :, width:].reshape(sections, width)
 
-    near, token = joined(
-        [
-            [whole(pieces[half][0])] + [whole(p) for p in spread(pieces[half][1:], axes[half])]
-            for half in halves
-        ],
-        [token],
-    )
+    near, token = joined([[SIDE * rank] + stacked(0, arrived[half]) for half in halves], [token])
     size = near[0].shape[0]
     before = [shifted(near[half], other_axes[half], 1) for half in halves]
     after = [shifted(near[half], other_axes[half], -1) for half in halves]
 
+    sent, token = cut(
+        [hidden],
+        [item for half in halves for item in slices(half, (0,), (up_wide,), rows, (1, -1, 2))],
+        [token],
+        wide=up_wide + down_wide,
+    )
     cotangents, token = chain(
         section.reshape(1).astype(jnp.int32),
         inputs,
@@ -412,48 +425,67 @@
     cotangent = lax.all_to_all(cotangents, "x", 0, 0, tiled=True).reshape(rows, width)
 
     forward, token = joined(
-        [[(array, half * size // 2, size // 2)] for half in halves for array in (before, after)[half]],
+        [
+            [size // 2, (0, array, half * size // 2, size // 2)]
+            for half in halves
+            for array in (before, after)[half]
+        ],
         [token],
     )
     far = [
         (shifted(forward[half], other_axes[half], 1), shifted(forward[2 + half], other_axes[half], -1))
         for half in halves
     ]
-    sent, token = cut(
-        [hidden, cotangent],
-        [item for half in halves for item in slices(half, (1,), (down_wide,), rows, (2,))]
-        + [
-            item
-            for half in halves
-            for item in slices(half, (0, 1), (up_wide, down_wide), rows, (1, -1))
+    ring = SIDE * size
+    (mine,), token = joined(
+        [
+            [2 * ring]
+            + [
+                block
+                for half in halves
+                for block in stacked(half * ring, (near[half], before[half], after[half]))
+            ]
         ],
         [token],
     )
-    far_down = [shifted(sent[half], axes[half], 2) for half in halves]
-    beside = [
-        [shifted(sent[2 + 2 * half], axes[half], 1), shifted(sent[3 + 2 * half], axes[half], -1)]
-        for half in halves
-    ]
-    mine, token = joined(
+    def completed(of_half, steps, after):
+        return cut(
+            [cotangent],
+            [item for half in halves for item in slices(half, (0,), (down_wide,), rows, steps)],
+            after,
+            wide=up_wide + down_wide,
+            into=[sent[half * (SIDE - 1) + at] for half in halves for at in of_half],
+            start=up_wide,
+        )
+
+    beside, token = completed((0, 1), (1, -1), [token])
+    (mine,), token = joined(
         [
-            [whole(part) for part in (near[half], before[half], after[half], *far[half])]
-            for half in halves
+            [2 * ring]
+            + [block for half in halves for block in stacked(half * ring + 3 * size, far[half])]
         ],
         [token],
-    )
-    factors = [array for half in halves for array in (mine[half], shifted(mine[half], "c", 1))]
+        into=mine,
+    )
+    factors = [mine, shifted(mine, "c", 1)]
+    farthest, token = completed((2,), (2,), [token, factors[1]])
+    arrived = [None, None]
+    for half in (1, 0):
+        arrived[half] = [
+            shifted(beside[2 * half], axes[half], 1),
+            shifted(beside[2 * half + 1], axes[half], -1),
+        ]
+    for half in halves:
+        arrived[half].append(shifted(farthest[half], axes[half], 2))
 
     parts = []
-    for distances in ((0, 2), (3, 1)):
-        plan = [(half, distance) for half in halves for distance in distances]
+    for plan in (((0, 0), (1, 0), (1, 3), (1, 1)), ((0, 3), (0, 1), (0, 2), (1, 2))):
         tokens = []
         for half, distance in plan:
             if distance == 0:
                 tokens.append(((hidden, None), (cotangent, None)))
-            elif distance == 2:
-                tokens.append(((far_up[half], 0), (far_down[half], 0)))
             else:
-                piece = beside[half][RELATIVE.index(distance) - 1]
+                piece = arrived[half][RELATIVE.index(distance) - 1]
                 tokens.append(((piece, 0), (piece, up_wide)))
         products, token = project(plan, where, tokens, factors, rank, up_wide, down_wide, [token])
         parts += [

time: 184 us -> 175 us (0.951)
  waiting for transfers between devices: 66.2 us -> 55.7 us
  Pallas kernels: 52.2 us -> 56.2 us
  starting transfers between devices: 53.8 us -> 51.6 us
    ppermute x30 -> x27, waiting for transfers between devices: 65 us -> 55.7 us  [shifted(): lax.ppermute(block, axis, [(i, (i + distance) % size) for i in range(size)])]
    pallas_call x8 -> x11, Pallas kernels: 45.3 us -> 49.4 us  [the longest x2 21.6 us: project(): pl.pallas_call(functools.partial(project_kernel, plan, sources, up_wide,...]
    ppermute x30 -> x27, starting transfers between devices: 44.8 us -> 42.6 us  [shifted(): lax.ppermute(block, axis, [(i, (i + distance) % size) for i in range(size)])]
    unnamed x57 -> x41, local copies, waits for them, and re-layouts: 4.57 us -> 4.81 us
  transfers between devices with their start and end apart: 32 -> 29, of which waited for: 19 -> 13; matrix products, arithmetic and copies ran while one was open for 2% -> 2% of each run, Pallas kernels for 20% -> 26%
where the time goes in v4:
time: 175 us; the launch traced here: 174 us
  Pallas kernels  56.2 us (32%)
  waiting for transfers between devices  55.7 us (32%)
  starting transfers between devices  51.6 us (29%)
  local copies, waits for them, and re-layouts  5.59 us (3%)
  other arithmetic  3.58 us (2%)
    ppermute x27, waiting for transfers between devices, shifted(): lax.ppermute(block, axis, [(i, (i + distance) % size) for i in range(size)])  55.7 us
    ppermute x27, starting transfers between devices, shifted(): lax.ppermute(block, axis, [(i, (i + distance) % size) for i in range(size)])  42.6 us
    pallas_call x2, Pallas kernels, project(): pl.pallas_call(functools.partial(project_kernel, plan, sources, up_wide,...  21.6 us
    pallas_call x5, Pallas kernels, cut(): pl.pallas_call(functools.partial(cut_kernel, plan, len(arrays), [start] *...  14.2 us
    pallas_call x4, Pallas kernels, joined(): pl.pallas_call(functools.partial(joined_kernel, blocks, len(arrays)), in_...  13.6 us
    unnamed x41, local copies, waits for them, and re-layouts  4.81 us
    all_to_all x1, starting transfers between devices, body(): lax.all_to_all(cotangents, 'x', 0, 0, tiled=True).reshape(rows, width)  4.71 us
    pallas_call x1, Pallas kernels, chain(): pl.pallas_call(chain_kernel, grid_spec=pltpu.PrefetchScalarGridSpec(num_s...  4.64 us
  transfers between devices with their start and end apart: 29, of which 13 were waited for; matrix products, arithmetic and copies ran while one was open for 2% of the time, Pallas kernels for 26%

profile of v4, /device:TPU:32, one launch (start us, length us, event | category | flops | bytes accessed | tf_op | source)
XLA Modules:
  0.0 173.8 jit_solution(11950997900482269326)
XLA Ops:
  0.0 0.8 reduce
  1.5 2.7 %cut.5 = (bf16[32,4608]{1,0:T(8,128)(2,1)}, bf16[32,4608]{1,0:T(8,128)(2,1)}, bf16[32,4608]{1,0:T(8,128)(2,1)}, bf16[32,4608]{1,0:T(8,128)(2,1)}, bf16[32,4608]{...) custom-call(bf16[32,28672]{1,0:T(8,128)(2,1)} %bitcast.42, ...), custom_call_target="tpu_custom_call" | custom-call | tf_op jit(solution)/shard_map/cut/pallas_call | solution.py:108
  4.1 3.0 %cut.6 = (bf16[128,8448]{1,0:T(8,128)(2,1)}, f32[8,128]{1,0:T(8,128)}) custom-call(bf16[128,8192]{1,0:T(8,128)(2,1)} %bitcast.41, bf16[32,256]{1,0:T(8,128)(2,1)} %reshape.241.refs_1_, f32[8,128]{1,0:T(8,128)} %get-tuple-element.62.refs_2_), custom_call_target="tpu_custom_call" | custom-call | tf_op jit(solution)/shard_map/cut/pallas_call | solution.py:108
  7.1 4.3 %all-to-all-start = ((bf16[4,32,8448]{2,1,0:T(8,128)(2,1)}), bf16[4,32,8448]{2,1,0:T(8,128)(2,1)S(1)}, u32[]{:S(2)}, u32[]{:S(2)}) async-start(bf16[4,32,8448]{2,1,0:T(8,128)(2,1)} %bitcast.40), calls=%async_computation | async-start | bytes 4325376 | tf_op jit(solution)/shard_map/all_to_all | solution.py:404
  11.4 1.9 %collective-permute-start = (bf16[32,4608]{1,0:T(8,128)(2,1)}, bf16[32,4608]{1,0:T(8,128)(2,1)S(1)}, u32[]{:S(2)}, u32[]{:S(2)}) collective-permute-start(bf16[32,4608]{1,0:T(8,128)(2,1)} %get-tuple-element.55), channel_id=1, source_target_pairs={{0,2},{2,4},{4,6},{6,0},{1,3},{3,5},{5,7},{7,1},{8,10},{10,12},{12... | collective-permute-start | bytes 884744 | tf_op jit(solution)/shard_map/ppermute | solution.py:23
  13.5 3.0 %collective-permute-start.2 = (bf16[32,4608]{1,0:T(8,128)(2,1)}, bf16[32,4608]{1,0:T(8,128)(2,1)S(1)}, u32[]{:S(2)}, u32[]{:S(2)}) collective-permute-start(bf16[32,4608]{1,0:T(8,128)(2,1)} %get-tuple-element.57), channel_id=1, source_target_pairs={{0,4},{2,6},{4,0},{6,2},{1,5},{3,7},{5,1},{7,3},{8,12},{10,14},{12... | collective-permute-start | bytes 884744 | tf_op jit(solution)/shard_map/ppermute | solution.py:23
  16.5 1.6 collective-permute-start.3
  18.0 1.7 collective-permute-start.4
  21.8 4.2 %collective-permute-done.refs_1_ = bf16[32,4608]{1,0:T(8,128)(2,1)S(1)} collective-permute-done((bf16[32,4608]{1,0:T(8,128)(2,1)}, bf16[32,4608]{1,0:T(8,128)(2,1)S(1)}, u32[]{:S(2)}, u32[]{:S(2)}) %collective-permute-start) | collective-permute-done | bytes 294944 | tf_op jit(solution)/shard_map/ppermute | solution.py:23
  26.0 3.2 %collective-permute-start.5 = (bf16[32,4608]{1,0:T(8,128)(2,1)}, bf16[32,4608]{1,0:T(8,128)(2,1)}, u32[]{:S(2)}, u32[]{:S(2)}) collective-permute-start(bf16[32,4608]{1,0:T(8,128)(2,1)} %get-tuple-element.61), channel_id=1, source_target_pairs={{0,16},{8,24},{16,0},{24,8},{1,17},{9,25},{17,1},{25,9},{2,18},{10... | collective-permute-start | bytes 884744 | tf_op jit(solution)/shard_map/ppermute | solution.py:23
  30.8 3.7 %collective-permute-done.5.refs_7_ = bf16[32,4608]{1,0:T(8,128)(2,1)} collective-permute-done((bf16[32,4608]{1,0:T(8,128)(2,1)}, bf16[32,4608]{1,0:T(8,128)(2,1)}, u32[]{:S(2)}, u32[]{:S(2)}) %collective-permute-start.5) | collective-permute-done | bytes 294944 | tf_op jit(solution)/shard_map/ppermute | solution.py:23
  34.6 2.5 %joined.4 = (bf16[128,4608]{1,0:T(8,128)(2,1)}, bf16[128,4608]{1,0:T(8,128)(2,1)}, f32[8,128]{1,0:T(8,128)}) custom-call(bf16[32,4608]{1,0:T(8,128)(2,1)} %get-tuple-element.54.refs_0_, bf16[32,4608]{1,0:T(8,128)(2,1)} %copy-done.8, bf16[32,4608]{1,0:T(8,128)(2,1)} %copy-done.9, bf16[32,4608]{1,0:T(8,128)(2,1)} %copy-done.10, ...), custom_call_target="tpu_custom_call" | custom-call | tf_op jit(solution)/shard_map/joined/pallas_call | solution.py:62
  37.1 3.1 %collective-permute-start.8 = (bf16[128,4608]{1,0:T(8,128)(2,1)}, bf16[128,4608]{1,0:T(8,128)(2,1)S(1)}, u32[]{:S(2)}, u32[]{:S(2)}) collective-permute-start(bf16[128,4608]{1,0:T(8,128)(2,1)} %get-tuple-element.64.refs_0_), channel_id=1, source_target_pairs={{0,24},{8,0},{16,8},{24,16},{1,25},{9,1},{17,9},{25,17},{2,26},{10... | collective-permute-start | bytes 3538952 | tf_op jit(solution)/shard_map/ppermute | solution.py:23
  40.2 3.1 %collective-permute-start.7 = (bf16[128,4608]{1,0:T(8,128)(2,1)}, bf16[128,4608]{1,0:T(8,128)(2,1)}, u32[]{:S(2)}, u32[]{:S(2)}) collective-permute-start(bf16[128,4608]{1,0:T(8,128)(2,1)} %get-tuple-element.65.refs_3_), channel_id=1, source_target_pairs={{0,2},{2,4},{4,6},{6,0},{1,3},{3,5},{5,7},{7,1},{8,10},{10,12},{12... | collective-permute-start | bytes 3538952 | tf_op jit(solution)/shard_map/ppermute | solution.py:23
  43.3 4.7 %cut.7 = (bf16[128,4608]{1,0:T(8,128)(2,1)}, bf16[128,4608]{1,0:T(8,128)(2,1)}, bf16[128,4608]{1,0:T(8,128)(2,1)}, bf16[128,4608]{1,0:T(8,128)(2,1)}, bf16[128,4...) custom-call(bf16[128,28672]{1,0:T(8,128)(2,1)} %bitcast.38, f32[8,128]{1,0:T(8,128)} %get-tuple-element.67.refs_1_), custom_call_target="tpu_custom_call" | custom-call | tf_op jit(solution)/shard_map/cut/pallas_call | solution.py:108
  48.1 0.8 copy.37
  49.4 4.6 %cotangent_chain.1 = (bf16[4,32,8192]{2,1,0:T(8,128)(2,1)}, f32[8,128]{1,0:T(8,128)}) custom-call(s32[1]{0:T(128)} %bitcast.10.section_ref, bf16[4,32,8448]{2,1,0:T(8,128)(2,1)} %copy-done.1, bf16[4,8192]{1,0:T(4,128)(2,1)} %bitcast.44, bf16[128,8192]{1,0:T(8,128)(2,1)} %top_ref.1, f32[8,128]{1,0:T(8,128)} %get-tuple-element.68.refs_0_, ...), custom_call_target="tpu_custom_call" | custom-call | tf_op jit(solution)/shard_map/cotangent_chain/pallas_call | solution.py:144
  54.1 4.7 %all-to-all-start.1 = ((bf16[4,32,8192]{2,1,0:T(8,128)(2,1)}), bf16[4,32,8192]{2,1,0:T(8,128)(2,1)S(1)}, u32[]{:S(2)}, u32[]{:S(2)}) async-start(bf16[4,32,8192]{2,1,0:T(8,128)(2,1)} %get-tuple-element.76), calls=%async_computation.1 | async-start | bytes 4194304 | tf_op jit(solution)/shard_map/all_to_all | solution.py:425
  58.8 1.9 %collective-permute-done.8.refs_2_ = bf16[128,4608]{1,0:T(8,128)(2,1)S(1)} collective-permute-done((bf16[128,4608]{1,0:T(8,128)(2,1)}, bf16[128,4608]{1,0:T(8,128)(2,1)S(1)}, u32[]{:S(2)}, u32[]{:S(2)}) %collective-permute-start.8) | collective-permute-done | bytes 1179680 | tf_op jit(solution)/shard_map/ppermute | solution.py:23
  60.7 2.6 %collective-permute-done.6.refs_0_.refs_1_ = bf16[128,4608]{1,0:T(8,128)(2,1)} collective-permute-done((bf16[128,4608]{1,0:T(8,128)(2,1)}, bf16[128,4608]{1,0:T(8,128)(2,1)}, u32[]{:S(2)}, u32[]{:S(2)}) %collective-permute-start.6) | collective-permute-done | bytes 1179680 | tf_op jit(solution)/shard_map/ppermute | solution.py:23
  63.3 1.1 collective-permute-done.7.refs_1_.refs_4_
  64.4 2.6 %joined.5 = (bf16[64,4608]{1,0:T(8,128)(2,1)}, bf16[64,4608]{1,0:T(8,128)(2,1)}, bf16[64,4608]{1,0:T(8,128)(2,1)}, bf16[64,4608]{1,0:T(8,128)(2,1)}, f32[8,128]{1,0:T(8,128)}) custom-call(bf16[128,4608]{1,0:T(8,128)(2,1)} %collective-permute-done.6.refs_0_.refs_1_, bf16[128,4608]{1,0:T(8,128)(2,1)} %collective-permute-done.7.refs_1_.refs_4_, ...), custom_call_target="tpu_custom_call" | custom-call | tf_op jit(solution)/shard_map/joined/pallas_call | solution.py:62
  67.0 1.6 collective-permute-start.10
  68.7 1.7 collective-permute-start.11
  70.6 1.7 collective-permute-start.13
  72.3 5.9 %joined.6 = (bf16[1024,4608]{1,0:T(8,128)(2,1)}, f32[8,128]{1,0:T(8,128)}) custom-call(bf16[128,4608]{1,0:T(8,128)(2,1)} %get-tuple-element.64.refs_0_, bf16[128,4608]{1,0:T(8,128)(2,1)} %collective-permute-done.6.refs_0_.refs_1_, bf16[128,4608]{1,0:T(8,128)(2,1)} %copy-done.2, bf16[128,4608]{1,0:T(8,128)(2,1)} %get-tuple-element.65.refs_3_, ...), custom_call_target="tpu_custom_call" | custom-call | tf_op jit(solution)/shard_map/joined/pallas_call | solution.py:62
  78.3 1.4 copy-done
  79.7 2.0 %cut.8 = (bf16[128,4608]{1,0:T(8,128)(2,1)}, bf16[128,4608]{1,0:T(8,128)(2,1)}, bf16[128,4608]{1,0:T(8,128)(2,1)}, bf16[128,4608]{1,0:T(8,128)(2,1)}, f32[8,128]{1,0:T(8,128)}) custom-call(bf16[128,8192]{1,0:T(8,128)(2,1)} %bitcast.35, ...), custom_call_target="tpu_custom_call", output_to_operand_aliasing={{0}: (1, {}), {1}: (2, {}), {2}: (3, {}), {3}: (4, {})} | custom-call | tf_op jit(solution)/shard_map/cut/pallas_call | solution.py:108
  81.8 0.8 copy-done.6
  82.8 2.5 %joined.7 = (bf16[1024,4608]{1,0:T(8,128)(2,1)}, f32[8,128]{1,0:T(8,128)}) custom-call(bf16[64,4608]{1,0:T(8,128)(2,1)} %copy-done.6, bf16[64,4608]{1,0:T(8,128)(2,1)} %copy-done.7, bf16[64,4608]{1,0:T(8,128)(2,1)} %collective-permute-done.12.refs_2_, bf16[64,4608]{1,0:T(8,128)(2,1)} %collective-permute-done.13.refs_3_, ...), custom_call_target="tpu_custom_call", output_to_operand_aliasing={{0}: (4, {})} | custom-call | tf_op jit(solution)/shard_map/joined/pallas_call | solution.py:62
  85.4 1.0 collective-permute-start.15
  86.4 2.3 %collective-permute-start.16 = (bf16[128,4608]{1,0:T(8,128)(2,1)}, bf16[128,4608]{1,0:T(8,128)(2,1)}, u32[]{:S(2)}, u32[]{:S(2)}) collective-permute-start(bf16[128,4608]{1,0:T(8,128)(2,1)} %get-tuple-element.85), channel_id=1, source_target_pairs={{0,24},{8,0},{16,8},{24,16},{1,25},{9,1},{17,9},{25,17},{2,26},{10... | collective-permute-start | bytes 3538952 | tf_op jit(solution)/shard_map/ppermute | solution.py:23
  88.7 1.3 collective-permute-start.19
  90.0 1.4 collective-permute-start.20
  91.4 8.9 %collective-permute-done.14.refs_4_.refs_1_ = bf16[1024,4608]{1,0:T(8,128)(2,1)} collective-permute-done((bf16[1024,4608]{1,0:T(8,128)(2,1)}, bf16[1024,4608]{1,0:T(8,128)(2,1)}, u32[]{:S(2)}, u32[]{:S(2)}) %collective-permute-start.14) | collective-permute-done | bytes 9437216 | tf_op jit(solution)/shard_map/ppermute | solution.py:23
  100.4 1.8 %cut.9 = (bf16[128,4608]{1,0:T(8,128)(2,1)}, bf16[128,4608]{1,0:T(8,128)(2,1)}, f32[8,128]{1,0:T(8,128)}) custom-call(bf16[128,8192]{1,0:T(8,128)(2,1)} %bitcast.36, bf16[128,4608]{1,0:T(8,128)(2,1)} %get-tuple-element.86.refs_1_, bf16[128,4608]{1,0:T(8,128)(2,1)} %get-tuple-element.87.refs_2_, ...), custom_call_target="tpu_custom_call", output_to_operand_aliasing={{0}: (1, {}), {1}: (2, {})} | custom-call | tf_op jit(solution)/shard_map/cut/pallas_call | solution.py:108
  102.2 3.8 %collective-permute-start.21 = (bf16[128,4608]{1,0:T(8,128)(2,1)}, bf16[128,4608]{1,0:T(8,128)(2,1)S(1)}, u32[]{:S(2)}, u32[]{:S(2)}) collective-permute-start(bf16[128,4608]{1,0:T(8,128)(2,1)} %get-tuple-element.96), channel_id=1, source_target_pairs={{0,4},{2,6},{4,0},{6,2},{1,5},{3,7},{5,1},{7,3},{8,12},{10,14},{12... | collective-permute-start | bytes 3538952 | tf_op jit(solution)/shard_map/ppermute | solution.py:23
  106.0 9.3 %collective-permute-done.15.refs_4_ = bf16[128,4608]{1,0:T(8,128)(2,1)} collective-permute-done((bf16[128,4608]{1,0:T(8,128)(2,1)}, bf16[128,4608]{1,0:T(8,128)(2,1)}, u32[]{:S(2)}, u32[]{:S(2)}) %collective-permute-start.15) | collective-permute-done | bytes 1179680 | tf_op jit(solution)/shard_map/ppermute | solution.py:23
  115.3 10.8 %project.2 = (f32[640,128]{1,0:T(8,128)}, f32[640,128]{1,0:T(8,128)}, bf16[640,128]{1,0:T(8,128)(2,1)}, bf16[640,128]{1,0:T(8,128)(2,1)}, f32[8,128]{1,0:T(8,128)}) custom-call(s32[64,10]{1,0:T(8,128)} %pad_add_fusion.refs_1_.where_ref, bf16[1024,4608]{1,0:T(8,128)(2,1)} %get-tuple-element.83.refs_0_, ...), custom_call_target="tpu_custom_call" | custom-call | tf_op jit(solution)/shard_map/project/pallas_call | solution.py:265
  126.2 2.9 %collective-permute-start.17 = (bf16[640,128]{1,0:T(8,128)(2,1)}, bf16[640,128]{1,0:T(8,128)(2,1)S(1)}, u32[]{:S(2)}, u32[]{:S(2)}) collective-permute-start(bf16[640,128]{1,0:T(8,128)(2,1)} %get-tuple-element.92), channel_id=1, source_target_pairs={{0,24},{8,0},{16,8},{24,16},{1,25},{9,1},{17,9},{25,17},{2,26},{10... | collective-permute-start | bytes 491528 | tf_op jit(solution)/shard_map/ppermute | solution.py:23
  129.1 16.2 %collective-permute-done.21.refs_4_ = bf16[128,4608]{1,0:T(8,128)(2,1)S(1)} collective-permute-done((bf16[128,4608]{1,0:T(8,128)(2,1)}, bf16[128,4608]{1,0:T(8,128)(2,1)S(1)}, u32[]{:S(2)}, u32[]{:S(2)}) %collective-permute-start.21) | collective-permute-done | bytes 1179680 | tf_op jit(solution)/shard_map/ppermute | solution.py:23
  146.4 10.8 %project.3 = (bf16[640,128]{1,0:T(8,128)(2,1)}, bf16[640,128]{1,0:T(8,128)(2,1)}, bf16[640,128]{1,0:T(8,128)(2,1)}, bf16[640,128]{1,0:T(8,128)(2,1)}, f32[8,128]{1,0:T(8,128)}) custom-call(s32[64,10]{1,0:T(8,128)} %pad_add_fusion.refs_1_.where_ref, bf16[1024,4608]{1,0:T(8,128)(2,1)} %get-tuple-element.83.refs_0_, ...), custom_call_target="tpu_custom_call" | custom-call | tf_op jit(solution)/shard_map/project/pallas_call | solution.py:265
  157.2 2.5 %collective-permute-start.23 = (bf16[640,128]{1,0:T(8,128)(2,1)}, bf16[640,128]{1,0:T(8,128)(2,1)S(1)}, u32[]{:S(2)}, u32[]{:S(2)}) collective-permute-start(bf16[640,128]{1,0:T(8,128)(2,1)} %get-tuple-element.99), channel_id=1, source_target_pairs={{0,6},{2,0},{4,2},{6,4},{1,7},{3,1},{5,3},{7,5},{8,14},{10,8},{12,... | collective-permute-start | bytes 491528 | tf_op jit(solution)/shard_map/ppermute | solution.py:23
  159.6 4.2 %collective-permute-start.25 = (bf16[640,128]{1,0:T(8,128)(2,1)}, bf16[640,128]{1,0:T(8,128)(2,1)S(1)}, u32[]{:S(2)}, u32[]{:S(2)}) collective-permute-start(bf16[640,128]{1,0:T(8,128)(2,1)} %get-tuple-element.101), channel_id=1, source_target_pairs={{0,4},{2,6},{4,0},{6,2},{1,5},{3,7},{5,1},{7,3},{8,12},{10,14},{12... | collective-permute-start | bytes 491528 | tf_op jit(solution)/shard_map/ppermute | solution.py:23
  164.3 1.1 collective-permute-done.24.refs_5_
  165.4 2.0 %collective-permute-done.25.refs_6_ = bf16[640,128]{1,0:T(8,128)(2,1)S(1)} collective-permute-done((bf16[640,128]{1,0:T(8,128)(2,1)}, bf16[640,128]{1,0:T(8,128)(2,1)S(1)}, u32[]{:S(2)}, u32[]{:S(2)}) %collective-permute-start.25) | collective-permute-done | bytes 163872 | tf_op jit(solution)/shard_map/ppermute | solution.py:23
  167.4 3.5 %collective-permute-done.26.refs_7_ = bf16[640,128]{1,0:T(8,128)(2,1)S(1)} collective-permute-done((bf16[640,128]{1,0:T(8,128)(2,1)}, bf16[640,128]{1,0:T(8,128)(2,1)S(1)}, u32[]{:S(2)}, u32[]{:S(2)}) %collective-permute-start.26) | collective-permute-done | bytes 163872 | tf_op jit(solution)/shard_map/ppermute | solution.py:23
  171.5 2.2 %scores.1 = f32[32,128]{1,0:T(8,128)} custom-call(f32[32,10]{1,0:T(8,128)} %convert_bitcast_fusion.refs_2_.hits_ref, f32[1,128]{1,0:T(1,128)} %compare_convert_fusion.refs_3_.live_ref, f32[640,128]{1,0:T(8,128)} %get-tuple-element.90.refs_0_, f32[640,128]{1,0:T(8,128)} %get-tuple-element.91.refs_1_, bf16[640,128]{1,0:T(8,128)(2,1)} %copy-done.12, ...), custom_call_target="tpu_custom_call" | custom-call | tf_op jit(solution)/shard_map/scores/pallas_call | solution.py:302
  (78 shorter events, 7.1 us)
Async XLA Ops:
  7.1 13.2 %copy-start.18 = (s32[32,8]{0,1:T(8,128)S(1)}, s32[32,8]{0,1:T(8,128)}, u32[]{:S(2)}) copy-start(s32[32,8]{0,1:T(8,128)} %param.15) | copy-start | bytes 3076
  7.1 40.9 %all-to-all-start = ((bf16[4,32,8448]{2,1,0:T(8,128)(2,1)}), bf16[4,32,8448]{2,1,0:T(8,128)(2,1)S(1)}, u32[]{:S(2)}, u32[]{:S(2)}) async-start(bf16[4,32,8448]{2,1,0:T(8,128)(2,1)} %bitcast.40), calls=%async_computation | async-start | bytes 4325376 | tf_op jit(solution)/shard_map/all_to_all | solution.py:404
  11.4 14.6 %collective-permute-start = (bf16[32,4608]{1,0:T(8,128)(2,1)}, bf16[32,4608]{1,0:T(8,128)(2,1)S(1)}, u32[]{:S(2)}, u32[]{:S(2)}) collective-permute-start(bf16[32,4608]{1,0:T(8,128)(2,1)} %get-tuple-element.55), channel_id=1, source_target_pairs={{0,2},{2,4},{4,6},{6,0},{1,3},{3,5},{5,7},{7,1},{8,10},{10,12},{12... | collective-permute-start | bytes 884744 | tf_op jit(solution)/shard_map/ppermute | solution.py:23
  13.4 17.4 %collective-permute-start.1 = (bf16[32,4608]{1,0:T(8,128)(2,1)}, bf16[32,4608]{1,0:T(8,128)(2,1)S(1)}, u32[]{:S(2)}, u32[]{:S(2)}) collective-permute-start(bf16[32,4608]{1,0:T(8,128)(2,1)} %get-tuple-element.56), channel_id=1, source_target_pairs={{0,6},{2,0},{4,2},{6,4},{1,7},{3,1},{5,3},{7,5},{8,14},{10,8},{12,... | collective-permute-start | bytes 884744 | tf_op jit(solution)/shard_map/ppermute | solution.py:23
  13.5 17.3 %collective-permute-start.2 = (bf16[32,4608]{1,0:T(8,128)(2,1)}, bf16[32,4608]{1,0:T(8,128)(2,1)S(1)}, u32[]{:S(2)}, u32[]{:S(2)}) collective-permute-start(bf16[32,4608]{1,0:T(8,128)(2,1)} %get-tuple-element.57), channel_id=1, source_target_pairs={{0,4},{2,6},{4,0},{6,2},{1,5},{3,7},{5,1},{7,3},{8,12},{10,14},{12... | collective-permute-start | bytes 884744 | tf_op jit(solution)/shard_map/ppermute | solution.py:23
  16.5 14.4 %collective-permute-start.3 = (bf16[32,4608]{1,0:T(8,128)(2,1)}, bf16[32,4608]{1,0:T(8,128)(2,1)S(1)}, u32[]{:S(2)}, u32[]{:S(2)}) collective-permute-start(bf16[32,4608]{1,0:T(8,128)(2,1)} %get-tuple-element.59), channel_id=1, source_target_pairs={{0,8},{8,16},{16,24},{24,0},{1,9},{9,17},{17,25},{25,1},{2,10},{10... | collective-permute-start | bytes 884744 | tf_op jit(solution)/shard_map/ppermute | solution.py:23
  18.0 12.8 %collective-permute-start.4 = (bf16[32,4608]{1,0:T(8,128)(2,1)}, bf16[32,4608]{1,0:T(8,128)(2,1)}, u32[]{:S(2)}, u32[]{:S(2)}) collective-permute-start(bf16[32,4608]{1,0:T(8,128)(2,1)} %get-tuple-element.60), channel_id=1, source_target_pairs={{0,24},{8,0},{16,8},{24,16},{1,25},{9,1},{17,9},{25,17},{2,26},{10... | collective-permute-start | bytes 884744 | tf_op jit(solution)/shard_map/ppermute | solution.py:23
  26.0 8.5 %copy-start.8 = (bf16[32,4608]{1,0:T(8,128)(2,1)}, bf16[32,4608]{1,0:T(8,128)(2,1)S(1)}, u32[]{:S(2)}) copy-start(bf16[32,4608]{1,0:T(8,128)(2,1)S(1)} %collective-permute-done.refs_1_) | copy-start | bytes 884740
  26.0 8.5 %collective-permute-start.5 = (bf16[32,4608]{1,0:T(8,128)(2,1)}, bf16[32,4608]{1,0:T(8,128)(2,1)}, u32[]{:S(2)}, u32[]{:S(2)}) collective-permute-start(bf16[32,4608]{1,0:T(8,128)(2,1)} %get-tuple-element.61), channel_id=1, source_target_pairs={{0,16},{8,24},{16,0},{24,8},{1,17},{9,25},{17,1},{25,9},{2,18},{10... | collective-permute-start | bytes 884744 | tf_op jit(solution)/shard_map/ppermute | solution.py:23
  30.8 3.8 %copy-start.9 = (bf16[32,4608]{1,0:T(8,128)(2,1)}, bf16[32,4608]{1,0:T(8,128)(2,1)S(1)}, u32[]{:S(2)}) copy-start(bf16[32,4608]{1,0:T(8,128)(2,1)S(1)} %collective-permute-done.1.refs_2_) | copy-start | bytes 884740
  30.8 3.8 %copy-start.10 = (bf16[32,4608]{1,0:T(8,128)(2,1)}, bf16[32,4608]{1,0:T(8,128)(2,1)S(1)}, u32[]{:S(2)}) copy-start(bf16[32,4608]{1,0:T(8,128)(2,1)S(1)} %collective-permute-done.2.refs_3_) | copy-start | bytes 884740
  30.8 3.8 %copy-start.11 = (bf16[32,4608]{1,0:T(8,128)(2,1)}, bf16[32,4608]{1,0:T(8,128)(2,1)S(1)}, u32[]{:S(2)}) copy-start(bf16[32,4608]{1,0:T(8,128)(2,1)S(1)} %collective-permute-done.3.refs_5_) | copy-start | bytes 884740
  37.1 23.6 %collective-permute-start.8 = (bf16[128,4608]{1,0:T(8,128)(2,1)}, bf16[128,4608]{1,0:T(8,128)(2,1)S(1)}, u32[]{:S(2)}, u32[]{:S(2)}) collective-permute-start(bf16[128,4608]{1,0:T(8,128)(2,1)} %get-tuple-element.64.refs_0_), channel_id=1, source_target_pairs={{0,24},{8,0},{16,8},{24,16},{1,25},{9,1},{17,9},{25,17},{2,26},{10... | collective-permute-start | bytes 3538952 | tf_op jit(solution)/shard_map/ppermute | solution.py:23
  40.2 23.1 %collective-permute-start.6 = (bf16[128,4608]{1,0:T(8,128)(2,1)}, bf16[128,4608]{1,0:T(8,128)(2,1)}, u32[]{:S(2)}, u32[]{:S(2)}) collective-permute-start(bf16[128,4608]{1,0:T(8,128)(2,1)} %get-tuple-element.64.refs_0_), channel_id=1, source_target_pairs={{0,8},{8,16},{16,24},{24,0},{1,9},{9,17},{17,25},{25,1},{2,10},{10... | collective-permute-start | bytes 3538952 | tf_op jit(solution)/shard_map/ppermute | solution.py:23
  40.2 23.1 %collective-permute-start.9 = (bf16[128,4608]{1,0:T(8,128)(2,1)}, bf16[128,4608]{1,0:T(8,128)(2,1)}, u32[]{:S(2)}, u32[]{:S(2)}) collective-permute-start(bf16[128,4608]{1,0:T(8,128)(2,1)} %get-tuple-element.65.refs_3_), channel_id=1, source_target_pairs={{0,6},{2,0},{4,2},{6,4},{1,7},{3,1},{5,3},{7,5},{8,14},{10,8},{12,... | collective-permute-start | bytes 3538952 | tf_op jit(solution)/shard_map/ppermute | solution.py:23
  40.2 24.2 %collective-permute-start.7 = (bf16[128,4608]{1,0:T(8,128)(2,1)}, bf16[128,4608]{1,0:T(8,128)(2,1)}, u32[]{:S(2)}, u32[]{:S(2)}) collective-permute-start(bf16[128,4608]{1,0:T(8,128)(2,1)} %get-tuple-element.65.refs_3_), channel_id=1, source_target_pairs={{0,2},{2,4},{4,6},{6,0},{1,3},{3,5},{5,7},{7,1},{8,10},{10,12},{12... | collective-permute-start | bytes 3538952 | tf_op jit(solution)/shard_map/ppermute | solution.py:23
  48.1 1.4 copy-start.1
  54.1 24.2 %all-to-all-start.1 = ((bf16[4,32,8192]{2,1,0:T(8,128)(2,1)}), bf16[4,32,8192]{2,1,0:T(8,128)(2,1)S(1)}, u32[]{:S(2)}, u32[]{:S(2)}) async-start(bf16[4,32,8192]{2,1,0:T(8,128)(2,1)} %get-tuple-element.76), calls=%async_computation.1 | async-start | bytes 4194304 | tf_op jit(solution)/shard_map/all_to_all | solution.py:425
  60.7 3.7 %copy-start.2 = (bf16[128,4608]{1,0:T(8,128)(2,1)}, bf16[128,4608]{1,0:T(8,128)(2,1)S(1)}, u32[]{:S(2)}) copy-start(bf16[128,4608]{1,0:T(8,128)(2,1)S(1)} %collective-permute-done.8.refs_2_) | copy-start | bytes 3538948
  67.0 14.7 %collective-permute-start.10 = (bf16[64,4608]{1,0:T(8,128)(2,1)}, bf16[64,4608]{1,0:T(8,128)(2,1)S(1)}, u32[]{:S(2)}, u32[]{:S(2)}) collective-permute-start(bf16[64,4608]{1,0:T(8,128)(2,1)} %get-tuple-element.70), channel_id=1, source_target_pairs={{0,8},{8,16},{16,24},{24,0},{1,9},{9,17},{17,25},{25,1},{2,10},{10... | collective-permute-start | bytes 1769480 | tf_op jit(solution)/shard_map/ppermute | solution.py:23
  68.7 13.1 %collective-permute-start.11 = (bf16[64,4608]{1,0:T(8,128)(2,1)}, bf16[64,4608]{1,0:T(8,128)(2,1)S(1)}, u32[]{:S(2)}, u32[]{:S(2)}) collective-permute-start(bf16[64,4608]{1,0:T(8,128)(2,1)} %get-tuple-element.71), channel_id=1, source_target_pairs={{0,24},{8,0},{16,8},{24,16},{1,25},{9,1},{17,9},{25,17},{2,26},{10... | collective-permute-start | bytes 1769480 | tf_op jit(solution)/shard_map/ppermute | solution.py:23
  70.3 11.4 %collective-permute-start.12 = (bf16[64,4608]{1,0:T(8,128)(2,1)}, bf16[64,4608]{1,0:T(8,128)(2,1)}, u32[]{:S(2)}, u32[]{:S(2)}) collective-permute-start(bf16[64,4608]{1,0:T(8,128)(2,1)} %get-tuple-element.72), channel_id=1, source_target_pairs={{0,2},{2,4},{4,6},{6,0},{1,3},{3,5},{5,7},{7,1},{8,10},{10,12},{12... | collective-permute-start | bytes 1769480 | tf_op jit(solution)/shard_map/ppermute | solution.py:23
  70.6 11.1 %collective-permute-start.13 = (bf16[64,4608]{1,0:T(8,128)(2,1)}, bf16[64,4608]{1,0:T(8,128)(2,1)}, u32[]{:S(2)}, u32[]{:S(2)}) collective-permute-start(bf16[64,4608]{1,0:T(8,128)(2,1)} %get-tuple-element.73), channel_id=1, source_target_pairs={{0,6},{2,0},{4,2},{6,4},{1,7},{3,1},{5,3},{7,5},{8,14},{10,8},{12,... | collective-permute-start | bytes 1769480 | tf_op jit(solution)/shard_map/ppermute | solution.py:23
  78.3 1.4 copy-start
  81.7 0.8 copy-start.6
  81.7 1.0 copy-start.7
  85.3 15.1 %collective-permute-start.14 = (bf16[1024,4608]{1,0:T(8,128)(2,1)}, bf16[1024,4608]{1,0:T(8,128)(2,1)}, u32[]{:S(2)}, u32[]{:S(2)}) collective-permute-start(bf16[1024,4608]{1,0:T(8,128)(2,1)} %get-tuple-element.83.refs_0_), channel_id=1, source_target_pairs={{0,1},{1,0},{2,3},{3,2},{4,5},{5,4},{6,7},{7,6},{8,9},{9,8},{10,11... | collective-permute-start | bytes 28311560 | tf_op jit(solution)/shard_map/ppermute | solution.py:23
  85.4 29.9 %collective-permute-start.15 = (bf16[128,4608]{1,0:T(8,128)(2,1)}, bf16[128,4608]{1,0:T(8,128)(2,1)}, u32[]{:S(2)}, u32[]{:S(2)}) collective-permute-start(bf16[128,4608]{1,0:T(8,128)(2,1)} %get-tuple-element.84), channel_id=1, source_target_pairs={{0,8},{8,16},{16,24},{24,0},{1,9},{9,17},{17,25},{25,1},{2,10},{10... | collective-permute-start | bytes 3538952 | tf_op jit(solution)/shard_map/ppermute | solution.py:23
  86.4 29.0 %collective-permute-start.16 = (bf16[128,4608]{1,0:T(8,128)(2,1)}, bf16[128,4608]{1,0:T(8,128)(2,1)}, u32[]{:S(2)}, u32[]{:S(2)}) collective-permute-start(bf16[128,4608]{1,0:T(8,128)(2,1)} %get-tuple-element.85), channel_id=1, source_target_pairs={{0,24},{8,0},{16,8},{24,16},{1,25},{9,1},{17,9},{25,17},{2,26},{10... | collective-permute-start | bytes 3538952 | tf_op jit(solution)/shard_map/ppermute | solution.py:23
  88.7 40.4 %collective-permute-start.19 = (bf16[128,4608]{1,0:T(8,128)(2,1)}, bf16[128,4608]{1,0:T(8,128)(2,1)S(1)}, u32[]{:S(2)}, u32[]{:S(2)}) collective-permute-start(bf16[128,4608]{1,0:T(8,128)(2,1)} %get-tuple-element.94), channel_id=1, source_target_pairs={{0,2},{2,4},{4,6},{6,0},{1,3},{3,5},{5,7},{7,1},{8,10},{10,12},{12... | collective-permute-start | bytes 3538952 | tf_op jit(solution)/shard_map/ppermute | solution.py:23
  90.0 39.1 %collective-permute-start.20 = (bf16[128,4608]{1,0:T(8,128)(2,1)}, bf16[128,4608]{1,0:T(8,128)(2,1)S(1)}, u32[]{:S(2)}, u32[]{:S(2)}) collective-permute-start(bf16[128,4608]{1,0:T(8,128)(2,1)} %get-tuple-element.95), channel_id=1, source_target_pairs={{0,6},{2,0},{4,2},{6,4},{1,7},{3,1},{5,3},{7,5},{8,14},{10,8},{12,... | collective-permute-start | bytes 3538952 | tf_op jit(solution)/shard_map/ppermute | solution.py:23
  102.2 43.2 %collective-permute-start.21 = (bf16[128,4608]{1,0:T(8,128)(2,1)}, bf16[128,4608]{1,0:T(8,128)(2,1)S(1)}, u32[]{:S(2)}, u32[]{:S(2)}) collective-permute-start(bf16[128,4608]{1,0:T(8,128)(2,1)} %get-tuple-element.96), channel_id=1, source_target_pairs={{0,4},{2,6},{4,0},{6,2},{1,5},{3,7},{5,1},{7,3},{8,12},{10,14},{12... | collective-permute-start | bytes 3538952 | tf_op jit(solution)/shard_map/ppermute | solution.py:23
  115.3 30.7 %collective-permute-start.22 = (bf16[128,4608]{1,0:T(8,128)(2,1)}, bf16[128,4608]{1,0:T(8,128)(2,1)}, u32[]{:S(2)}, u32[]{:S(2)}) collective-permute-start(bf16[128,4608]{1,0:T(8,128)(2,1)} %get-tuple-element.97), channel_id=1, source_target_pairs={{0,16},{8,24},{16,0},{24,8},{1,17},{9,25},{17,1},{25,9},{2,18},{10... | collective-permute-start | bytes 3538952 | tf_op jit(solution)/shard_map/ppermute | solution.py:23
  126.2 37.7 %collective-permute-start.17 = (bf16[640,128]{1,0:T(8,128)(2,1)}, bf16[640,128]{1,0:T(8,128)(2,1)S(1)}, u32[]{:S(2)}, u32[]{:S(2)}) collective-permute-start(bf16[640,128]{1,0:T(8,128)(2,1)} %get-tuple-element.92), channel_id=1, source_target_pairs={{0,24},{8,0},{16,8},{24,16},{1,25},{9,1},{17,9},{25,17},{2,26},{10... | collective-permute-start | bytes 491528 | tf_op jit(solution)/shard_map/ppermute | solution.py:23
  129.1 16.9 %copy-start.3 = (bf16[128,4608]{1,0:T(8,128)(2,1)}, bf16[128,4608]{1,0:T(8,128)(2,1)S(1)}, u32[]{:S(2)}) copy-start(bf16[128,4608]{1,0:T(8,128)(2,1)S(1)} %collective-permute-done.19.refs_2_) | copy-start | bytes 3538948
  129.1 34.8 %collective-permute-start.18 = (bf16[640,128]{1,0:T(8,128)(2,1)}, bf16[640,128]{1,0:T(8,128)(2,1)S(1)}, u32[]{:S(2)}, u32[]{:S(2)}) collective-permute-start(bf16[640,128]{1,0:T(8,128)(2,1)} %get-tuple-element.93), channel_id=1, source_target_pairs={{0,8},{8,16},{16,24},{24,0},{1,9},{9,17},{17,25},{25,1},{2,10},{10... | collective-permute-start | bytes 491528 | tf_op jit(solution)/shard_map/ppermute | solution.py:23
  129.1 16.9 %copy-start.4 = (bf16[128,4608]{1,0:T(8,128)(2,1)}, bf16[128,4608]{1,0:T(8,128)(2,1)S(1)}, u32[]{:S(2)}) copy-start(bf16[128,4608]{1,0:T(8,128)(2,1)S(1)} %collective-permute-done.20.refs_3_) | copy-start | bytes 3538948
  145.4 1.0 copy-start.5
  157.2 7.1 %collective-permute-start.23 = (bf16[640,128]{1,0:T(8,128)(2,1)}, bf16[640,128]{1,0:T(8,128)(2,1)S(1)}, u32[]{:S(2)}, u32[]{:S(2)}) collective-permute-start(bf16[640,128]{1,0:T(8,128)(2,1)} %get-tuple-element.99), channel_id=1, source_target_pairs={{0,6},{2,0},{4,2},{6,4},{1,7},{3,1},{5,3},{7,5},{8,14},{10,8},{12,... | collective-permute-start | bytes 491528 | tf_op jit(solution)/shard_map/ppermute | solution.py:23
  159.6 5.8 %collective-permute-start.24 = (bf16[640,128]{1,0:T(8,128)(2,1)}, bf16[640,128]{1,0:T(8,128)(2,1)S(1)}, u32[]{:S(2)}, u32[]{:S(2)}) collective-permute-start(bf16[640,128]{1,0:T(8,128)(2,1)} %get-tuple-element.100), channel_id=1, source_target_pairs={{0,2},{2,4},{4,6},{6,0},{1,3},{3,5},{5,7},{7,1},{8,10},{10,12},{12... | collective-permute-start | bytes 491528 | tf_op jit(solution)/shard_map/ppermute | solution.py:23
  159.6 7.7 %collective-permute-start.25 = (bf16[640,128]{1,0:T(8,128)(2,1)}, bf16[640,128]{1,0:T(8,128)(2,1)S(1)}, u32[]{:S(2)}, u32[]{:S(2)}) collective-permute-start(bf16[640,128]{1,0:T(8,128)(2,1)} %get-tuple-element.101), channel_id=1, source_target_pairs={{0,4},{2,6},{4,0},{6,2},{1,5},{3,7},{5,1},{7,3},{8,12},{10,14},{12... | collective-permute-start | bytes 491528 | tf_op jit(solution)/shard_map/ppermute | solution.py:23
  163.9 7.0 %copy-start.12 = (bf16[640,128]{1,0:T(8,128)(2,1)}, bf16[640,128]{1,0:T(8,128)(2,1)S(1)}, u32[]{:S(2)}) copy-start(bf16[640,128]{1,0:T(8,128)(2,1)S(1)} %collective-permute-done.17.refs_2_) | copy-start | bytes 491524
  163.9 7.0 %collective-permute-start.26 = (bf16[640,128]{1,0:T(8,128)(2,1)}, bf16[640,128]{1,0:T(8,128)(2,1)S(1)}, u32[]{:S(2)}, u32[]{:S(2)}) collective-permute-start(bf16[640,128]{1,0:T(8,128)(2,1)} %get-tuple-element.102), channel_id=1, source_target_pairs={{0,16},{8,24},{16,0},{24,8},{1,17},{9,25},{17,1},{25,9},{2,18},{10... | collective-permute-start | bytes 491528 | tf_op jit(solution)/shard_map/ppermute | solution.py:23
  163.9 7.0 %copy-start.13 = (bf16[640,128]{1,0:T(8,128)(2,1)}, bf16[640,128]{1,0:T(8,128)(2,1)S(1)}, u32[]{:S(2)}) copy-start(bf16[640,128]{1,0:T(8,128)(2,1)S(1)} %collective-permute-done.18.refs_3_) | copy-start | bytes 491524
  164.3 6.6 %copy-start.14 = (bf16[640,128]{1,0:T(8,128)(2,1)}, bf16[640,128]{1,0:T(8,128)(2,1)S(1)}, u32[]{:S(2)}) copy-start(bf16[640,128]{1,0:T(8,128)(2,1)S(1)} %collective-permute-done.23.refs_4_) | copy-start | bytes 491524
  165.4 5.5 %copy-start.15 = (bf16[640,128]{1,0:T(8,128)(2,1)}, bf16[640,128]{1,0:T(8,128)(2,1)S(1)}, u32[]{:S(2)}) copy-start(bf16[640,128]{1,0:T(8,128)(2,1)S(1)} %collective-permute-done.24.refs_5_) | copy-start | bytes 491524
  167.4 3.6 %copy-start.16 = (bf16[640,128]{1,0:T(8,128)(2,1)}, bf16[640,128]{1,0:T(8,128)(2,1)S(1)}, u32[]{:S(2)}) copy-start(bf16[640,128]{1,0:T(8,128)(2,1)S(1)} %collective-permute-done.25.refs_6_) | copy-start | bytes 491524
  170.9 0.7 copy-start.17

commit v5 on v4

--- a/solution.py
+++ b/solution.py
@@ -118,6 +118,39 @@
         name="cut",
     )(*arrays, *into, *after)
     return outs, token
+
+
+def payload_kernel(sections, inputs_ref, gains_ref, *refs):
+    out_ref, _, held, sems = refs[-4:]
+    rows, width = inputs_ref.shape
+    block = rows // sections
+    extra = width // block
+    into = pltpu.make_async_copy(inputs_ref, held.at[:, pl.ds(0, width)], sems.at[0])
+    into.start()
+    gains = gains_ref[...].astype(jnp.float32)
+    folded = jnp.concatenate(
+        [gains[:, row * extra : (row + 1) * extra] for row in range(block)], axis=0
+    ).astype(held.dtype)
+    for part in range(sections):
+        held[part * block : (part + 1) * block, width:] = folded
+    into.wait()
+    out = pltpu.make_async_copy(held, out_ref, sems.at[1])
+    out.start()
+    out.wait()
+
+
+def payload_of(inputs, gains, sections, after):
+    rows, width = inputs.shape
+    out = jax.ShapeDtypeStruct((rows, width + width * sections // rows), inputs.dtype)
+    return pl.pallas_call(
+        functools.partial(payload_kernel, sections),
+        in_specs=[ANY, pl.BlockSpec(memory_space=pltpu.VMEM)] + [ANY] * len(after),
+        out_specs=[ANY, ANY],
+        out_shape=[out, TOKEN],
+        scratch_shapes=[pltpu.VMEM(out.shape, out.dtype), pltpu.SemaphoreType.DMA((2,))],
+        compiler_params=pltpu.CompilerParams(vmem_limit_bytes=VMEM_BYTES),
+        name="payload",
+    )(inputs, gains, *after)
 
 
 def chain_kernel(section_ref, inputs_ref, gains_ref, top_ref, *refs):
@@ -381,26 +414,18 @@
         ],
         [],
     )
+    opposite = [shifted(outs[half * SIDE + 3], axes[half], 2) for half in halves]
     arrived = [
-        outs[half * SIDE : half * SIDE + 1] + spread(outs[half * SIDE + 1 : (half + 1) * SIDE], axes[half])
+        [
+            outs[half * SIDE],
+            shifted(outs[half * SIDE + 1], axes[half], 1),
+            shifted(outs[half * SIDE + 2], axes[half], -1),
+            opposite[half],
+        ]
         for half in halves
     ]
     block = rows // sections
-    extra = width // block
-    (payload,), token = cut(
-        [layer_inputs[0], norm_gains.reshape(block, extra)],
-        [
-            [
-                item
-                for part in range(sections)
-                for item in (
-                    (0, (part * block, block), part * block, 0, 0, width, None, 0),
-                    (1, (0, block), part * block, width, 0, extra, None, 0),
-                )
-            ]
-        ],
-        [token],
-    )
+    payload, token = payload_of(layer_inputs[0], norm_gains, sections, [token])
     inputs = lax.all_to_all(payload.reshape(sections, block, -1), "x", 0, 0, tiled=True)
     gains = inputs[:, :, width:].reshape(sections, width)
 

time: 175 us -> 174 us (level)
    pallas_call x0 -> x1, Pallas kernels: none -> 3.72 us  [payload_of(): pl.pallas_call(functools.partial(payload_kernel, sections), in_specs=[ANY...]
    pallas_call x5 -> x4, Pallas kernels: 14.2 us -> 11.3 us  [cut(): pl.pallas_call(functools.partial(cut_kernel, plan, len(arrays), [start] *...]
  transfers between devices with their start and end apart: 29 -> 29, of which waited for: 13 -> 13; matrix products, arithmetic and copies ran while one was open for 2% -> 2% of each run, Pallas kernels for 26% -> 27%
where the time goes in v5:
time: 174 us; the launch traced here: 173 us
  Pallas kernels  57.1 us (33%)
  waiting for transfers between devices  55.6 us (32%)
  starting transfers between devices  51.8 us (30%)
  local copies, waits for them, and re-layouts  4.96 us (3%)
  other arithmetic  2.77 us (2%)
    ppermute x27, waiting for transfers between devices, shifted(): lax.ppermute(block, axis, [(i, (i + distance) % size) for i in range(size)])  55.6 us
    ppermute x27, starting transfers between devices, shifted(): lax.ppermute(block, axis, [(i, (i + distance) % size) for i in range(size)])  42.7 us
    pallas_call x2, Pallas kernels, project(): pl.pallas_call(functools.partial(project_kernel, plan, sources, up_wide,...  21.6 us
    pallas_call x4, Pallas kernels, joined(): pl.pallas_call(functools.partial(joined_kernel, blocks, len(arrays)), in_...  13.6 us
    pallas_call x4, Pallas kernels, cut(): pl.pallas_call(functools.partial(cut_kernel, plan, len(arrays), [start] *...  11.3 us
    unnamed x41, local copies, waits for them, and re-layouts  4.8 us
    all_to_all x1, starting transfers between devices, body(): lax.all_to_all(cotangents, 'x', 0, 0, tiled=True).reshape(rows, width)  4.7 us
    pallas_call x1, Pallas kernels, chain(): pl.pallas_call(chain_kernel, grid_spec=pltpu.PrefetchScalarGridSpec(num_s...  4.62 us
  transfers between devices with their start and end apart: 29, of which 13 were waited for; matrix products, arithmetic and copies ran while one was open for 2% of the time, Pallas kernels for 27%

profile of v5, /device:TPU:32, one launch (start us, length us, event | category | flops | bytes accessed | tf_op | source)
XLA Modules:
  0.0 173.2 jit_solution(18435324268663079693)
XLA Ops:
  0.0 2.7 %cut.4 = (bf16[32,4608]{1,0:T(8,128)(2,1)}, bf16[32,4608]{1,0:T(8,128)(2,1)}, bf16[32,4608]{1,0:T(8,128)(2,1)}, bf16[32,4608]{1,0:T(8,128)(2,1)}, bf16[32,4608]{...) custom-call(bf16[32,28672]{1,0:T(8,128)(2,1)} %bitcast.42, ...), custom_call_target="tpu_custom_call" | custom-call | tf_op jit(solution)/shard_map/cut/pallas_call | solution.py:108
  2.7 3.7 %payload.1 = (bf16[128,8448]{1,0:T(8,128)(2,1)}, f32[8,128]{1,0:T(8,128)}) custom-call(bf16[128,8192]{1,0:T(8,128)(2,1)} %bitcast.41, bf16[1,8192]{1,0:T(2,128)(2,1)} %gains_ref.1, f32[8,128]{1,0:T(8,128)} %get-tuple-element.62.refs_0_), custom_call_target="tpu_custom_call" | custom-call | tf_op jit(solution)/shard_map/payload/pallas_call | solution.py:145
  6.4 4.3 %all-to-all-start = ((bf16[4,32,8448]{2,1,0:T(8,128)(2,1)}), bf16[4,32,8448]{2,1,0:T(8,128)(2,1)S(1)}, u32[]{:S(2)}, u32[]{:S(2)}) async-start(bf16[4,32,8448]{2,1,0:T(8,128)(2,1)} %bitcast.40), calls=%async_computation | async-start | bytes 4325376 | tf_op jit(solution)/shard_map/all_to_all | solution.py:429
  10.7 1.9 %collective-permute-start = (bf16[32,4608]{1,0:T(8,128)(2,1)}, bf16[32,4608]{1,0:T(8,128)(2,1)S(1)}, u32[]{:S(2)}, u32[]{:S(2)}) collective-permute-start(bf16[32,4608]{1,0:T(8,128)(2,1)} %get-tuple-element.55), channel_id=1, source_target_pairs={{0,2},{2,4},{4,6},{6,0},{1,3},{3,5},{5,7},{7,1},{8,10},{10,12},{12... | collective-permute-start | bytes 884744 | tf_op jit(solution)/shard_map/ppermute | solution.py:23
  12.7 3.0 %collective-permute-start.2 = (bf16[32,4608]{1,0:T(8,128)(2,1)}, bf16[32,4608]{1,0:T(8,128)(2,1)S(1)}, u32[]{:S(2)}, u32[]{:S(2)}) collective-permute-start(bf16[32,4608]{1,0:T(8,128)(2,1)} %get-tuple-element.57), channel_id=1, source_target_pairs={{0,4},{2,6},{4,0},{6,2},{1,5},{3,7},{5,1},{7,3},{8,12},{10,14},{12... | collective-permute-start | bytes 884744 | tf_op jit(solution)/shard_map/ppermute | solution.py:23
  15.7 1.6 collective-permute-start.3
  17.3 1.7 collective-permute-start.4
  21.1 4.2 %collective-permute-done.refs_1_ = bf16[32,4608]{1,0:T(8,128)(2,1)S(1)} collective-permute-done((bf16[32,4608]{1,0:T(8,128)(2,1)}, bf16[32,4608]{1,0:T(8,128)(2,1)S(1)}, u32[]{:S(2)}, u32[]{:S(2)}) %collective-permute-start) | collective-permute-done | bytes 294944 | tf_op jit(solution)/shard_map/ppermute | solution.py:23
  25.3 3.2 %collective-permute-start.5 = (bf16[32,4608]{1,0:T(8,128)(2,1)}, bf16[32,4608]{1,0:T(8,128)(2,1)}, u32[]{:S(2)}, u32[]{:S(2)}) collective-permute-start(bf16[32,4608]{1,0:T(8,128)(2,1)} %get-tuple-element.61), channel_id=1, source_target_pairs={{0,16},{8,24},{16,0},{24,8},{1,17},{9,25},{17,1},{25,9},{2,18},{10... | collective-permute-start | bytes 884744 | tf_op jit(solution)/shard_map/ppermute | solution.py:23
  30.1 3.7 %collective-permute-done.5.refs_7_ = bf16[32,4608]{1,0:T(8,128)(2,1)} collective-permute-done((bf16[32,4608]{1,0:T(8,128)(2,1)}, bf16[32,4608]{1,0:T(8,128)(2,1)}, u32[]{:S(2)}, u32[]{:S(2)}) %collective-permute-start.5) | collective-permute-done | bytes 294944 | tf_op jit(solution)/shard_map/ppermute | solution.py:23
  33.9 2.5 %joined.4 = (bf16[128,4608]{1,0:T(8,128)(2,1)}, bf16[128,4608]{1,0:T(8,128)(2,1)}, f32[8,128]{1,0:T(8,128)}) custom-call(bf16[32,4608]{1,0:T(8,128)(2,1)} %get-tuple-element.54.refs_0_, bf16[32,4608]{1,0:T(8,128)(2,1)} %copy-done.8, bf16[32,4608]{1,0:T(8,128)(2,1)} %copy-done.9, bf16[32,4608]{1,0:T(8,128)(2,1)} %copy-done.10, ...), custom_call_target="tpu_custom_call" | custom-call | tf_op jit(solution)/shard_map/joined/pallas_call | solution.py:62
  36.4 3.1 %collective-permute-start.8 = (bf16[128,4608]{1,0:T(8,128)(2,1)}, bf16[128,4608]{1,0:T(8,128)(2,1)S(1)}, u32[]{:S(2)}, u32[]{:S(2)}) collective-permute-start(bf16[128,4608]{1,0:T(8,128)(2,1)} %get-tuple-element.64.refs_0_), channel_id=1, source_target_pairs={{0,24},{8,0},{16,8},{24,16},{1,25},{9,1},{17,9},{25,17},{2,26},{10... | collective-permute-start | bytes 3538952 | tf_op jit(solution)/shard_map/ppermute | solution.py:23
  39.5 3.1 %collective-permute-start.7 = (bf16[128,4608]{1,0:T(8,128)(2,1)}, bf16[128,4608]{1,0:T(8,128)(2,1)}, u32[]{:S(2)}, u32[]{:S(2)}) collective-permute-start(bf16[128,4608]{1,0:T(8,128)(2,1)} %get-tuple-element.65.refs_3_), channel_id=1, source_target_pairs={{0,2},{2,4},{4,6},{6,0},{1,3},{3,5},{5,7},{7,1},{8,10},{10,12},{12... | collective-permute-start | bytes 3538952 | tf_op jit(solution)/shard_map/ppermute | solution.py:23
  42.6 4.7 %cut.5 = (bf16[128,4608]{1,0:T(8,128)(2,1)}, bf16[128,4608]{1,0:T(8,128)(2,1)}, bf16[128,4608]{1,0:T(8,128)(2,1)}, bf16[128,4608]{1,0:T(8,128)(2,1)}, bf16[128,4...) custom-call(bf16[128,28672]{1,0:T(8,128)(2,1)} %bitcast.38, f32[8,128]{1,0:T(8,128)} %get-tuple-element.67.refs_1_), custom_call_target="tpu_custom_call" | custom-call | tf_op jit(solution)/shard_map/cut/pallas_call | solution.py:108
  47.4 0.8 copy.37
  48.7 4.6 %cotangent_chain.1 = (bf16[4,32,8192]{2,1,0:T(8,128)(2,1)}, f32[8,128]{1,0:T(8,128)}) custom-call(s32[1]{0:T(128)} %bitcast.10.section_ref, bf16[4,32,8448]{2,1,0:T(8,128)(2,1)} %copy-done.1, bf16[4,8192]{1,0:T(4,128)(2,1)} %bitcast.44, bf16[128,8192]{1,0:T(8,128)(2,1)} %top_ref.1, f32[8,128]{1,0:T(8,128)} %get-tuple-element.68.refs_0_, ...), custom_call_target="tpu_custom_call" | custom-call | tf_op jit(solution)/shard_map/cotangent_chain/pallas_call | solution.py:177
  53.3 4.7 %all-to-all-start.1 = ((bf16[4,32,8192]{2,1,0:T(8,128)(2,1)}), bf16[4,32,8192]{2,1,0:T(8,128)(2,1)S(1)}, u32[]{:S(2)}, u32[]{:S(2)}) async-start(bf16[4,32,8192]{2,1,0:T(8,128)(2,1)} %get-tuple-element.76), calls=%async_computation.1 | async-start | bytes 4194304 | tf_op jit(solution)/shard_map/all_to_all | solution.py:450
  58.0 2.0 %collective-permute-done.8.refs_2_ = bf16[128,4608]{1,0:T(8,128)(2,1)S(1)} collective-permute-done((bf16[128,4608]{1,0:T(8,128)(2,1)}, bf16[128,4608]{1,0:T(8,128)(2,1)S(1)}, u32[]{:S(2)}, u32[]{:S(2)}) %collective-permute-start.8) | collective-permute-done | bytes 1179680 | tf_op jit(solution)/shard_map/ppermute | solution.py:23
  60.0 2.6 %collective-permute-done.6.refs_0_.refs_1_ = bf16[128,4608]{1,0:T(8,128)(2,1)} collective-permute-done((bf16[128,4608]{1,0:T(8,128)(2,1)}, bf16[128,4608]{1,0:T(8,128)(2,1)}, u32[]{:S(2)}, u32[]{:S(2)}) %collective-permute-start.6) | collective-permute-done | bytes 1179680 | tf_op jit(solution)/shard_map/ppermute | solution.py:23
  62.6 1.1 collective-permute-done.7.refs_1_.refs_4_
  63.7 2.6 %joined.5 = (bf16[64,4608]{1,0:T(8,128)(2,1)}, bf16[64,4608]{1,0:T(8,128)(2,1)}, bf16[64,4608]{1,0:T(8,128)(2,1)}, bf16[64,4608]{1,0:T(8,128)(2,1)}, f32[8,128]{1,0:T(8,128)}) custom-call(bf16[128,4608]{1,0:T(8,128)(2,1)} %collective-permute-done.6.refs_0_.refs_1_, bf16[128,4608]{1,0:T(8,128)(2,1)} %collective-permute-done.7.refs_1_.refs_4_, ...), custom_call_target="tpu_custom_call" | custom-call | tf_op jit(solution)/shard_map/joined/pallas_call | solution.py:62
  66.3 1.6 collective-permute-start.10
  67.9 1.7 collective-permute-start.11
  69.9 1.7 collective-permute-start.13
  71.6 5.9 %joined.6 = (bf16[1024,4608]{1,0:T(8,128)(2,1)}, f32[8,128]{1,0:T(8,128)}) custom-call(bf16[128,4608]{1,0:T(8,128)(2,1)} %get-tuple-element.64.refs_0_, bf16[128,4608]{1,0:T(8,128)(2,1)} %collective-permute-done.6.refs_0_.refs_1_, bf16[128,4608]{1,0:T(8,128)(2,1)} %copy-done.2, bf16[128,4608]{1,0:T(8,128)(2,1)} %get-tuple-element.65.refs_3_, ...), custom_call_target="tpu_custom_call" | custom-call | tf_op jit(solution)/shard_map/joined/pallas_call | solution.py:62
  77.6 1.3 copy-done
  78.9 2.1 %cut.6 = (bf16[128,4608]{1,0:T(8,128)(2,1)}, bf16[128,4608]{1,0:T(8,128)(2,1)}, bf16[128,4608]{1,0:T(8,128)(2,1)}, bf16[128,4608]{1,0:T(8,128)(2,1)}, f32[8,128]{1,0:T(8,128)}) custom-call(bf16[128,8192]{1,0:T(8,128)(2,1)} %bitcast.35, ...), custom_call_target="tpu_custom_call", output_to_operand_aliasing={{0}: (1, {}), {1}: (2, {}), {2}: (3, {}), {3}: (4, {})} | custom-call | tf_op jit(solution)/shard_map/cut/pallas_call | solution.py:108
  81.1 0.8 copy-done.6
  82.0 2.5 %joined.7 = (bf16[1024,4608]{1,0:T(8,128)(2,1)}, f32[8,128]{1,0:T(8,128)}) custom-call(bf16[64,4608]{1,0:T(8,128)(2,1)} %copy-done.6, bf16[64,4608]{1,0:T(8,128)(2,1)} %copy-done.7, bf16[64,4608]{1,0:T(8,128)(2,1)} %collective-permute-done.12.refs_2_, bf16[64,4608]{1,0:T(8,128)(2,1)} %collective-permute-done.13.refs_3_, ...), custom_call_target="tpu_custom_call", output_to_operand_aliasing={{0}: (4, {})} | custom-call | tf_op jit(solution)/shard_map/joined/pallas_call | solution.py:62
  84.7 1.0 collective-permute-start.15
  85.7 2.3 %collective-permute-start.16 = (bf16[128,4608]{1,0:T(8,128)(2,1)}, bf16[128,4608]{1,0:T(8,128)(2,1)}, u32[]{:S(2)}, u32[]{:S(2)}) collective-permute-start(bf16[128,4608]{1,0:T(8,128)(2,1)} %get-tuple-element.85), channel_id=1, source_target_pairs={{0,24},{8,0},{16,8},{24,16},{1,25},{9,1},{17,9},{25,17},{2,26},{10... | collective-permute-start | bytes 3538952 | tf_op jit(solution)/shard_map/ppermute | solution.py:23
  88.0 1.3 collective-permute-start.19
  89.3 1.4 collective-permute-start.20
  90.7 8.9 %collective-permute-done.14.refs_4_.refs_1_ = bf16[1024,4608]{1,0:T(8,128)(2,1)} collective-permute-done((bf16[1024,4608]{1,0:T(8,128)(2,1)}, bf16[1024,4608]{1,0:T(8,128)(2,1)}, u32[]{:S(2)}, u32[]{:S(2)}) %collective-permute-start.14) | collective-permute-done | bytes 9437216 | tf_op jit(solution)/shard_map/ppermute | solution.py:23
  99.6 1.8 %cut.7 = (bf16[128,4608]{1,0:T(8,128)(2,1)}, bf16[128,4608]{1,0:T(8,128)(2,1)}, f32[8,128]{1,0:T(8,128)}) custom-call(bf16[128,8192]{1,0:T(8,128)(2,1)} %bitcast.36, bf16[128,4608]{1,0:T(8,128)(2,1)} %get-tuple-element.86.refs_1_, bf16[128,4608]{1,0:T(8,128)(2,1)} %get-tuple-element.87.refs_2_, ...), custom_call_target="tpu_custom_call", output_to_operand_aliasing={{0}: (1, {}), {1}: (2, {})} | custom-call | tf_op jit(solution)/shard_map/cut/pallas_call | solution.py:108
  101.5 3.8 %collective-permute-start.21 = (bf16[128,4608]{1,0:T(8,128)(2,1)}, bf16[128,4608]{1,0:T(8,128)(2,1)S(1)}, u32[]{:S(2)}, u32[]{:S(2)}) collective-permute-start(bf16[128,4608]{1,0:T(8,128)(2,1)} %get-tuple-element.96), channel_id=1, source_target_pairs={{0,4},{2,6},{4,0},{6,2},{1,5},{3,7},{5,1},{7,3},{8,12},{10,14},{12... | collective-permute-start | bytes 3538952 | tf_op jit(solution)/shard_map/ppermute | solution.py:23
  105.3 9.3 %collective-permute-done.15.refs_4_ = bf16[128,4608]{1,0:T(8,128)(2,1)} collective-permute-done((bf16[128,4608]{1,0:T(8,128)(2,1)}, bf16[128,4608]{1,0:T(8,128)(2,1)}, u32[]{:S(2)}, u32[]{:S(2)}) %collective-permute-start.15) | collective-permute-done | bytes 1179680 | tf_op jit(solution)/shard_map/ppermute | solution.py:23
  114.7 10.8 %project.2 = (f32[640,128]{1,0:T(8,128)}, f32[640,128]{1,0:T(8,128)}, bf16[640,128]{1,0:T(8,128)(2,1)}, bf16[640,128]{1,0:T(8,128)(2,1)}, f32[8,128]{1,0:T(8,128)}) custom-call(s32[64,10]{1,0:T(8,128)} %pad_add_fusion.refs_1_.where_ref, bf16[1024,4608]{1,0:T(8,128)(2,1)} %get-tuple-element.83.refs_0_, ...), custom_call_target="tpu_custom_call" | custom-call | tf_op jit(solution)/shard_map/project/pallas_call | solution.py:298
  125.5 3.0 %collective-permute-start.17 = (bf16[640,128]{1,0:T(8,128)(2,1)}, bf16[640,128]{1,0:T(8,128)(2,1)S(1)}, u32[]{:S(2)}, u32[]{:S(2)}) collective-permute-start(bf16[640,128]{1,0:T(8,128)(2,1)} %get-tuple-element.92), channel_id=1, source_target_pairs={{0,24},{8,0},{16,8},{24,16},{1,25},{9,1},{17,9},{25,17},{2,26},{10... | collective-permute-start | bytes 491528 | tf_op jit(solution)/shard_map/ppermute | solution.py:23
  128.5 16.1 %collective-permute-done.21.refs_4_ = bf16[128,4608]{1,0:T(8,128)(2,1)S(1)} collective-permute-done((bf16[128,4608]{1,0:T(8,128)(2,1)}, bf16[128,4608]{1,0:T(8,128)(2,1)S(1)}, u32[]{:S(2)}, u32[]{:S(2)}) %collective-permute-start.21) | collective-permute-done | bytes 1179680 | tf_op jit(solution)/shard_map/ppermute | solution.py:23
  144.6 0.7 collective-permute-done.22.refs_5_
  145.7 10.8 %project.3 = (bf16[640,128]{1,0:T(8,128)(2,1)}, bf16[640,128]{1,0:T(8,128)(2,1)}, bf16[640,128]{1,0:T(8,128)(2,1)}, bf16[640,128]{1,0:T(8,128)(2,1)}, f32[8,128]{1,0:T(8,128)}) custom-call(s32[64,10]{1,0:T(8,128)} %pad_add_fusion.refs_1_.where_ref, bf16[1024,4608]{1,0:T(8,128)(2,1)} %get-tuple-element.83.refs_0_, ...), custom_call_target="tpu_custom_call" | custom-call | tf_op jit(solution)/shard_map/project/pallas_call | solution.py:298
  156.5 2.4 %collective-permute-start.23 = (bf16[640,128]{1,0:T(8,128)(2,1)}, bf16[640,128]{1,0:T(8,128)(2,1)S(1)}, u32[]{:S(2)}, u32[]{:S(2)}) collective-permute-start(bf16[640,128]{1,0:T(8,128)(2,1)} %get-tuple-element.99), channel_id=1, source_target_pairs={{0,6},{2,0},{4,2},{6,4},{1,7},{3,1},{5,3},{7,5},{8,14},{10,8},{12,... | collective-permute-start | bytes 491528 | tf_op jit(solution)/shard_map/ppermute | solution.py:23
  158.9 4.4 %collective-permute-start.25 = (bf16[640,128]{1,0:T(8,128)(2,1)}, bf16[640,128]{1,0:T(8,128)(2,1)S(1)}, u32[]{:S(2)}, u32[]{:S(2)}) collective-permute-start(bf16[640,128]{1,0:T(8,128)(2,1)} %get-tuple-element.101), channel_id=1, source_target_pairs={{0,4},{2,6},{4,0},{6,2},{1,5},{3,7},{5,1},{7,3},{8,12},{10,14},{12... | collective-permute-start | bytes 491528 | tf_op jit(solution)/shard_map/ppermute | solution.py:23
  163.5 1.4 collective-permute-done.24.refs_5_
  164.9 1.9 %collective-permute-done.25.refs_6_ = bf16[640,128]{1,0:T(8,128)(2,1)S(1)} collective-permute-done((bf16[640,128]{1,0:T(8,128)(2,1)}, bf16[640,128]{1,0:T(8,128)(2,1)S(1)}, u32[]{:S(2)}, u32[]{:S(2)}) %collective-permute-start.25) | collective-permute-done | bytes 163872 | tf_op jit(solution)/shard_map/ppermute | solution.py:23
  166.8 3.5 %collective-permute-done.26.refs_7_ = bf16[640,128]{1,0:T(8,128)(2,1)S(1)} collective-permute-done((bf16[640,128]{1,0:T(8,128)(2,1)}, bf16[640,128]{1,0:T(8,128)(2,1)S(1)}, u32[]{:S(2)}, u32[]{:S(2)}) %collective-permute-start.26) | collective-permute-done | bytes 163872 | tf_op jit(solution)/shard_map/ppermute | solution.py:23
  171.0 2.2 %scores.1 = f32[32,128]{1,0:T(8,128)} custom-call(f32[32,10]{1,0:T(8,128)} %convert_bitcast_fusion.refs_2_.hits_ref, f32[1,128]{1,0:T(1,128)} %compare_convert_fusion.refs_3_.live_ref, f32[640,128]{1,0:T(8,128)} %get-tuple-element.90.refs_0_, f32[640,128]{1,0:T(8,128)} %get-tuple-element.91.refs_1_, bf16[640,128]{1,0:T(8,128)(2,1)} %copy-done.12, ...), custom_call_target="tpu_custom_call" | custom-call | tf_op jit(solution)/shard_map/scores/pallas_call | solution.py:335
  (76 shorter events, 5.7 us)
Async XLA Ops:
  6.4 13.2 %copy-start.18 = (s32[32,8]{0,1:T(8,128)S(1)}, s32[32,8]{0,1:T(8,128)}, u32[]{:S(2)}) copy-start(s32[32,8]{0,1:T(8,128)} %param.15) | copy-start | bytes 3076
  6.4 40.9 %all-to-all-start = ((bf16[4,32,8448]{2,1,0:T(8,128)(2,1)}), bf16[4,32,8448]{2,1,0:T(8,128)(2,1)S(1)}, u32[]{:S(2)}, u32[]{:S(2)}) async-start(bf16[4,32,8448]{2,1,0:T(8,128)(2,1)} %bitcast.40), calls=%async_computation | async-start | bytes 4325376 | tf_op jit(solution)/shard_map/all_to_all | solution.py:429
  10.7 14.6 %collective-permute-start = (bf16[32,4608]{1,0:T(8,128)(2,1)}, bf16[32,4608]{1,0:T(8,128)(2,1)S(1)}, u32[]{:S(2)}, u32[]{:S(2)}) collective-permute-start(bf16[32,4608]{1,0:T(8,128)(2,1)} %get-tuple-element.55), channel_id=1, source_target_pairs={{0,2},{2,4},{4,6},{6,0},{1,3},{3,5},{5,7},{7,1},{8,10},{10,12},{12... | collective-permute-start | bytes 884744 | tf_op jit(solution)/shard_map/ppermute | solution.py:23
  12.6 17.5 %collective-permute-start.1 = (bf16[32,4608]{1,0:T(8,128)(2,1)}, bf16[32,4608]{1,0:T(8,128)(2,1)S(1)}, u32[]{:S(2)}, u32[]{:S(2)}) collective-permute-start(bf16[32,4608]{1,0:T(8,128)(2,1)} %get-tuple-element.56), channel_id=1, source_target_pairs={{0,6},{2,0},{4,2},{6,4},{1,7},{3,1},{5,3},{7,5},{8,14},{10,8},{12,... | collective-permute-start | bytes 884744 | tf_op jit(solution)/shard_map/ppermute | solution.py:23
  12.7 17.3 %collective-permute-start.2 = (bf16[32,4608]{1,0:T(8,128)(2,1)}, bf16[32,4608]{1,0:T(8,128)(2,1)S(1)}, u32[]{:S(2)}, u32[]{:S(2)}) collective-permute-start(bf16[32,4608]{1,0:T(8,128)(2,1)} %get-tuple-element.57), channel_id=1, source_target_pairs={{0,4},{2,6},{4,0},{6,2},{1,5},{3,7},{5,1},{7,3},{8,12},{10,14},{12... | collective-permute-start | bytes 884744 | tf_op jit(solution)/shard_map/ppermute | solution.py:23
  15.7 14.4 %collective-permute-start.3 = (bf16[32,4608]{1,0:T(8,128)(2,1)}, bf16[32,4608]{1,0:T(8,128)(2,1)S(1)}, u32[]{:S(2)}, u32[]{:S(2)}) collective-permute-start(bf16[32,4608]{1,0:T(8,128)(2,1)} %get-tuple-element.59), channel_id=1, source_target_pairs={{0,8},{8,16},{16,24},{24,0},{1,9},{9,17},{17,25},{25,1},{2,10},{10... | collective-permute-start | bytes 884744 | tf_op jit(solution)/shard_map/ppermute | solution.py:23
  17.3 12.8 %collective-permute-start.4 = (bf16[32,4608]{1,0:T(8,128)(2,1)}, bf16[32,4608]{1,0:T(8,128)(2,1)}, u32[]{:S(2)}, u32[]{:S(2)}) collective-permute-start(bf16[32,4608]{1,0:T(8,128)(2,1)} %get-tuple-element.60), channel_id=1, source_target_pairs={{0,24},{8,0},{16,8},{24,16},{1,25},{9,1},{17,9},{25,17},{2,26},{10... | collective-permute-start | bytes 884744 | tf_op jit(solution)/shard_map/ppermute | solution.py:23
  25.3 8.5 %copy-start.8 = (bf16[32,4608]{1,0:T(8,128)(2,1)}, bf16[32,4608]{1,0:T(8,128)(2,1)S(1)}, u32[]{:S(2)}) copy-start(bf16[32,4608]{1,0:T(8,128)(2,1)S(1)} %collective-permute-done.refs_1_) | copy-start | bytes 884740
  25.3 8.5 %collective-permute-start.5 = (bf16[32,4608]{1,0:T(8,128)(2,1)}, bf16[32,4608]{1,0:T(8,128)(2,1)}, u32[]{:S(2)}, u32[]{:S(2)}) collective-permute-start(bf16[32,4608]{1,0:T(8,128)(2,1)} %get-tuple-element.61), channel_id=1, source_target_pairs={{0,16},{8,24},{16,0},{24,8},{1,17},{9,25},{17,1},{25,9},{2,18},{10... | collective-permute-start | bytes 884744 | tf_op jit(solution)/shard_map/ppermute | solution.py:23
  30.1 3.8 %copy-start.9 = (bf16[32,4608]{1,0:T(8,128)(2,1)}, bf16[32,4608]{1,0:T(8,128)(2,1)S(1)}, u32[]{:S(2)}) copy-start(bf16[32,4608]{1,0:T(8,128)(2,1)S(1)} %collective-permute-done.1.refs_2_) | copy-start | bytes 884740
  30.1 3.7 %copy-start.10 = (bf16[32,4608]{1,0:T(8,128)(2,1)}, bf16[32,4608]{1,0:T(8,128)(2,1)S(1)}, u32[]{:S(2)}) copy-start(bf16[32,4608]{1,0:T(8,128)(2,1)S(1)} %collective-permute-done.2.refs_3_) | copy-start | bytes 884740
  30.1 3.7 %copy-start.11 = (bf16[32,4608]{1,0:T(8,128)(2,1)}, bf16[32,4608]{1,0:T(8,128)(2,1)S(1)}, u32[]{:S(2)}) copy-start(bf16[32,4608]{1,0:T(8,128)(2,1)S(1)} %collective-permute-done.3.refs_5_) | copy-start | bytes 884740
  36.4 23.6 %collective-permute-start.8 = (bf16[128,4608]{1,0:T(8,128)(2,1)}, bf16[128,4608]{1,0:T(8,128)(2,1)S(1)}, u32[]{:S(2)}, u32[]{:S(2)}) collective-permute-start(bf16[128,4608]{1,0:T(8,128)(2,1)} %get-tuple-element.64.refs_0_), channel_id=1, source_target_pairs={{0,24},{8,0},{16,8},{24,16},{1,25},{9,1},{17,9},{25,17},{2,26},{10... | collective-permute-start | bytes 3538952 | tf_op jit(solution)/shard_map/ppermute | solution.py:23
  39.5 23.1 %collective-permute-start.6 = (bf16[128,4608]{1,0:T(8,128)(2,1)}, bf16[128,4608]{1,0:T(8,128)(2,1)}, u32[]{:S(2)}, u32[]{:S(2)}) collective-permute-start(bf16[128,4608]{1,0:T(8,128)(2,1)} %get-tuple-element.64.refs_0_), channel_id=1, source_target_pairs={{0,8},{8,16},{16,24},{24,0},{1,9},{9,17},{17,25},{25,1},{2,10},{10... | collective-permute-start | bytes 3538952 | tf_op jit(solution)/shard_map/ppermute | solution.py:23
  39.5 23.1 %collective-permute-start.9 = (bf16[128,4608]{1,0:T(8,128)(2,1)}, bf16[128,4608]{1,0:T(8,128)(2,1)}, u32[]{:S(2)}, u32[]{:S(2)}) collective-permute-start(bf16[128,4608]{1,0:T(8,128)(2,1)} %get-tuple-element.65.refs_3_), channel_id=1, source_target_pairs={{0,6},{2,0},{4,2},{6,4},{1,7},{3,1},{5,3},{7,5},{8,14},{10,8},{12,... | collective-permute-start | bytes 3538952 | tf_op jit(solution)/shard_map/ppermute | solution.py:23
  39.5 24.2 %collective-permute-start.7 = (bf16[128,4608]{1,0:T(8,128)(2,1)}, bf16[128,4608]{1,0:T(8,128)(2,1)}, u32[]{:S(2)}, u32[]{:S(2)}) collective-permute-start(bf16[128,4608]{1,0:T(8,128)(2,1)} %get-tuple-element.65.refs_3_), channel_id=1, source_target_pairs={{0,2},{2,4},{4,6},{6,0},{1,3},{3,5},{5,7},{7,1},{8,10},{10,12},{12... | collective-permute-start | bytes 3538952 | tf_op jit(solution)/shard_map/ppermute | solution.py:23
  47.3 1.4 copy-start.1
  53.3 24.2 %all-to-all-start.1 = ((bf16[4,32,8192]{2,1,0:T(8,128)(2,1)}), bf16[4,32,8192]{2,1,0:T(8,128)(2,1)S(1)}, u32[]{:S(2)}, u32[]{:S(2)}) async-start(bf16[4,32,8192]{2,1,0:T(8,128)(2,1)} %get-tuple-element.76), calls=%async_computation.1 | async-start | bytes 4194304 | tf_op jit(solution)/shard_map/all_to_all | solution.py:450
  60.0 3.7 %copy-start.2 = (bf16[128,4608]{1,0:T(8,128)(2,1)}, bf16[128,4608]{1,0:T(8,128)(2,1)S(1)}, u32[]{:S(2)}) copy-start(bf16[128,4608]{1,0:T(8,128)(2,1)S(1)} %collective-permute-done.8.refs_2_) | copy-start | bytes 3538948
  66.3 14.7 %collective-permute-start.10 = (bf16[64,4608]{1,0:T(8,128)(2,1)}, bf16[64,4608]{1,0:T(8,128)(2,1)S(1)}, u32[]{:S(2)}, u32[]{:S(2)}) collective-permute-start(bf16[64,4608]{1,0:T(8,128)(2,1)} %get-tuple-element.70), channel_id=1, source_target_pairs={{0,8},{8,16},{16,24},{24,0},{1,9},{9,17},{17,25},{25,1},{2,10},{10... | collective-permute-start | bytes 1769480 | tf_op jit(solution)/shard_map/ppermute | solution.py:23
  67.9 13.1 %collective-permute-start.11 = (bf16[64,4608]{1,0:T(8,128)(2,1)}, bf16[64,4608]{1,0:T(8,128)(2,1)S(1)}, u32[]{:S(2)}, u32[]{:S(2)}) collective-permute-start(bf16[64,4608]{1,0:T(8,128)(2,1)} %get-tuple-element.71), channel_id=1, source_target_pairs={{0,24},{8,0},{16,8},{24,16},{1,25},{9,1},{17,9},{25,17},{2,26},{10... | collective-permute-start | bytes 1769480 | tf_op jit(solution)/shard_map/ppermute | solution.py:23
  69.6 11.5 %collective-permute-start.12 = (bf16[64,4608]{1,0:T(8,128)(2,1)}, bf16[64,4608]{1,0:T(8,128)(2,1)}, u32[]{:S(2)}, u32[]{:S(2)}) collective-permute-start(bf16[64,4608]{1,0:T(8,128)(2,1)} %get-tuple-element.72), channel_id=1, source_target_pairs={{0,2},{2,4},{4,6},{6,0},{1,3},{3,5},{5,7},{7,1},{8,10},{10,12},{12... | collective-permute-start | bytes 1769480 | tf_op jit(solution)/shard_map/ppermute | solution.py:23
  69.9 11.2 %collective-permute-start.13 = (bf16[64,4608]{1,0:T(8,128)(2,1)}, bf16[64,4608]{1,0:T(8,128)(2,1)}, u32[]{:S(2)}, u32[]{:S(2)}) collective-permute-start(bf16[64,4608]{1,0:T(8,128)(2,1)} %get-tuple-element.73), channel_id=1, source_target_pairs={{0,6},{2,0},{4,2},{6,4},{1,7},{3,1},{5,3},{7,5},{8,14},{10,8},{12,... | collective-permute-start | bytes 1769480 | tf_op jit(solution)/shard_map/ppermute | solution.py:23
  77.6 1.4 copy-start
  81.0 0.8 copy-start.6
  81.0 1.0 copy-start.7
  84.6 15.1 %collective-permute-start.14 = (bf16[1024,4608]{1,0:T(8,128)(2,1)}, bf16[1024,4608]{1,0:T(8,128)(2,1)}, u32[]{:S(2)}, u32[]{:S(2)}) collective-permute-start(bf16[1024,4608]{1,0:T(8,128)(2,1)} %get-tuple-element.83.refs_0_), channel_id=1, source_target_pairs={{0,1},{1,0},{2,3},{3,2},{4,5},{5,4},{6,7},{7,6},{8,9},{9,8},{10,11... | collective-permute-start | bytes 28311560 | tf_op jit(solution)/shard_map/ppermute | solution.py:23
  84.7 29.9 %collective-permute-start.15 = (bf16[128,4608]{1,0:T(8,128)(2,1)}, bf16[128,4608]{1,0:T(8,128)(2,1)}, u32[]{:S(2)}, u32[]{:S(2)}) collective-permute-start(bf16[128,4608]{1,0:T(8,128)(2,1)} %get-tuple-element.84), channel_id=1, source_target_pairs={{0,8},{8,16},{16,24},{24,0},{1,9},{9,17},{17,25},{25,1},{2,10},{10... | collective-permute-start | bytes 3538952 | tf_op jit(solution)/shard_map/ppermute | solution.py:23
  85.7 29.0 %collective-permute-start.16 = (bf16[128,4608]{1,0:T(8,128)(2,1)}, bf16[128,4608]{1,0:T(8,128)(2,1)}, u32[]{:S(2)}, u32[]{:S(2)}) collective-permute-start(bf16[128,4608]{1,0:T(8,128)(2,1)} %get-tuple-element.85), channel_id=1, source_target_pairs={{0,24},{8,0},{16,8},{24,16},{1,25},{9,1},{17,9},{25,17},{2,26},{10... | collective-permute-start | bytes 3538952 | tf_op jit(solution)/shard_map/ppermute | solution.py:23
  88.0 40.5 %collective-permute-start.19 = (bf16[128,4608]{1,0:T(8,128)(2,1)}, bf16[128,4608]{1,0:T(8,128)(2,1)S(1)}, u32[]{:S(2)}, u32[]{:S(2)}) collective-permute-start(bf16[128,4608]{1,0:T(8,128)(2,1)} %get-tuple-element.94), channel_id=1, source_target_pairs={{0,2},{2,4},{4,6},{6,0},{1,3},{3,5},{5,7},{7,1},{8,10},{10,12},{12... | collective-permute-start | bytes 3538952 | tf_op jit(solution)/shard_map/ppermute | solution.py:23
  89.3 39.2 %collective-permute-start.20 = (bf16[128,4608]{1,0:T(8,128)(2,1)}, bf16[128,4608]{1,0:T(8,128)(2,1)S(1)}, u32[]{:S(2)}, u32[]{:S(2)}) collective-permute-start(bf16[128,4608]{1,0:T(8,128)(2,1)} %get-tuple-element.95), channel_id=1, source_target_pairs={{0,6},{2,0},{4,2},{6,4},{1,7},{3,1},{5,3},{7,5},{8,14},{10,8},{12,... | collective-permute-start | bytes 3538952 | tf_op jit(solution)/shard_map/ppermute | solution.py:23
  101.5 43.2 %collective-permute-start.21 = (bf16[128,4608]{1,0:T(8,128)(2,1)}, bf16[128,4608]{1,0:T(8,128)(2,1)S(1)}, u32[]{:S(2)}, u32[]{:S(2)}) collective-permute-start(bf16[128,4608]{1,0:T(8,128)(2,1)} %get-tuple-element.96), channel_id=1, source_target_pairs={{0,4},{2,6},{4,0},{6,2},{1,5},{3,7},{5,1},{7,3},{8,12},{10,14},{12... | collective-permute-start | bytes 3538952 | tf_op jit(solution)/shard_map/ppermute | solution.py:23
  114.6 30.7 %collective-permute-start.22 = (bf16[128,4608]{1,0:T(8,128)(2,1)}, bf16[128,4608]{1,0:T(8,128)(2,1)}, u32[]{:S(2)}, u32[]{:S(2)}) collective-permute-start(bf16[128,4608]{1,0:T(8,128)(2,1)} %get-tuple-element.97), channel_id=1, source_target_pairs={{0,16},{8,24},{16,0},{24,8},{1,17},{9,25},{17,1},{25,9},{2,18},{10... | collective-permute-start | bytes 3538952 | tf_op jit(solution)/shard_map/ppermute | solution.py:23
  125.5 37.8 %collective-permute-start.17 = (bf16[640,128]{1,0:T(8,128)(2,1)}, bf16[640,128]{1,0:T(8,128)(2,1)S(1)}, u32[]{:S(2)}, u32[]{:S(2)}) collective-permute-start(bf16[640,128]{1,0:T(8,128)(2,1)} %get-tuple-element.92), channel_id=1, source_target_pairs={{0,24},{8,0},{16,8},{24,16},{1,25},{9,1},{17,9},{25,17},{2,26},{10... | collective-permute-start | bytes 491528 | tf_op jit(solution)/shard_map/ppermute | solution.py:23
  128.5 16.8 %copy-start.3 = (bf16[128,4608]{1,0:T(8,128)(2,1)}, bf16[128,4608]{1,0:T(8,128)(2,1)S(1)}, u32[]{:S(2)}) copy-start(bf16[128,4608]{1,0:T(8,128)(2,1)S(1)} %collective-permute-done.19.refs_2_) | copy-start | bytes 3538948
  128.5 34.8 %collective-permute-start.18 = (bf16[640,128]{1,0:T(8,128)(2,1)}, bf16[640,128]{1,0:T(8,128)(2,1)S(1)}, u32[]{:S(2)}, u32[]{:S(2)}) collective-permute-start(bf16[640,128]{1,0:T(8,128)(2,1)} %get-tuple-element.93), channel_id=1, source_target_pairs={{0,8},{8,16},{16,24},{24,0},{1,9},{9,17},{17,25},{25,1},{2,10},{10... | collective-permute-start | bytes 491528 | tf_op jit(solution)/shard_map/ppermute | solution.py:23
  128.5 16.8 %copy-start.4 = (bf16[128,4608]{1,0:T(8,128)(2,1)}, bf16[128,4608]{1,0:T(8,128)(2,1)S(1)}, u32[]{:S(2)}) copy-start(bf16[128,4608]{1,0:T(8,128)(2,1)S(1)} %collective-permute-done.20.refs_3_) | copy-start | bytes 3538948
  144.6 1.0 copy-start.5
  156.5 7.0 %collective-permute-start.23 = (bf16[640,128]{1,0:T(8,128)(2,1)}, bf16[640,128]{1,0:T(8,128)(2,1)S(1)}, u32[]{:S(2)}, u32[]{:S(2)}) collective-permute-start(bf16[640,128]{1,0:T(8,128)(2,1)} %get-tuple-element.99), channel_id=1, source_target_pairs={{0,6},{2,0},{4,2},{6,4},{1,7},{3,1},{5,3},{7,5},{8,14},{10,8},{12,... | collective-permute-start | bytes 491528 | tf_op jit(solution)/shard_map/ppermute | solution.py:23
  158.9 6.0 %collective-permute-start.24 = (bf16[640,128]{1,0:T(8,128)(2,1)}, bf16[640,128]{1,0:T(8,128)(2,1)S(1)}, u32[]{:S(2)}, u32[]{:S(2)}) collective-permute-start(bf16[640,128]{1,0:T(8,128)(2,1)} %get-tuple-element.100), channel_id=1, source_target_pairs={{0,2},{2,4},{4,6},{6,0},{1,3},{3,5},{5,7},{7,1},{8,10},{10,12},{12... | collective-permute-start | bytes 491528 | tf_op jit(solution)/shard_map/ppermute | solution.py:23
  158.9 7.9 %collective-permute-start.25 = (bf16[640,128]{1,0:T(8,128)(2,1)}, bf16[640,128]{1,0:T(8,128)(2,1)S(1)}, u32[]{:S(2)}, u32[]{:S(2)}) collective-permute-start(bf16[640,128]{1,0:T(8,128)(2,1)} %get-tuple-element.101), channel_id=1, source_target_pairs={{0,4},{2,6},{4,0},{6,2},{1,5},{3,7},{5,1},{7,3},{8,12},{10,14},{12... | collective-permute-start | bytes 491528 | tf_op jit(solution)/shard_map/ppermute | solution.py:23
  163.3 7.0 %copy-start.12 = (bf16[640,128]{1,0:T(8,128)(2,1)}, bf16[640,128]{1,0:T(8,128)(2,1)S(1)}, u32[]{:S(2)}) copy-start(bf16[640,128]{1,0:T(8,128)(2,1)S(1)} %collective-permute-done.17.refs_2_) | copy-start | bytes 491524
  163.3 7.0 %collective-permute-start.26 = (bf16[640,128]{1,0:T(8,128)(2,1)}, bf16[640,128]{1,0:T(8,128)(2,1)S(1)}, u32[]{:S(2)}, u32[]{:S(2)}) collective-permute-start(bf16[640,128]{1,0:T(8,128)(2,1)} %get-tuple-element.102), channel_id=1, source_target_pairs={{0,16},{8,24},{16,0},{24,8},{1,17},{9,25},{17,1},{25,9},{2,18},{10... | collective-permute-start | bytes 491528 | tf_op jit(solution)/shard_map/ppermute | solution.py:23
  163.3 7.0 %copy-start.13 = (bf16[640,128]{1,0:T(8,128)(2,1)}, bf16[640,128]{1,0:T(8,128)(2,1)S(1)}, u32[]{:S(2)}) copy-start(bf16[640,128]{1,0:T(8,128)(2,1)S(1)} %collective-permute-done.18.refs_3_) | copy-start | bytes 491524
  163.5 6.8 %copy-start.14 = (bf16[640,128]{1,0:T(8,128)(2,1)}, bf16[640,128]{1,0:T(8,128)(2,1)S(1)}, u32[]{:S(2)}) copy-start(bf16[640,128]{1,0:T(8,128)(2,1)S(1)} %collective-permute-done.23.refs_4_) | copy-start | bytes 491524
  164.9 5.5 %copy-start.15 = (bf16[640,128]{1,0:T(8,128)(2,1)}, bf16[640,128]{1,0:T(8,128)(2,1)S(1)}, u32[]{:S(2)}) copy-start(bf16[640,128]{1,0:T(8,128)(2,1)S(1)} %collective-permute-done.24.refs_5_) | copy-start | bytes 491524
  166.8 3.6 %copy-start.16 = (bf16[640,128]{1,0:T(8,128)(2,1)}, bf16[640,128]{1,0:T(8,128)(2,1)S(1)}, u32[]{:S(2)}) copy-start(bf16[640,128]{1,0:T(8,128)(2,1)S(1)} %collective-permute-done.25.refs_6_) | copy-start | bytes 491524
  170.3 0.7 copy-start.17
